TPU v7x, 32 devices: a whole 2x2x4 slice. The times are simulated.
32 devices in a mesh: row: 4 (over y, core), col: 8 (over z, x).
Axes of the slice: x: 2, y: 2, z: 4, core: 2. Of those that a mesh axis runs over, the one named last changes fastest.
Arguments:
- amplitudes: bfloat16 [8, 8, 4, 128, 128], P('row', 'col'), may hold values from -6 to 6
- cholesky: bfloat16 [8, 8, 10, 128, 128], P('row', 'col'), may hold values from -0.5 to 0.5, as said below
- tile_mask: int32 [8, 8], P('row', 'col'), may hold values 0 or 1
Outputs:
- antisymmetrized: bfloat16 [8, 8, 4, 128, 128], P('row', 'col')
Inputs may be any that keep to these rules, and one draw needn't show every extreme that they name: cholesky is symmetric: cholesky[a,c,q,x,u] equals cholesky[c,a,q,u,x].
All inputs are finite; a program needn't handle non-finite values. No bound on the sum of `tile_mask` on one device may be relied on, other than what follows from the above.
Results may differ from a plain program's by a relative error of at most 0.0059.
Values may be sent and summed in bfloat16 or wider, within the bound.
No kernel may reach another device: no remote copies, remote signals or barrier semaphores. Data moves between devices by JAX's collectives and lax.ppermute only.
A program may use at most 128 MiB of HBM per device.

v0:
```python
import math

import jax
import jax.numpy as jnp
from jax import lax
from jax.sharding import PartitionSpec as P


def from_partner(value, axis, apart):
    mask = 2**apart
    pairs = [(source, source ^ mask) for source in range(lax.axis_size(axis))]
    return lax.ppermute(value, axis, pairs)


def flip_row(tile_set, bit_pos):
    bit_value = lax.axis_index("row") >> bit_pos & 1
    kept = lax.dynamic_index_in_dim(tile_set, bit_value, 0, keepdims=False)
    outgoing = lax.dynamic_index_in_dim(tile_set, 1 - bit_value, 0, keepdims=False)
    incoming = from_partner(outgoing, "row", bit_pos)
    slot_zero = jnp.where(bit_value == 0, kept, incoming)
    slot_one = jnp.where(bit_value == 0, incoming, kept)
    return jnp.stack([slot_zero, slot_one])


def flip_col(tile_set, bit_pos):
    bit_value = lax.axis_index("col") >> bit_pos & 1
    kept = lax.dynamic_index_in_dim(tile_set, bit_value, 0, keepdims=False)
    outgoing = lax.dynamic_index_in_dim(tile_set, 1 - bit_value, 0, keepdims=False)
    incoming = from_partner(outgoing, "col", bit_pos)
    slot_zero = jnp.where(bit_value == 0, kept, incoming)
    slot_one = jnp.where(bit_value == 0, incoming, kept)
    return jnp.stack([slot_zero, slot_one])


def mirror_cascade(tile_set):
    col_bits = lax.axis_size("col").bit_length() - 1
    tile_set = flip_col(tile_set, 0)
    for bit_pos in range(1, col_bits):
        tile_set = flip_row(tile_set, bit_pos - 1)
        tile_set = flip_col(tile_set, bit_pos)
        tile_set = flip_row(tile_set, bit_pos - 1)
    return tile_set


def body(amplitudes, cholesky, tile_mask):
    tile_rows = amplitudes.shape[0]
    pair_count = amplitudes.shape[2]
    tile_edge = amplitudes.shape[3]
    vectors = cholesky.shape[2]
    occupied = math.isqrt(pair_count)
    column = lax.all_gather(cholesky, "row", axis=0, tiled=True)
    column_mats = jnp.transpose(column[:, 0], (0, 2, 1, 3)).reshape(
        column.shape[0], tile_edge, vectors * tile_edge
    )
    amp_block = lax.all_gather(amplitudes, "col", axis=1, tiled=True)
    mask_block = lax.all_gather(tile_mask, "col", axis=1, tiled=True)
    tile_count = amp_block.shape[1]
    masked = amp_block * mask_block.astype(jnp.bfloat16)[:, :, None, None, None]
    masked = masked.reshape(amp_block.shape[0], tile_count, pair_count * tile_edge, tile_edge)
    halves = jnp.einsum("cnmv,nvz->cmz", masked, column_mats, preferred_element_type=jnp.float32)
    halves = halves.astype(jnp.bfloat16).reshape(
        tile_rows, pair_count, tile_edge, vectors, tile_edge
    )
    spread = lax.all_gather(cholesky, "col", axis=1, tiled=True)
    ladder = lax.psum_scatter(
        jnp.einsum("caqux,cpuqy->apxy", spread, halves, preferred_element_type=jnp.float32),
        "row",
        scatter_dimension=0,
        tiled=True,
    )
    rounded = ladder.astype(jnp.bfloat16)
    mirror = mirror_cascade(rounded)
    own_tiles = lax.optimization_barrier(rounded).astype(jnp.float32)
    flipped = mirror.reshape(tile_rows, occupied, occupied, tile_edge, tile_edge)
    flipped = jnp.transpose(flipped, (0, 2, 1, 4, 3)).reshape(
        tile_rows, pair_count, tile_edge, tile_edge
    )
    result_tiles = (own_tiles - flipped.astype(jnp.float32)).astype(jnp.bfloat16)
    return result_tiles.reshape(tile_rows, 1, pair_count, tile_edge, tile_edge)


def solution(mesh):
    in_specs = (
        P("row", "col", None, None, None),
        P("row", "col", None, None, None),
        P("row", "col"),
    )
    out_specs = P("row", "col", None, None, None)
    return jax.shard_map(body, mesh=mesh, in_specs=in_specs, out_specs=out_specs, check_vma=False)
```

profile of v0, /device:TPU:0, one launch (start us, length us, event | category | flops | bytes accessed | tf_op | source)
XLA Modules:
  0.0 264.9 jit_solution(10606480142979248206)
XLA Ops:
  6.5 0.7 all-gather.5.cloned.1.call-update
  7.3 0.7 all-gather.7.cloned.1.call-update
  8.1 0.7 all-gather.9.cloned.1.call-update
  8.7 22.3 %all-gather = s32[8,1,2]{2,1,0:T(1,128)S(1)} all-gather(s32[1,1,2]{2,1,0:T(1,128)} %bitcast.137), channel_id=1, replica_groups=mesh['row'=4,'col'=8] {'col'}, dimensions={0}, use_global_device_ids=true | all-gather | bytes 72 | tf_op jit(solution)/shard_map/all_gather | solution.py:56
  31.1 0.1 copy.44
  31.1 1.2 dynamic-slice
  33.0 28.5 %all-gather.5.cloned.1.call-done = bf16[2,8,4,128,128]{4,3,2,1,0:T(8,128)(2,1)} async-done(((bf16[2,1,4,128,128]{4,3,2,1,0:T(8,128)(2,1)}), bf16[2,8,4,128,128]{4,3,2,1,0:T(8,128)(2,1)}) %all-gather.5.cloned.1.call-update) | async-done | bytes 2097168 | tf_op jit(solution)/shard_map/all_gather | solution.py:55
  61.5 3.2 %broadcast_multiply_fusion = bf16[2,8,4,128,128]{4,3,2,1,0:T(8,128)(2,1)} fusion(bf16[2,8,4,128,128]{4,3,2,1,0:T(8,128)(2,1)} %all-gather.5.cloned.1.call-done, bf16[2,8]{1,0:T(2,128)(2,1)S(1)} %convert_bitcast_fusion.1), kind=kLoop, calls=%fused_computation.5 | loop fusion | flops 1048576 | bytes 4194336 | tf_op jit(solution)/shard_map/mul | solution.py:58
  64.7 22.5 %all-gather.7.cloned.1.call-done = bf16[8,1,10,128,128]{4,3,2,1,0:T(8,128)(2,1)} async-done(((bf16[2,1,10,128,128]{4,3,2,1,0:T(8,128)(2,1)}), bf16[8,1,10,128,128]{4,3,2,1,0:T(8,128)(2,1)}) %all-gather.7.cloned.1.call-update) | async-done | bytes 2621456 | tf_op jit(solution)/shard_map/all_gather | solution.py:51
  87.2 3.2 %copy.45 = bf16[8,1,10,128,128]{3,4,2,0,1:T(8,128)(2,1)S(1)} copy(bf16[8,1,10,128,128]{4,3,2,1,0:T(8,128)(2,1)} %all-gather.7.cloned.1.call-done) | data formatting | bytes 5242880 | tf_op jit(solution)/shard_map/all_gather | solution.py:51
  90.4 6.0 %bitcast_convert_fusion = bf16[2,512,1280]{2,1,0:T(8,128)(2,1)} fusion(bf16[2,8,512,128]{3,2,1,0:T(8,128)(2,1)} %bitcast.133, bf16[8,128,1280,1]{1,2,0,3:T(8,128)(2,1)S(1)} %bitcast.131), kind=kOutput, calls=%fused_computation.2 | convolution fusion | flops 2685665280 | bytes 7340032 | tf_op jit(solution)/shard_map/cnmv,nvz->cmz/dot_general | solution.py:60
  96.4 6.4 %reshape.36 = bf16[2,4,128,10,128]{4,3,2,1,0:T(8,128)(2,1)} reshape(bf16[2,512,1280]{2,1,0:T(8,128)(2,1)} %bitcast_convert_fusion) | data formatting | bytes 5242880 | tf_op jit(solution)/shard_map/reshape | solution.py:61
  102.8 72.9 %all-gather.9.cloned.1.call-done = bf16[2,8,10,128,128]{4,3,2,0,1:T(8,128)(2,1)} async-done(((bf16[2,1,10,128,128]{4,3,2,0,1:T(8,128)(2,1)}), bf16[2,8,10,128,128]{4,3,2,0,1:T(8,128)(2,1)}) %all-gather.9.cloned.1.call-update) | async-done | bytes 5242896 | tf_op jit(solution)/shard_map/all_gather | solution.py:64
  175.7 6.1 %fusion.3 = f32[8,4,128,128]{2,3,0,1:T(8,128)S(1)} fusion(bf16[2,8,10,128,128]{4,3,2,0,1:T(8,128)(2,1)} %all-gather.9.cloned.1.call-done, bf16[2,4,128,10,128,1]{4,3,2,1,0,5:T(8,128)(2,1)} %bitcast.130), kind=kOutput, calls=%fused_computation.4 | convolution fusion | flops 2684354560 | bytes 9961472 | tf_op jit(solution)/shard_map/caqux,cpuqy->apxy/dot_general | solution.py:66
  181.8 40.2 %all-reduce.2 = bf16[8,4,128,128]{2,3,0,1:T(8,128)(2,1)S(1)} all-reduce(f32[8,4,128,128]{2,3,0,1:T(8,128)S(1)} %fusion.3), channel_id=2, replica_groups=mesh['row'=4,'col'=8] {'row'}, use_global_device_ids=true, to_apply=%region_0.0.clone | all-reduce | flops 524288 | bytes 3145728
  222.0 0.2 copy.50
  222.2 0.6 collective-permute-start
  222.9 5.0 %collective-permute-done = bf16[4,128,128]{2,1,0:T(8,128)(2,1)S(1)} collective-permute-done((bf16[4,128,128]{2,1,0:T(8,128)(2,1)S(1)}, bf16[4,128,128]{2,1,0:T(8,128)(2,1)S(1)}, u32[]{:S(2)}, u32[]{:S(2)}) %collective-permute-start) | collective-permute-done | bytes 131104 | tf_op jit(solution)/shard_map/ppermute | solution.py:12
  228.0 0.1 collective-permute-start.1
  228.0 1.3 collective-permute-done.1
  229.5 0.4 collective-permute-start.2
  229.9 5.2 %collective-permute-done.2 = bf16[4,128,128]{2,1,0:T(8,128)(2,1)S(1)} collective-permute-done((bf16[4,128,128]{2,1,0:T(8,128)(2,1)S(1)}, bf16[4,128,128]{2,1,0:T(8,128)(2,1)S(1)}, u32[]{:S(2)}, u32[]{:S(2)}) %collective-permute-start.2) | collective-permute-done | bytes 131104 | tf_op jit(solution)/shard_map/ppermute | solution.py:12
  235.3 0.1 collective-permute-start.3
  235.3 1.3 collective-permute-done.3
  236.8 2.2 collective-permute-start.4
  239.0 3.8 %collective-permute-done.4 = bf16[4,128,128]{2,1,0:T(8,128)(2,1)S(1)} collective-permute-done((bf16[4,128,128]{2,1,0:T(8,128)(2,1)S(1)}, bf16[4,128,128]{2,1,0:T(8,128)(2,1)S(1)}, u32[]{:S(2)}, u32[]{:S(2)}) %collective-permute-start.4) | collective-permute-done | bytes 131104 | tf_op jit(solution)/shard_map/ppermute | solution.py:12
  243.0 2.1 collective-permute-start.5
  245.1 6.5 %collective-permute-done.5 = bf16[4,128,128]{2,1,0:T(8,128)(2,1)S(1)} collective-permute-done((bf16[4,128,128]{2,1,0:T(8,128)(2,1)S(1)}, bf16[4,128,128]{2,1,0:T(8,128)(2,1)S(1)}, u32[]{:S(2)}, u32[]{:S(2)}) %collective-permute-start.5) | collective-permute-done | bytes 131104 | tf_op jit(solution)/shard_map/ppermute | solution.py:12
  251.8 1.5 collective-permute-start.6
  253.3 4.0 %collective-permute-done.6 = bf16[4,128,128]{2,1,0:T(8,128)(2,1)S(1)} collective-permute-done((bf16[4,128,128]{2,1,0:T(8,128)(2,1)S(1)}, bf16[4,128,128]{2,1,0:T(8,128)(2,1)S(1)}, u32[]{:S(2)}, u32[]{:S(2)}) %collective-permute-start.6) | collective-permute-done | bytes 131104 | tf_op jit(solution)/shard_map/ppermute | solution.py:12
  257.4 0.2 copy.51
  257.6 0.8 fusion.8
  (20 shorter events, 1.0 us)
Async XLA Ops:
  6.5 55.0 %all-gather.5.cloned.1.call-start = ((), (), s32[]{:S(2)}) async-start(), calls=%async_computation | async-start | bytes 2359296 | tf_op jit(solution)/shard_map/all_gather | solution.py:55
  7.3 79.9 %all-gather.7.cloned.1.call-start = ((), (), s32[]{:S(2)}) async-start(), calls=%async_computation.1 | async-start | bytes 3276800 | tf_op jit(solution)/shard_map/all_gather | solution.py:51
  8.0 167.7 %all-gather.9.cloned.1.call-start = ((), (), s32[]{:S(2)}) async-start(), calls=%async_computation.2 | async-start | bytes 5898240 | tf_op jit(solution)/shard_map/all_gather | solution.py:64
  222.2 5.6 %collective-permute-start = (bf16[4,128,128]{2,1,0:T(8,128)(2,1)S(1)}, bf16[4,128,128]{2,1,0:T(8,128)(2,1)S(1)}, u32[]{:S(2)}, u32[]{:S(2)}) collective-permute-start(bf16[4,128,128]{2,1,0:T(8,128)(2,1)S(1)} %dynamic-slice_bitcast_fusion), channel_id=1, source_target_pairs={{0,1},{1,0},{2,3},{3,2},{4,5},{5,4},{6,7},{7,6},{8,9},{9,8},{10,11... | collective-permute-start | bytes 393224 | tf_op jit(solution)/shard_map/ppermute | solution.py:12
  228.0 1.4 collective-permute-start.1
  229.5 5.6 %collective-permute-start.2 = (bf16[4,128,128]{2,1,0:T(8,128)(2,1)S(1)}, bf16[4,128,128]{2,1,0:T(8,128)(2,1)S(1)}, u32[]{:S(2)}, u32[]{:S(2)}) collective-permute-start(bf16[4,128,128]{2,1,0:T(8,128)(2,1)S(1)} %fusion.26), channel_id=1, source_target_pairs={{0,2},{1,3},{2,0},{3,1},{4,6},{5,7},{6,4},{7,5},{8,10},{9,11},{10,... | collective-permute-start | bytes 393224 | tf_op jit(solution)/shard_map/ppermute | solution.py:12
  235.3 1.4 collective-permute-start.3
  236.8 6.0 %collective-permute-start.4 = (bf16[4,128,128]{2,1,0:T(8,128)(2,1)S(1)}, bf16[4,128,128]{2,1,0:T(8,128)(2,1)S(1)}, u32[]{:S(2)}, u32[]{:S(2)}) collective-permute-start(bf16[4,128,128]{2,1,0:T(8,128)(2,1)S(1)} %fusion.18), channel_id=1, source_target_pairs={{0,16},{8,24},{16,0},{24,8},{1,17},{9,25},{17,1},{25,9},{2,18},{10... | collective-permute-start | bytes 393224 | tf_op jit(solution)/shard_map/ppermute | solution.py:12
  243.0 8.6 %collective-permute-start.5 = (bf16[4,128,128]{2,1,0:T(8,128)(2,1)S(1)}, bf16[4,128,128]{2,1,0:T(8,128)(2,1)S(1)}, u32[]{:S(2)}, u32[]{:S(2)}) collective-permute-start(bf16[4,128,128]{2,1,0:T(8,128)(2,1)S(1)} %fusion.14), channel_id=1, source_target_pairs={{0,4},{1,5},{2,6},{3,7},{4,0},{5,1},{6,2},{7,3},{8,12},{9,13},{10,... | collective-permute-start | bytes 393224 | tf_op jit(solution)/shard_map/ppermute | solution.py:12
  251.8 5.5 %collective-permute-start.6 = (bf16[4,128,128]{2,1,0:T(8,128)(2,1)S(1)}, bf16[4,128,128]{2,1,0:T(8,128)(2,1)S(1)}, u32[]{:S(2)}, u32[]{:S(2)}) collective-permute-start(bf16[4,128,128]{2,1,0:T(8,128)(2,1)S(1)} %fusion.10), channel_id=1, source_target_pairs={{0,16},{8,24},{16,0},{24,8},{1,17},{9,25},{17,1},{25,9},{2,18},{10... | collective-permute-start | bytes 393224 | tf_op jit(solution)/shard_map/ppermute | solution.py:12
Sparse Core Ops, SparseCore 0:
  9.5 51.9 all-gather.4
  63.1 24.0 all-gather.6
  89.4 86.2 all-gather.8
where the time goes:
time: 265 us
  waiting for transfers between devices  153 us (58%)
  blocking collectives  62.5 us (24%)
  between operations  13.9 us (5%)
  matrix products  12.1 us (5%)
  local copies, waits for them, and re-layouts  11.3 us (4%)
  starting transfers between devices  7.09 us (3%)
  other arithmetic  4.77 us (2%)
    all_gather x1, waiting for transfers between devices, body(): spread = lax.all_gather(cholesky, 'col', axis=1, tiled=True)  72.9 us
    unnamed x1, blocking collectives  40.2 us
    all_gather x1, waiting for transfers between devices, body(): amp_block = lax.all_gather(amplitudes, 'col', axis=1, tiled=True)  28.5 us
    ppermute x7, waiting for transfers between devices, from_partner(): return lax.ppermute(value, axis, pairs)  27.2 us
    all_gather x1, waiting for transfers between devices, body(): column = lax.all_gather(cholesky, 'row', axis=0, tiled=True)  22.5 us
    all_gather x1, blocking collectives, body(): mask_block = lax.all_gather(tile_mask, 'col', axis=1, tiled=True)  22.3 us
    ppermute x7, starting transfers between devices, from_partner(): return lax.ppermute(value, axis, pairs)  7.02 us
    reshape x1, local copies, waits for them, and re-layouts, body(): halves.astype(jnp.bfloat16)  6.38 us
  transfers between devices with their start and end apart: 10, of which 10 were waited for; matrix products, arithmetic and copies ran while one was open for 8% of the time, Pallas kernels for 0%

commit v1 on v0

--- a/solution.py
+++ b/solution.py
@@ -1,9 +1,248 @@
+import functools
 import math
 
 import jax
 import jax.numpy as jnp
 from jax import lax
+from jax.experimental import pallas as pl
+from jax.experimental.pallas import tpu as pltpu
 from jax.sharding import PartitionSpec as P
+
+ROWS, PLANES, BLOCKS = 4, 4, 10
+SLOT_OF = {
+    (0, 0): 0, (1, 0): 1, (2, 0): 2, (3, 0): 3, (1, 1): 4,
+    (3, 1): 5, (2, 2): 6, (3, 2): 7, (3, 3): 8, (2, 1): 9,
+}
+
+
+def move(value, rule):
+    pairs = []
+    for r in range(ROWS):
+        for z in range(PLANES):
+            for x in range(2):
+                to = rule(r, z, x)
+                if to is not None:
+                    pairs.append((r * 2 * PLANES + 2 * z + x, to[0] * 2 * PLANES + 2 * to[1] + to[2]))
+    return lax.ppermute(value, ("row", "col"), pairs)
+
+
+def swap_core(value):
+    return move(value, lambda r, z, x: (r ^ 1, z, x))
+
+
+def swap_y(value):
+    return move(value, lambda r, z, x: (r ^ 2, z, x))
+
+
+def swap_x(value):
+    return move(value, lambda r, z, x: (r, z, x ^ 1))
+
+
+def antisym_kernel(info, own, side, mirror_own, mirror_side, out):
+    x = info[0]
+    for rr in range(2):
+        for cc in range(2):
+            for p in range(2):
+                tiles = (own, side)[cc]
+                mirror = (mirror_own, mirror_side)[rr]
+                swapped = jnp.where(x == 0, 1 - p, p)
+                here = tiles[rr ^ x, p].astype(jnp.float32)
+                there = mirror[cc ^ x, swapped].astype(jnp.float32)
+                out[p, pl.ds(rr * 128, 128), pl.ds(cc * 128, 128)] = (here - there.T).astype(jnp.bfloat16)
+
+
+def halves_kernel(vectors, info, e_ref, ce_ref, xe_ref, cxe_ref, a0, a1, a2, a3, d0, d1, d2, d3, c0, c1, out, col, amp, rowm, col_sem, amp_sem):
+    x, core, g = info[0], info[1], info[2]
+    col_copies = []
+    for half in range(2):
+        for t in range(2):
+            for rt in range(2):
+                n = half * 4 + t * 2 + rt
+                slot = g ^ (half + 2 * t)
+                dst = col.at[slot, :, pl.ds(pl.multiple_of((rt ^ x) * 128, 128), 128), :]
+                for which, srcs in enumerate(((e_ref, ce_ref), (xe_ref, cxe_ref))):
+                    copy = pltpu.make_async_copy(srcs[half].at[t, rt], dst, col_sem.at[n])
+                    pl.when(core == which)(copy.start)
+                col_copies.append(copy)
+    slots = [g, g ^ 2, g ^ 1, g ^ 3]
+    for m in (0, 2, 1, 3):
+        h = g ^ m
+        slots.append(jnp.where(h == 0, 7, jnp.where(h == 1, 4, jnp.where(h == 2, 9, 5))))
+    slots += [6 + 2 * (g & 1), 8 - 2 * (g & 1)]
+    amp_copies = []
+    for n, (ref, slot) in enumerate(zip((a0, a2, a1, a3, d0, d2, d1, d3, c0, c1), slots)):
+        copy = pltpu.make_async_copy(ref, amp.at[slot], amp_sem.at[n])
+        copy.start()
+        amp_copies.append(copy)
+    for copy in col_copies:
+        copy.wait()
+    for w in range(PLANES):
+        for q in range(vectors):
+            rowm[w, pl.ds(q * 128, 128), :] = col[w, q].T
+    for copy in amp_copies:
+        copy.wait()
+    for w in range(PLANES):
+        for p in range(2):
+            total = None
+            for j in range(PLANES):
+                if j <= w:
+                    term = lax.dot_general(
+                        rowm[j], amp[SLOT_OF[w, j], p], (((1,), (1,)), ((), ())), preferred_element_type=jnp.float32
+                    )
+                    total = term if total is None else total + term
+                else:
+                    swapped = jnp.where(x == 0, 1 - p, p)
+                    term = jnp.dot(rowm[j], amp[SLOT_OF[j, w], swapped], preferred_element_type=jnp.float32)
+                    total = -term if total is None else total - term
+            total = total.astype(jnp.bfloat16)
+            for q in range(vectors):
+                out[w, q, pl.ds(p * 128, 128), :] = total[q * 128 : (q + 1) * 128]
+
+
+def ladder_kernel(vectors, info, *refs):
+    own = refs[:4]
+    far = refs[4:16]
+    halves, out, mat, sem = refs[16:]
+    x, core, g = info[0], info[1], info[2]
+    copies = []
+
+    def load(src, slot, cc, rt):
+        dst = mat.at[slot, :, pl.ds(pl.multiple_of((rt ^ x) * 128, 128), 128), pl.ds(cc * 128, 128)]
+        copy = pltpu.make_async_copy(src, dst, sem.at[len(copies)])
+        copy.start()
+        copies.append(copy)
+
+    for cc in range(2):
+        for half in range(2):
+            ref = own[cc * 2 + half]
+            for t in range(2):
+                for rt in range(2):
+                    load(ref.at[t, rt], g ^ (half + 2 * t), cc, rt)
+    for group in range(3):
+        for cc in range(2):
+            for half in range(2):
+                ref = far[group * 4 + cc * 2 + half]
+                for rt in range(2):
+                    load(ref.at[rt], 4 + 2 * group + (core ^ half), cc, rt)
+    for copy in copies:
+        copy.wait()
+    for w in range(PLANES):
+        def step(q, total):
+            for j in range(PLANES):
+                if j <= w:
+                    total = total + lax.dot_general(
+                        halves[j, q], mat[SLOT_OF[w, j], q], (((1,), (1,)), ((), ())), preferred_element_type=jnp.float32
+                    )
+                else:
+                    total = total + jnp.dot(halves[j, q], mat[SLOT_OF[j, w], q], preferred_element_type=jnp.float32)
+            return total
+
+        total = jnp.zeros((256, 256), jnp.float32)
+        for q in range(vectors):
+            total = step(q, total)
+        for rr in range(2):
+            for p in range(2):
+                out[w, rr, p] = total[p * 128 : (p + 1) * 128, rr * 128 : (rr + 1) * 128].T.astype(jnp.bfloat16)
+
+
+SMEM = pl.BlockSpec(memory_space=pltpu.SMEM)
+VMEM = pl.BlockSpec(memory_space=pltpu.VMEM)
+ANY = pl.BlockSpec(memory_space=pl.ANY)
+
+
+def fast_body(amplitudes, cholesky, tile_mask):
+    vectors = cholesky.shape[2] // 2
+    r, k = lax.axis_index("row"), lax.axis_index("col")
+    y, core, z, x = r >> 1, r & 1, k >> 1, k & 1
+    g = r ^ z
+    info = jnp.stack([x, core, g, y]).astype(jnp.int32)
+
+    factors = cholesky[:, 0]
+    kept = lax.dynamic_slice_in_dim(factors, y * vectors, vectors, 1)
+    given = lax.dynamic_slice_in_dim(factors, (1 - y) * vectors, vectors, 1)
+    e = jnp.stack([kept, swap_y(given)])
+    ce = swap_core(e)
+    every = jnp.concatenate([e, ce])
+
+    def piece(s):
+        m = s ^ g
+        return lax.dynamic_index_in_dim(every, (m >> 1) + 2 * (m & 1), 0, keepdims=False)
+
+    far = []
+    for by_core in (((0, 1), (2, 1)), ((0, 2), (1, 2)), ((0, 3), (3, 1))):
+        s = jnp.where(core == 0, by_core[0][0], by_core[1][0])
+        got = move(piece(s), lambda r, z, x: (r, z ^ by_core[r & 1][1], x))
+        beside = swap_x(got)
+        far += [got, swap_core(got), beside, swap_core(beside)]
+    xe = swap_x(e)
+    cxe = swap_core(xe)
+
+    masked = jnp.where(tile_mask[:, :, None, None, None] != 0, amplitudes, jnp.bfloat16(0))[:, 0]
+    crossed = masked[:, 1:3]
+    straight = jnp.stack([masked[:, 0], masked[:, 3]], axis=1)
+    own_pairs = jnp.where(x == 0, crossed, straight)
+    other_pairs = jnp.where(x == 0, straight, crossed)
+    beside = swap_x(other_pairs)
+    mirror_own = move(own_pairs, lambda r, z, x: (z, r, x))
+    mirror_beside = move(other_pairs, lambda r, z, x: (z, r, x ^ 1))
+    a0 = pl.pallas_call(
+        antisym_kernel,
+        out_shape=jax.ShapeDtypeStruct((2, 256, 256), jnp.bfloat16),
+        in_specs=[SMEM] + [VMEM] * 4,
+        out_specs=VMEM,
+        cost_estimate=pl.CostEstimate(flops=1 << 20, bytes_accessed=3 << 20, transcendentals=0),
+    )(info, own_pairs, beside, mirror_own, mirror_beside)
+    a2 = swap_y(a0)
+    a1, a3 = swap_core(a0), swap_core(a2)
+    d0 = move(a0, lambda r, z, x: (r ^ 3, z ^ 2, x) if r ^ z == 1 else (r, z ^ 1, x))
+    d2 = swap_y(d0)
+    d1, d3 = swap_core(d0), swap_core(d2)
+    far2 = move(a0, lambda r, z, x: (r, z ^ 2, x) if r == z else None)
+    far3 = move(a0, lambda r, z, x: (r, z ^ 3, x) if r == z else None)
+    c0 = jnp.where(g == 2, far2, far3)
+    c_other = move(c0, lambda r, z, x: (r ^ 2, z, x) if r ^ z >= 2 else None)
+    c0 = jnp.where(g >= 2, c0, c_other)
+    c1 = swap_core(c0)
+
+    halves = pl.pallas_call(
+        functools.partial(halves_kernel, vectors),
+        out_shape=jax.ShapeDtypeStruct((PLANES, vectors, 256, 256), jnp.bfloat16),
+        in_specs=[SMEM] + [ANY] * 14,
+        out_specs=VMEM,
+        scratch_shapes=[
+            pltpu.VMEM((PLANES, vectors, 256, 128), jnp.bfloat16),
+            pltpu.VMEM((BLOCKS, 2, 256, 256), jnp.bfloat16),
+            pltpu.VMEM((PLANES, vectors * 128, 256), jnp.bfloat16),
+            pltpu.SemaphoreType.DMA((8,)),
+            pltpu.SemaphoreType.DMA((10,)),
+        ],
+        compiler_params=pltpu.CompilerParams(vmem_limit_bytes=40 << 20),
+        cost_estimate=pl.CostEstimate(flops=2700 << 20, bytes_accessed=8 << 20, transcendentals=0),
+    )(info, e, ce, xe, cxe, a0, a1, a2, a3, d0, d1, d2, d3, c0, c1)
+
+    partial = pl.pallas_call(
+        functools.partial(ladder_kernel, vectors),
+        out_shape=jax.ShapeDtypeStruct((PLANES, 2, 2, 128, 128), jnp.bfloat16),
+        in_specs=[SMEM] + [ANY] * 16 + [VMEM],
+        out_specs=VMEM,
+        scratch_shapes=[
+            pltpu.VMEM((BLOCKS, vectors, 256, 256), jnp.bfloat16),
+            pltpu.SemaphoreType.DMA((40,)),
+        ],
+        compiler_params=pltpu.CompilerParams(vmem_limit_bytes=40 << 20),
+        cost_estimate=pl.CostEstimate(flops=2700 << 20, bytes_accessed=12 << 20, transcendentals=0),
+    )(info, e, ce, xe, cxe, *far, halves)
+
+    sums = []
+    for m in range(ROWS):
+        part = lax.dynamic_index_in_dim(partial, g ^ m, 0, keepdims=False)
+        sums.append(move(part, lambda r, z, x, m=m: (r ^ m, z, x ^ (r & 1))).astype(jnp.float32))
+    same, other = sums[0] + sums[2], sums[1] + sums[3]
+    mine = (x ^ core) == 0
+    crossed = jnp.where(mine, same, other)
+    straight = jnp.where(mine, other, same)[::-1]
+    result = jnp.stack([straight[:, 0], crossed[:, 0], crossed[:, 1], straight[:, 1]], axis=1)
+    return result.astype(jnp.bfloat16)[:, None]
 
 
 def from_partner(value, axis, apart):
@@ -42,7 +281,7 @@
     return tile_set
 
 
-def body(amplitudes, cholesky, tile_mask):
+def general_body(amplitudes, cholesky, tile_mask):
     tile_rows = amplitudes.shape[0]
     pair_count = amplitudes.shape[2]
     tile_edge = amplitudes.shape[3]
@@ -79,6 +318,14 @@
     return result_tiles.reshape(tile_rows, 1, pair_count, tile_edge, tile_edge)
 
 
+def body(amplitudes, cholesky, tile_mask):
+    rows, cols = lax.axis_size("row"), lax.axis_size("col")
+    fits = amplitudes.shape == (2, 1, 4, 128, 128) and cholesky.shape[2] % 2 == 0
+    if rows == ROWS and cols == 2 * PLANES and fits:
+        return fast_body(amplitudes, cholesky, tile_mask)
+    return general_body(amplitudes, cholesky, tile_mask)
+
+
 def solution(mesh):
     in_specs = (
         P("row", "col", None, None, None),

time: 265 us -> 140 us (0.53)
  waiting for transfers between devices: 153 us -> 49.5 us
  blocking collectives: 62.5 us -> 0 us
  starting transfers between devices: 7.09 us -> 60 us
  between operations: 13.9 us -> 0.36 us
  Pallas kernels: 0 us -> 13.3 us
  matrix products: 12.1 us -> 0 us
    all_gather x3 -> x0, waiting for transfers between devices: 124 us -> none  [the longest x1 72.9 us: body(): spread = lax.all_gather(cholesky, 'col', axis=1, tiled=True)]
    ppermute x7 -> x34, starting transfers between devices: 7.02 us -> 60 us  [move(): return lax.ppermute(value, ('row', 'col'), pairs)]
    unnamed x1 -> x0, blocking collectives: 40.2 us -> none
    ppermute x7 -> x34, waiting for transfers between devices: 27.2 us -> 49.5 us  [move(): return lax.ppermute(value, ('row', 'col'), pairs)]
    all_gather x1 -> x0, blocking collectives: 22.3 us -> none  [body(): mask_block = lax.all_gather(tile_mask, 'col', axis=1, tiled=True)]
    pallas_call x0 -> x3, Pallas kernels: none -> 13.3 us  [the longest x1 6.28 us: fast_body(): pl.pallas_call(functools.partial(ladder_kernel, vectors), out_shape=jax.S...]
    dot_general x2 -> x0, matrix products: 12.1 us -> none  [the longest x1 6.13 us: body(): jnp.einsum('caqux,cpuqy->apxy', spread, halves, preferred_element_type=jn...]
    unnamed x2 -> x48, local copies, waits for them, and re-layouts: 1.26 us -> 11.4 us
  transfers between devices with their start and end apart: 10 -> 34, of which waited for: 10 -> 15; matrix products, arithmetic and copies ran while one was open for 8% -> 2% of each run, Pallas kernels for 0% -> 5%
where the time goes in v1:
time: 140 us; the launch traced here: 139 us
  starting transfers between devices  60 us (43%)
  waiting for transfers between devices  49.5 us (35%)
  Pallas kernels  13.3 us (10%)
  local copies, waits for them, and re-layouts  12.7 us (9%)
  other arithmetic  3.56 us (3%)
    ppermute x34, starting transfers between devices, move(): return lax.ppermute(value, ('row', 'col'), pairs)  60 us
    ppermute x34, waiting for transfers between devices, move(): return lax.ppermute(value, ('row', 'col'), pairs)  49.5 us
    unnamed x48, local copies, waits for them, and re-layouts  11.4 us
    pallas_call x1, Pallas kernels, fast_body(): pl.pallas_call(functools.partial(ladder_kernel, vectors), out_shape=jax.S...  6.28 us
    pallas_call x1, Pallas kernels, fast_body(): pl.pallas_call(functools.partial(halves_kernel, vectors), out_shape=jax.S...  5.08 us
  transfers between devices with their start and end apart: 34, of which 15 were waited for; matrix products, arithmetic and copies ran while one was open for 2% of the time, Pallas kernels for 5%

profile of v1, /device:TPU:0, one launch (start us, length us, event | category | flops | bytes accessed | tf_op | source)
XLA Modules:
  0.0 139.5 jit_solution(9776804260794833035)
XLA Ops:
  0.0 1.2 dynamic-slice_bitcast_fusion.4
  1.2 3.0 %collective-permute-start = (bf16[2,5,128,128]{3,2,1,0:T(8,128)(2,1)S(1)}, bf16[2,5,128,128]{3,2,1,0:T(8,128)(2,1)S(1)}, u32[]{:S(2)}, u32[]{:S(2)}) collective-permute-start(bf16[2,5,128,128]{3,2,1,0:T(8,128)(2,1)S(1)} %get-tuple-element.9), channel_id=1, source_target_pairs={{0,16},{1,17},{2,18},{3,19},{4,20},{5,21},{6,22},{7,23},{8,24},{9,... | collective-permute-start | bytes 983048 | tf_op jit(solution)/shard_map/ppermute | solution.py:26
  4.4 1.6 %collective-permute-start.16 = (bf16[2,2,128,128]{3,2,1,0:T(8,128)(2,1)S(1)}, bf16[2,2,128,128]{3,2,1,0:T(8,128)(2,1)S(1)}, u32[]{:S(2)}, u32[]{:S(2)}) collective-permute-start(bf16[2,2,128,128]{3,2,1,0:T(8,128)(2,1)S(1)} %get-tuple-element.14), channel_id=1, source_target_pairs={{0,1},{1,0},{2,3},{3,2},{4,5},{5,4},{6,7},{7,6},{8,9},{9,8},{10,11... | collective-permute-start | bytes 393224 | tf_op jit(solution)/shard_map/ppermute | solution.py:26
  7.8 1.6 %collective-permute-done.16.side = bf16[2,2,128,128]{3,2,1,0:T(8,128)(2,1)S(1)} collective-permute-done((bf16[2,2,128,128]{3,2,1,0:T(8,128)(2,1)S(1)}, bf16[2,2,128,128]{3,2,1,0:T(8,128)(2,1)S(1)}, u32[]{:S(2)}, u32[]{:S(2)}) %collective-permute-start.16) | collective-permute-done | bytes 131104 | tf_op jit(solution)/shard_map/ppermute | solution.py:26
  9.4 2.2 %collective-permute-done.18.mirror_side = bf16[2,2,128,128]{3,2,1,0:T(8,128)(2,1)S(1)} collective-permute-done((bf16[2,2,128,128]{3,2,1,0:T(8,128)(2,1)S(1)}, bf16[2,2,128,128]{3,2,1,0:T(8,128)(2,1)S(1)}, u32[]{:S(2)}, u32[]{:S(2)}) %collective-permute-start.18) | collective-permute-done | bytes 131104 | tf_op jit(solution)/shard_map/ppermute | solution.py:26
  12.3 2.0 %shard_map.37.a0 = bf16[2,256,256]{2,1,0:T(8,128)(2,1)} custom-call(s32[4]{0:T(128)} %pad_add_fusion.info, bf16[2,2,128,128]{3,2,1,0:T(8,128)(2,1)} %copy-done.18, bf16[2,2,128,128]{3,2,1,0:T(8,128)(2,1)} %copy-done.20, bf16[2,2,128,128]{3,2,1,0:T(8,128)(2,1)} %copy-done.21, bf16[2,2,128,128]{3,2,1,0:T(8,128)(2,1)} %copy-done.22), custom_call_target="tpu_custom_call" | custom-call | flops 1048576 | bytes 3145728 | tf_op jit(solution)/shard_map/pallas_call | solution.py:188
  14.2 12.8 %collective-permute-start.26 = (bf16[2,256,256]{2,1,0:T(8,128)(2,1)}, bf16[2,256,256]{2,1,0:T(8,128)(2,1)S(1)}, u32[]{:S(2)}, u32[]{:S(2)}) collective-permute-start(bf16[2,256,256]{2,1,0:T(8,128)(2,1)} %shard_map.37.a0), channel_id=1, source_target_pairs={{0,4},{1,5},{10,14},{11,15},{20,16},{21,17},{30,26},{31,27}} | collective-permute-start | bytes 786440 | tf_op jit(solution)/shard_map/ppermute | solution.py:26
  27.1 1.3 collective-permute-start.27
  28.6 4.3 %collective-permute-start.1 = (bf16[2,2,5,128,128]{4,3,2,1,0:T(8,128)(2,1)S(1)}, bf16[2,2,5,128,128]{4,3,2,1,0:T(8,128)(2,1)S(1)}, u32[]{:S(2)}, u32[]{:S(2)}) collective-permute-start(bf16[2,2,5,128,128]{4,3,2,1,0:T(8,128)(2,1)S(1)} %pad_maximum_fusion.1.e_ref.refs_0_), channel_id=1, source_target_pairs={{0,8},{1,9},{2,10},{3,11},{4,12},{5,13},{6,14},{7,15},{8,0},{9,1},... | collective-permute-start | bytes 1966088 | tf_op jit(solution)/shard_map/ppermute | solution.py:26
  32.9 1.9 %collective-permute-done.27 = bf16[2,256,256]{2,1,0:T(8,128)(2,1)S(1)} collective-permute-done((bf16[2,256,256]{2,1,0:T(8,128)(2,1)}, bf16[2,256,256]{2,1,0:T(8,128)(2,1)S(1)}, u32[]{:S(2)}, u32[]{:S(2)}) %collective-permute-start.27) | collective-permute-done | bytes 262176 | tf_op jit(solution)/shard_map/ppermute | solution.py:26
  35.5 1.3 collective-permute-start.28
  36.9 12.0 %collective-permute-start.20 = (bf16[2,256,256]{2,1,0:T(8,128)(2,1)S(1)}, bf16[2,256,256]{2,1,0:T(8,128)(2,1)}, u32[]{:S(2)}, u32[]{:S(2)}) collective-permute-start(bf16[2,256,256]{2,1,0:T(8,128)(2,1)S(1)} %copy-done), channel_id=1, source_target_pairs={{0,16},{1,17},{2,18},{3,19},{4,20},{5,21},{6,22},{7,23},{8,24},{9,... | collective-permute-start | bytes 786440 | tf_op jit(solution)/shard_map/ppermute | solution.py:26
  48.9 3.3 %collective-permute-done.28 = bf16[2,256,256]{2,1,0:T(8,128)(2,1)} collective-permute-done((bf16[2,256,256]{2,1,0:T(8,128)(2,1)}, bf16[2,256,256]{2,1,0:T(8,128)(2,1)}, u32[]{:S(2)}, u32[]{:S(2)}) %collective-permute-start.28) | collective-permute-done | bytes 262176 | tf_op jit(solution)/shard_map/ppermute | solution.py:26
  52.2 1.0 broadcast_select_fusion.1.c0
  53.2 4.5 %collective-permute-done.20.a2 = bf16[2,256,256]{2,1,0:T(8,128)(2,1)} collective-permute-done((bf16[2,256,256]{2,1,0:T(8,128)(2,1)S(1)}, bf16[2,256,256]{2,1,0:T(8,128)(2,1)}, u32[]{:S(2)}, u32[]{:S(2)}) %collective-permute-start.20) | collective-permute-done | bytes 262176 | tf_op jit(solution)/shard_map/ppermute | solution.py:26
  58.5 2.0 %collective-permute-done.24.d2 = bf16[2,256,256]{2,1,0:T(8,128)(2,1)S(1)} collective-permute-done((bf16[2,256,256]{2,1,0:T(8,128)(2,1)}, bf16[2,256,256]{2,1,0:T(8,128)(2,1)S(1)}, u32[]{:S(2)}, u32[]{:S(2)}) %collective-permute-start.24) | collective-permute-done | bytes 262176 | tf_op jit(solution)/shard_map/ppermute | solution.py:26
  60.6 7.5 %collective-permute-start.8 = (bf16[2,5,128,128]{3,2,1,0:T(8,128)(2,1)S(1)}, bf16[2,5,128,128]{3,2,1,0:T(8,128)(2,1)S(1)}, u32[]{:S(2)}, u32[]{:S(2)}) collective-permute-start(bf16[2,5,128,128]{3,2,1,0:T(8,128)(2,1)S(1)} %get-tuple-element.6), channel_id=1, source_target_pairs={{0,4},{1,5},{2,6},{3,7},{4,0},{5,1},{6,2},{7,3},{8,12},{9,13},{10,... | collective-permute-start | bytes 983048 | tf_op jit(solution)/shard_map/ppermute | solution.py:26
  68.7 3.6 %collective-permute-start.12 = (bf16[2,5,128,128]{3,2,1,0:T(8,128)(2,1)S(1)}, bf16[2,5,128,128]{3,2,1,0:T(8,128)(2,1)S(1)}, u32[]{:S(2)}, u32[]{:S(2)}) collective-permute-start(bf16[2,5,128,128]{3,2,1,0:T(8,128)(2,1)S(1)} %get-tuple-element.5), channel_id=1, source_target_pairs={{0,6},{1,7},{2,4},{3,5},{4,2},{5,3},{6,0},{7,1},{8,10},{9,11},{10,... | collective-permute-start | bytes 983048 | tf_op jit(solution)/shard_map/ppermute | solution.py:26
  74.5 9.8 %collective-permute-done.8.refs_8_ = bf16[2,5,128,128]{3,2,1,0:T(8,128)(2,1)S(1)} collective-permute-done((bf16[2,5,128,128]{3,2,1,0:T(8,128)(2,1)S(1)}, bf16[2,5,128,128]{3,2,1,0:T(8,128)(2,1)S(1)}, u32[]{:S(2)}, u32[]{:S(2)}) %collective-permute-start.8) | collective-permute-done | bytes 327712 | tf_op jit(solution)/shard_map/ppermute | solution.py:26
  84.5 2.6 %collective-permute-done.12.refs_12_ = bf16[2,5,128,128]{3,2,1,0:T(8,128)(2,1)S(1)} collective-permute-done((bf16[2,5,128,128]{3,2,1,0:T(8,128)(2,1)S(1)}, bf16[2,5,128,128]{3,2,1,0:T(8,128)(2,1)S(1)}, u32[]{:S(2)}, u32[]{:S(2)}) %collective-permute-start.12) | collective-permute-done | bytes 327712 | tf_op jit(solution)/shard_map/ppermute | solution.py:26
  87.7 1.6 %collective-permute-done.4.refs_4_ = bf16[2,5,128,128]{3,2,1,0:T(8,128)(2,1)} collective-permute-done((bf16[2,5,128,128]{3,2,1,0:T(8,128)(2,1)S(1)}, bf16[2,5,128,128]{3,2,1,0:T(8,128)(2,1)}, u32[]{:S(2)}, u32[]{:S(2)}) %collective-permute-start.4) | collective-permute-done | bytes 327712 | tf_op jit(solution)/shard_map/ppermute | solution.py:26
  91.6 3.4 %collective-permute-done.10.refs_10_ = bf16[2,5,128,128]{3,2,1,0:T(8,128)(2,1)} collective-permute-done((bf16[2,5,128,128]{3,2,1,0:T(8,128)(2,1)S(1)}, bf16[2,5,128,128]{3,2,1,0:T(8,128)(2,1)}, u32[]{:S(2)}, u32[]{:S(2)}) %collective-permute-start.10) | collective-permute-done | bytes 327712 | tf_op jit(solution)/shard_map/ppermute | solution.py:26
  95.0 6.4 %collective-permute-done.14.refs_14_ = bf16[2,5,128,128]{3,2,1,0:T(8,128)(2,1)} collective-permute-done((bf16[2,5,128,128]{3,2,1,0:T(8,128)(2,1)S(1)}, bf16[2,5,128,128]{3,2,1,0:T(8,128)(2,1)}, u32[]{:S(2)}, u32[]{:S(2)}) %collective-permute-start.14) | collective-permute-done | bytes 327712 | tf_op jit(solution)/shard_map/ppermute | solution.py:26
  101.4 3.5 %collective-permute-done.6.refs_6_ = bf16[2,5,128,128]{3,2,1,0:T(8,128)(2,1)} collective-permute-done((bf16[2,5,128,128]{3,2,1,0:T(8,128)(2,1)}, bf16[2,5,128,128]{3,2,1,0:T(8,128)(2,1)}, u32[]{:S(2)}, u32[]{:S(2)}) %collective-permute-start.6) | collective-permute-done | bytes 327712 | tf_op jit(solution)/shard_map/ppermute | solution.py:26
  106.1 0.9 copy-done.7
  108.0 0.9 copy-done.11
  111.8 5.1 %shard_map.38.refs_16_ = bf16[4,5,256,256]{3,2,1,0:T(8,128)(2,1)S(1)} custom-call(s32[4]{0:T(128)S(1)} %copy-done.1, bf16[2,2,5,128,128]{4,3,2,1,0:T(8,128)(2,1)S(1)} %pad_maximum_fusion.1.e_ref.refs_0_, bf16[2,2,5,128,128]{4,3,2,1,0:T(8,128)(2,1)S(1)} %collective-permute-done.1.ce_ref.refs_1_, ...), custom_call_target="tpu_custom_call" | custom-call | flops 2831155200 | bytes 8388608 | tf_op jit(solution)/shard_map/pallas_call | solution.py:207
  117.0 6.3 %shard_map.39 = bf16[4,2,2,128,128]{4,3,2,1,0:T(8,128)(2,1)S(1)} custom-call(s32[4]{0:T(128)S(1)} %copy-done.1, bf16[2,2,5,128,128]{4,3,2,1,0:T(8,128)(2,1)S(1)} %pad_maximum_fusion.1.e_ref.refs_0_, bf16[2,2,5,128,128]{4,3,2,1,0:T(8,128)(2,1)S(1)} %collective-permute-done.1.ce_ref.refs_1_, ...), custom_call_target="tpu_custom_call" | custom-call | flops 2831155200 | bytes 12582912 | tf_op jit(solution)/shard_map/pallas_call | solution.py:223
  124.0 5.7 %collective-permute-start.33 = (bf16[2,2,128,128]{3,2,0,1:T(8,128)(2,1)S(1)}, bf16[2,2,128,128]{3,2,0,1:T(8,128)(2,1)S(1)}, u32[]{:S(2)}, u32[]{:S(2)}) collective-permute-start(bf16[2,2,128,128]{3,2,0,1:T(8,128)(2,1)S(1)} %copy.9), channel_id=1, source_target_pairs={{0,16},{1,17},{2,18},{3,19},{4,20},{5,21},{6,22},{7,23},{8,25},{9,... | collective-permute-start | bytes 393224 | tf_op jit(solution)/shard_map/ppermute | solution.py:26
  129.8 2.1 %collective-permute-start.30 = (bf16[2,2,128,128]{3,2,1,0:T(8,128)(2,1)S(1)}, bf16[2,2,128,128]{3,2,1,0:T(8,128)(2,1)S(1)}, u32[]{:S(2)}, u32[]{:S(2)}) collective-permute-start(bf16[2,2,128,128]{3,2,1,0:T(8,128)(2,1)S(1)} %get-tuple-element.13), channel_id=1, source_target_pairs={{0,8},{1,9},{2,10},{3,11},{4,12},{5,13},{6,14},{7,15},{8,1},{9,0},... | collective-permute-start | bytes 393224 | tf_op jit(solution)/shard_map/ppermute | solution.py:26
  132.7 3.2 %collective-permute-done.30 = bf16[2,2,128,128]{3,2,1,0:T(8,128)(2,1)S(1)} collective-permute-done((bf16[2,2,128,128]{3,2,1,0:T(8,128)(2,1)S(1)}, bf16[2,2,128,128]{3,2,1,0:T(8,128)(2,1)S(1)}, u32[]{:S(2)}, u32[]{:S(2)}) %collective-permute-start.30) | collective-permute-done | bytes 131104 | tf_op jit(solution)/shard_map/ppermute | solution.py:26
  135.9 2.6 %collective-permute-done.31 = bf16[2,2,128,128]{3,2,1,0:T(8,128)(2,1)S(1)} collective-permute-done((bf16[2,2,128,128]{3,2,1,0:T(8,128)(2,1)S(1)}, bf16[2,2,128,128]{3,2,1,0:T(8,128)(2,1)S(1)}, u32[]{:S(2)}, u32[]{:S(2)}) %collective-permute-start.31) | collective-permute-done | bytes 131104 | tf_op jit(solution)/shard_map/ppermute | solution.py:26
  (106 shorter events, 17.9 us)
Async XLA Ops:
  1.2 27.3 %collective-permute-start = (bf16[2,5,128,128]{3,2,1,0:T(8,128)(2,1)S(1)}, bf16[2,5,128,128]{3,2,1,0:T(8,128)(2,1)S(1)}, u32[]{:S(2)}, u32[]{:S(2)}) collective-permute-start(bf16[2,5,128,128]{3,2,1,0:T(8,128)(2,1)S(1)} %get-tuple-element.9), channel_id=1, source_target_pairs={{0,16},{1,17},{2,18},{3,19},{4,20},{5,21},{6,22},{7,23},{8,24},{9,... | collective-permute-start | bytes 983048 | tf_op jit(solution)/shard_map/ppermute | solution.py:26
  4.4 5.0 %collective-permute-start.16 = (bf16[2,2,128,128]{3,2,1,0:T(8,128)(2,1)S(1)}, bf16[2,2,128,128]{3,2,1,0:T(8,128)(2,1)S(1)}, u32[]{:S(2)}, u32[]{:S(2)}) collective-permute-start(bf16[2,2,128,128]{3,2,1,0:T(8,128)(2,1)S(1)} %get-tuple-element.14), channel_id=1, source_target_pairs={{0,1},{1,0},{2,3},{3,2},{4,5},{5,4},{6,7},{7,6},{8,9},{9,8},{10,11... | collective-permute-start | bytes 393224 | tf_op jit(solution)/shard_map/ppermute | solution.py:26
  14.2 18.6 %collective-permute-start.26 = (bf16[2,256,256]{2,1,0:T(8,128)(2,1)}, bf16[2,256,256]{2,1,0:T(8,128)(2,1)S(1)}, u32[]{:S(2)}, u32[]{:S(2)}) collective-permute-start(bf16[2,256,256]{2,1,0:T(8,128)(2,1)} %shard_map.37.a0), channel_id=1, source_target_pairs={{0,4},{1,5},{10,14},{11,15},{20,16},{21,17},{30,26},{31,27}} | collective-permute-start | bytes 786440 | tf_op jit(solution)/shard_map/ppermute | solution.py:26
  27.1 7.7 %collective-permute-start.27 = (bf16[2,256,256]{2,1,0:T(8,128)(2,1)}, bf16[2,256,256]{2,1,0:T(8,128)(2,1)S(1)}, u32[]{:S(2)}, u32[]{:S(2)}) collective-permute-start(bf16[2,256,256]{2,1,0:T(8,128)(2,1)} %shard_map.37.a0), channel_id=1, source_target_pairs={{0,6},{1,7},{10,12},{11,13},{20,18},{21,19},{30,24},{31,25}} | collective-permute-start | bytes 786440 | tf_op jit(solution)/shard_map/ppermute | solution.py:26
  28.4 20.5 %collective-permute-start.22 = (bf16[2,256,256]{2,1,0:T(8,128)(2,1)}, bf16[2,256,256]{2,1,0:T(8,128)(2,1)}, u32[]{:S(2)}, u32[]{:S(2)}) collective-permute-start(bf16[2,256,256]{2,1,0:T(8,128)(2,1)} %shard_map.37.a0), channel_id=1, source_target_pairs={{0,2},{1,3},{2,30},{3,31},{4,6},{5,7},{6,4},{7,5},{8,20},{9,21},{1... | collective-permute-start | bytes 786440 | tf_op jit(solution)/shard_map/ppermute | solution.py:26
  28.6 29.7 %collective-permute-start.1 = (bf16[2,2,5,128,128]{4,3,2,1,0:T(8,128)(2,1)S(1)}, bf16[2,2,5,128,128]{4,3,2,1,0:T(8,128)(2,1)S(1)}, u32[]{:S(2)}, u32[]{:S(2)}) collective-permute-start(bf16[2,2,5,128,128]{4,3,2,1,0:T(8,128)(2,1)S(1)} %pad_maximum_fusion.1.e_ref.refs_0_), channel_id=1, source_target_pairs={{0,8},{1,9},{2,10},{3,11},{4,12},{5,13},{6,14},{7,15},{8,0},{9,1},... | collective-permute-start | bytes 1966088 | tf_op jit(solution)/shard_map/ppermute | solution.py:26
  35.5 16.7 %collective-permute-start.28 = (bf16[2,256,256]{2,1,0:T(8,128)(2,1)}, bf16[2,256,256]{2,1,0:T(8,128)(2,1)}, u32[]{:S(2)}, u32[]{:S(2)}) collective-permute-start(bf16[2,256,256]{2,1,0:T(8,128)(2,1)} %broadcast_select_fusion), channel_id=1, source_target_pairs={{4,20},{5,21},{6,22},{7,23},{12,28},{13,29},{14,30},{15,31},{16,0}... | collective-permute-start | bytes 786440 | tf_op jit(solution)/shard_map/ppermute | solution.py:26
  36.8 31.2 %collective-permute-start.2 = (bf16[2,2,5,128,128]{4,3,2,1,0:T(8,128)(2,1)S(1)}, bf16[2,2,5,128,128]{4,3,2,1,0:T(8,128)(2,1)S(1)}, u32[]{:S(2)}, u32[]{:S(2)}) collective-permute-start(bf16[2,2,5,128,128]{4,3,2,1,0:T(8,128)(2,1)S(1)} %pad_maximum_fusion.1.e_ref.refs_0_), channel_id=1, source_target_pairs={{0,1},{1,0},{2,3},{3,2},{4,5},{5,4},{6,7},{7,6},{8,9},{9,8},{10,11... | collective-permute-start | bytes 1966088 | tf_op jit(solution)/shard_map/ppermute | solution.py:26
  36.9 20.8 %collective-permute-start.20 = (bf16[2,256,256]{2,1,0:T(8,128)(2,1)S(1)}, bf16[2,256,256]{2,1,0:T(8,128)(2,1)}, u32[]{:S(2)}, u32[]{:S(2)}) collective-permute-start(bf16[2,256,256]{2,1,0:T(8,128)(2,1)S(1)} %copy-done), channel_id=1, source_target_pairs={{0,16},{1,17},{2,18},{3,19},{4,20},{5,21},{6,22},{7,23},{8,24},{9,... | collective-permute-start | bytes 786440 | tf_op jit(solution)/shard_map/ppermute | solution.py:26
  48.9 8.8 %collective-permute-start.19 = (bf16[2,256,256]{2,1,0:T(8,128)(2,1)S(1)}, bf16[2,256,256]{2,1,0:T(8,128)(2,1)S(1)}, u32[]{:S(2)}, u32[]{:S(2)}) collective-permute-start(bf16[2,256,256]{2,1,0:T(8,128)(2,1)S(1)} %copy-done), channel_id=1, source_target_pairs={{0,8},{1,9},{2,10},{3,11},{4,12},{5,13},{6,14},{7,15},{8,0},{9,1},... | collective-permute-start | bytes 786440 | tf_op jit(solution)/shard_map/ppermute | solution.py:26
  52.2 8.3 %collective-permute-start.24 = (bf16[2,256,256]{2,1,0:T(8,128)(2,1)}, bf16[2,256,256]{2,1,0:T(8,128)(2,1)S(1)}, u32[]{:S(2)}, u32[]{:S(2)}) collective-permute-start(bf16[2,256,256]{2,1,0:T(8,128)(2,1)} %collective-permute-done.22.d0), channel_id=1, source_target_pairs={{0,16},{1,17},{2,18},{3,19},{4,20},{5,21},{6,22},{7,23},{8,24},{9,... | collective-permute-start | bytes 786440 | tf_op jit(solution)/shard_map/ppermute | solution.py:26
  57.7 10.3 %collective-permute-start.23 = (bf16[2,256,256]{2,1,0:T(8,128)(2,1)}, bf16[2,256,256]{2,1,0:T(8,128)(2,1)S(1)}, u32[]{:S(2)}, u32[]{:S(2)}) collective-permute-start(bf16[2,256,256]{2,1,0:T(8,128)(2,1)} %collective-permute-done.22.d0), channel_id=1, source_target_pairs={{0,8},{1,9},{2,10},{3,11},{4,12},{5,13},{6,14},{7,15},{8,0},{9,1},... | collective-permute-start | bytes 786440 | tf_op jit(solution)/shard_map/ppermute | solution.py:26
  57.7 14.6 %collective-permute-start.21 = (bf16[2,256,256]{2,1,0:T(8,128)(2,1)}, bf16[2,256,256]{2,1,0:T(8,128)(2,1)S(1)}, u32[]{:S(2)}, u32[]{:S(2)}) collective-permute-start(bf16[2,256,256]{2,1,0:T(8,128)(2,1)} %collective-permute-done.20.a2), channel_id=1, source_target_pairs={{0,8},{1,9},{2,10},{3,11},{4,12},{5,13},{6,14},{7,15},{8,0},{9,1},... | collective-permute-start | bytes 786440 | tf_op jit(solution)/shard_map/ppermute | solution.py:26
  58.2 14.8 %collective-permute-start.29 = (bf16[2,256,256]{2,1,0:T(8,128)(2,1)S(1)}, bf16[2,256,256]{2,1,0:T(8,128)(2,1)S(1)}, u32[]{:S(2)}, u32[]{:S(2)}) collective-permute-start(bf16[2,256,256]{2,1,0:T(8,128)(2,1)S(1)} %broadcast_select_fusion.1.c0), channel_id=1, source_target_pairs={{0,8},{1,9},{2,10},{3,11},{4,12},{5,13},{6,14},{7,15},{8,0},{9,1},... | collective-permute-start | bytes 786440 | tf_op jit(solution)/shard_map/ppermute | solution.py:26
  60.6 23.7 %collective-permute-start.8 = (bf16[2,5,128,128]{3,2,1,0:T(8,128)(2,1)S(1)}, bf16[2,5,128,128]{3,2,1,0:T(8,128)(2,1)S(1)}, u32[]{:S(2)}, u32[]{:S(2)}) collective-permute-start(bf16[2,5,128,128]{3,2,1,0:T(8,128)(2,1)S(1)} %get-tuple-element.6), channel_id=1, source_target_pairs={{0,4},{1,5},{2,6},{3,7},{4,0},{5,1},{6,2},{7,3},{8,12},{9,13},{10,... | collective-permute-start | bytes 983048 | tf_op jit(solution)/shard_map/ppermute | solution.py:26
  68.0 23.0 %collective-permute-start.3 = (bf16[2,2,5,128,128]{4,3,2,1,0:T(8,128)(2,1)S(1)}, bf16[2,2,5,128,128]{4,3,2,1,0:T(8,128)(2,1)S(1)}, u32[]{:S(2)}, u32[]{:S(2)}) collective-permute-start(bf16[2,2,5,128,128]{4,3,2,1,0:T(8,128)(2,1)S(1)} %collective-permute-done.2.xe_ref.refs_2_), channel_id=1, source_target_pairs={{0,8},{1,9},{2,10},{3,11},{4,12},{5,13},{6,14},{7,15},{8,0},{9,1},... | collective-permute-start | bytes 1966088 | tf_op jit(solution)/shard_map/ppermute | solution.py:26
  68.7 18.4 %collective-permute-start.12 = (bf16[2,5,128,128]{3,2,1,0:T(8,128)(2,1)S(1)}, bf16[2,5,128,128]{3,2,1,0:T(8,128)(2,1)S(1)}, u32[]{:S(2)}, u32[]{:S(2)}) collective-permute-start(bf16[2,5,128,128]{3,2,1,0:T(8,128)(2,1)S(1)} %get-tuple-element.5), channel_id=1, source_target_pairs={{0,6},{1,7},{2,4},{3,5},{4,2},{5,3},{6,0},{7,1},{8,10},{9,11},{10,... | collective-permute-start | bytes 983048 | tf_op jit(solution)/shard_map/ppermute | solution.py:26
  73.0 16.2 %collective-permute-start.4 = (bf16[2,5,128,128]{3,2,1,0:T(8,128)(2,1)S(1)}, bf16[2,5,128,128]{3,2,1,0:T(8,128)(2,1)}, u32[]{:S(2)}, u32[]{:S(2)}) collective-permute-start(bf16[2,5,128,128]{3,2,1,0:T(8,128)(2,1)S(1)} %get-tuple-element.7), channel_id=1, source_target_pairs={{0,2},{1,3},{2,0},{3,1},{4,6},{5,7},{6,4},{7,5},{8,10},{9,11},{10,... | collective-permute-start | bytes 983048 | tf_op jit(solution)/shard_map/ppermute | solution.py:26
  73.7 15.9 %collective-permute-start.25 = (bf16[2,256,256]{2,1,0:T(8,128)(2,1)S(1)}, bf16[2,256,256]{2,1,0:T(8,128)(2,1)S(1)}, u32[]{:S(2)}, u32[]{:S(2)}) collective-permute-start(bf16[2,256,256]{2,1,0:T(8,128)(2,1)S(1)} %collective-permute-done.24.d2), channel_id=1, source_target_pairs={{0,8},{1,9},{2,10},{3,11},{4,12},{5,13},{6,14},{7,15},{8,0},{9,1},... | collective-permute-start | bytes 786440 | tf_op jit(solution)/shard_map/ppermute | solution.py:26
  84.2 10.8 %collective-permute-start.10 = (bf16[2,5,128,128]{3,2,1,0:T(8,128)(2,1)S(1)}, bf16[2,5,128,128]{3,2,1,0:T(8,128)(2,1)}, u32[]{:S(2)}, u32[]{:S(2)}) collective-permute-start(bf16[2,5,128,128]{3,2,1,0:T(8,128)(2,1)S(1)} %collective-permute-done.8.refs_8_), channel_id=1, source_target_pairs={{0,1},{1,0},{2,3},{3,2},{4,5},{5,4},{6,7},{7,6},{8,9},{9,8},{10,11... | collective-permute-start | bytes 983048 | tf_op jit(solution)/shard_map/ppermute | solution.py:26
  87.2 14.2 %collective-permute-start.14 = (bf16[2,5,128,128]{3,2,1,0:T(8,128)(2,1)S(1)}, bf16[2,5,128,128]{3,2,1,0:T(8,128)(2,1)}, u32[]{:S(2)}, u32[]{:S(2)}) collective-permute-start(bf16[2,5,128,128]{3,2,1,0:T(8,128)(2,1)S(1)} %collective-permute-done.12.refs_12_), channel_id=1, source_target_pairs={{0,1},{1,0},{2,3},{3,2},{4,5},{5,4},{6,7},{7,6},{8,9},{9,8},{10,11... | collective-permute-start | bytes 983048 | tf_op jit(solution)/shard_map/ppermute | solution.py:26
  89.3 15.6 %collective-permute-start.6 = (bf16[2,5,128,128]{3,2,1,0:T(8,128)(2,1)}, bf16[2,5,128,128]{3,2,1,0:T(8,128)(2,1)}, u32[]{:S(2)}, u32[]{:S(2)}) collective-permute-start(bf16[2,5,128,128]{3,2,1,0:T(8,128)(2,1)} %collective-permute-done.4.refs_4_), channel_id=1, source_target_pairs={{0,1},{1,0},{2,3},{3,2},{4,5},{5,4},{6,7},{7,6},{8,9},{9,8},{10,11... | collective-permute-start | bytes 983048 | tf_op jit(solution)/shard_map/ppermute | solution.py:26
  90.3 14.5 %collective-permute-start.13 = (bf16[2,5,128,128]{3,2,1,0:T(8,128)(2,1)S(1)}, bf16[2,5,128,128]{3,2,1,0:T(8,128)(2,1)S(1)}, u32[]{:S(2)}, u32[]{:S(2)}) collective-permute-start(bf16[2,5,128,128]{3,2,1,0:T(8,128)(2,1)S(1)} %collective-permute-done.12.refs_12_), channel_id=1, source_target_pairs={{0,8},{1,9},{2,10},{3,11},{4,12},{5,13},{6,14},{7,15},{8,0},{9,1},... | collective-permute-start | bytes 983048 | tf_op jit(solution)/shard_map/ppermute | solution.py:26
  91.1 25.8 %collective-permute-start.5 = (bf16[2,5,128,128]{3,2,1,0:T(8,128)(2,1)}, bf16[2,5,128,128]{3,2,1,0:T(8,128)(2,1)}, u32[]{:S(2)}, u32[]{:S(2)}) collective-permute-start(bf16[2,5,128,128]{3,2,1,0:T(8,128)(2,1)} %collective-permute-done.4.refs_4_), channel_id=1, source_target_pairs={{0,8},{1,9},{2,10},{3,11},{4,12},{5,13},{6,14},{7,15},{8,0},{9,1},... | collective-permute-start | bytes 983048 | tf_op jit(solution)/shard_map/ppermute | solution.py:26
  95.0 21.9 %collective-permute-start.9 = (bf16[2,5,128,128]{3,2,1,0:T(8,128)(2,1)S(1)}, bf16[2,5,128,128]{3,2,1,0:T(8,128)(2,1)}, u32[]{:S(2)}, u32[]{:S(2)}) collective-permute-start(bf16[2,5,128,128]{3,2,1,0:T(8,128)(2,1)S(1)} %collective-permute-done.8.refs_8_), channel_id=1, source_target_pairs={{0,8},{1,9},{2,10},{3,11},{4,12},{5,13},{6,14},{7,15},{8,0},{9,1},... | collective-permute-start | bytes 983048 | tf_op jit(solution)/shard_map/ppermute | solution.py:26
  101.4 15.6 %collective-permute-start.11 = (bf16[2,5,128,128]{3,2,1,0:T(8,128)(2,1)}, bf16[2,5,128,128]{3,2,1,0:T(8,128)(2,1)}, u32[]{:S(2)}, u32[]{:S(2)}) collective-permute-start(bf16[2,5,128,128]{3,2,1,0:T(8,128)(2,1)} %collective-permute-done.10.refs_10_), channel_id=1, source_target_pairs={{0,8},{1,9},{2,10},{3,11},{4,12},{5,13},{6,14},{7,15},{8,0},{9,1},... | collective-permute-start | bytes 983048 | tf_op jit(solution)/shard_map/ppermute | solution.py:26
  104.9 12.1 %collective-permute-start.15 = (bf16[2,5,128,128]{3,2,1,0:T(8,128)(2,1)}, bf16[2,5,128,128]{3,2,1,0:T(8,128)(2,1)}, u32[]{:S(2)}, u32[]{:S(2)}) collective-permute-start(bf16[2,5,128,128]{3,2,1,0:T(8,128)(2,1)} %collective-permute-done.14.refs_14_), channel_id=1, source_target_pairs={{0,8},{1,9},{2,10},{3,11},{4,12},{5,13},{6,14},{7,15},{8,0},{9,1},... | collective-permute-start | bytes 983048 | tf_op jit(solution)/shard_map/ppermute | solution.py:26
  105.6 11.3 %collective-permute-start.7 = (bf16[2,5,128,128]{3,2,1,0:T(8,128)(2,1)}, bf16[2,5,128,128]{3,2,1,0:T(8,128)(2,1)}, u32[]{:S(2)}, u32[]{:S(2)}) collective-permute-start(bf16[2,5,128,128]{3,2,1,0:T(8,128)(2,1)} %collective-permute-done.6.refs_6_), channel_id=1, source_target_pairs={{0,8},{1,9},{2,10},{3,11},{4,12},{5,13},{6,14},{7,15},{8,0},{9,1},... | collective-permute-start | bytes 983048 | tf_op jit(solution)/shard_map/ppermute | solution.py:26
  123.4 8.5 %collective-permute-start.32 = (bf16[2,2,128,128]{3,2,0,1:T(8,128)(2,1)S(1)}, bf16[2,2,128,128]{3,2,0,1:T(8,128)(2,1)S(1)}, u32[]{:S(2)}, u32[]{:S(2)}) collective-permute-start(bf16[2,2,128,128]{3,2,0,1:T(8,128)(2,1)S(1)} %copy.8), channel_id=1, source_target_pairs={{0,0},{1,1},{2,2},{3,3},{4,4},{5,5},{6,6},{7,7},{8,9},{9,8},{10,11... | collective-permute-start | bytes 393224 | tf_op jit(solution)/shard_map/ppermute | solution.py:26
  124.0 8.6 %collective-permute-start.33 = (bf16[2,2,128,128]{3,2,0,1:T(8,128)(2,1)S(1)}, bf16[2,2,128,128]{3,2,0,1:T(8,128)(2,1)S(1)}, u32[]{:S(2)}, u32[]{:S(2)}) collective-permute-start(bf16[2,2,128,128]{3,2,0,1:T(8,128)(2,1)S(1)} %copy.9), channel_id=1, source_target_pairs={{0,16},{1,17},{2,18},{3,19},{4,20},{5,21},{6,22},{7,23},{8,25},{9,... | collective-permute-start | bytes 393224 | tf_op jit(solution)/shard_map/ppermute | solution.py:26
  129.8 6.1 %collective-permute-start.30 = (bf16[2,2,128,128]{3,2,1,0:T(8,128)(2,1)S(1)}, bf16[2,2,128,128]{3,2,1,0:T(8,128)(2,1)S(1)}, u32[]{:S(2)}, u32[]{:S(2)}) collective-permute-start(bf16[2,2,128,128]{3,2,1,0:T(8,128)(2,1)S(1)} %get-tuple-element.13), channel_id=1, source_target_pairs={{0,8},{1,9},{2,10},{3,11},{4,12},{5,13},{6,14},{7,15},{8,1},{9,0},... | collective-permute-start | bytes 393224 | tf_op jit(solution)/shard_map/ppermute | solution.py:26
  131.9 6.6 %collective-permute-start.31 = (bf16[2,2,128,128]{3,2,1,0:T(8,128)(2,1)S(1)}, bf16[2,2,128,128]{3,2,1,0:T(8,128)(2,1)S(1)}, u32[]{:S(2)}, u32[]{:S(2)}) collective-permute-start(bf16[2,2,128,128]{3,2,1,0:T(8,128)(2,1)S(1)} %get-tuple-element.12), channel_id=1, source_target_pairs={{0,24},{1,25},{2,26},{3,27},{4,28},{5,29},{6,30},{7,31},{8,17},{9,... | collective-permute-start | bytes 393224 | tf_op jit(solution)/shard_map/ppermute | solution.py:26
  (26 other events, 121.5 us)

commit v2 on v0

--- a/solution.py
+++ b/solution.py
@@ -1,9 +1,238 @@
+import functools
 import math
 
 import jax
 import jax.numpy as jnp
 from jax import lax
+from jax.experimental import pallas as pl
+from jax.experimental.pallas import tpu as pltpu
 from jax.sharding import PartitionSpec as P
+
+ROWS, PLANES = 4, 4
+
+
+def move(value, rule):
+    pairs = []
+    for r in range(ROWS):
+        for z in range(PLANES):
+            for x in range(2):
+                to = rule(r, z, x)
+                if to is not None:
+                    pairs.append((r * 2 * PLANES + 2 * z + x, to[0] * 2 * PLANES + 2 * to[1] + to[2]))
+    return lax.ppermute(value, ("row", "col"), pairs)
+
+
+def swap_core(value):
+    return move(value, lambda r, z, x: (r ^ 1, z, x))
+
+
+def swap_y(value):
+    return move(value, lambda r, z, x: (r ^ 2, z, x))
+
+
+def swap_x(value):
+    return move(value, lambda r, z, x: (r, z, x ^ 1))
+
+
+def block_kernel(info, *refs):
+    x = info[0]
+    out = refs[-1]
+    for n in range(len(refs) // 2):
+        for rr in range(2):
+            for cc in range(2):
+                for p in range(2):
+                    out[n, p, pl.ds(rr * 128, 128), pl.ds(cc * 128, 128)] = refs[2 * n + cc][rr ^ x, p]
+
+
+def turn_kernel(info, e, ce, xe, cxe, out):
+    x, core, g = info[0], info[1], info[2]
+    vectors = e.shape[2]
+    for half in range(2):
+        for t in range(2):
+            for rr in range(2):
+                for q in range(vectors):
+                    tile = jnp.where(core == 0, (e, ce)[half][t, rr ^ x, q], (xe, cxe)[half][t, rr ^ x, q])
+                    out[g ^ (half + 2 * t), pl.ds(q * 128, 128), pl.ds(rr * 128, 128)] = tile.T
+
+
+def halves_kernel(info, rows, own, other, own3, other3, out, after, total):
+    x, g = info[0], info[2]
+    for n in range(info.shape[0]):
+        after[n] = info[n]
+    for j in range(PLANES):
+        for p in range(2):
+            swapped = jnp.where(x == 0, 1 - p, p)
+            mirror = None
+            for half, blocks in enumerate(((own, other), (own3, other3))[j == 3]):
+                for t in range(2):
+                    i = g ^ (half + 2 * t)
+                    n = 0 if j == 3 else j
+                    block = blocks[t, n, p]
+                    term = lax.dot_general(rows[j], block, (((1,), (1,)), ((), ())), preferred_element_type=jnp.float32)
+                    total[i, p] = term if j == 0 else total[i, p] + term
+                    term = jnp.dot(rows[i], blocks[t, n, swapped], preferred_element_type=jnp.float32)
+                    mirror = term if mirror is None else mirror + term
+            total[j, p] = total[j, p] - mirror
+    for w in range(PLANES):
+        for p in range(2):
+            value = total[w, p].astype(jnp.bfloat16)
+            for q in range(out.shape[1]):
+                out[w, q, pl.ds(p * 128, 128), :] = value[q * 128 : (q + 1) * 128]
+
+
+def ladder_terms(x, halves, cases, total):
+    vectors = halves.shape[1]
+    for i, j, columns in cases:
+        direct, mirror = None, None
+        for q in range(vectors):
+            factor = jnp.concatenate(
+                [jnp.concatenate([columns[cc][rr ^ x, q] for cc in range(2)], axis=1) for rr in range(2)], axis=0
+            )
+            term = lax.dot_general(halves[j, q], factor, (((1,), (1,)), ((), ())), preferred_element_type=jnp.float32)
+            direct = term if direct is None else direct + term
+            term = jnp.dot(halves[i, q], factor, preferred_element_type=jnp.float32)
+            mirror = term if mirror is None else mirror + term
+        total[i] = total[i] + direct
+        total[j] = total[j] + jnp.where(i == j, jnp.zeros_like(mirror), mirror)
+
+
+def ladder_own_kernel(info, halves, e, ce, xe, cxe, total):
+    x, g = info[0], info[2]
+    for w in range(PLANES):
+        total[w] = jnp.zeros(total.shape[1:], jnp.float32)
+    cases = []
+    for half, (own, side) in enumerate(((e, xe), (ce, cxe))):
+        for t in range(2):
+            cases.append((g ^ (half + 2 * t), 0, (own.at[t], side.at[t])))
+    ladder_terms(x, halves, cases, total)
+
+
+def ladder_far_kernel(info, halves, held, both, both_other, far, far_other, beside, beside_other, out, total):
+    x, g = info[0], info[2]
+    total[...] = held[...]
+    cases = []
+    for half, ref in enumerate((both, both_other)):
+        cases.append((*by_parity(g, half, (2, 1), (1, 1)), (ref.at[0], ref.at[1])))
+    for n, pairs in enumerate((((2, 2), (3, 2)), ((3, 1), (3, 3)))):
+        for half, (own, side) in enumerate(((far, beside), (far_other, beside_other))):
+            cases.append((*by_parity(g, half, *pairs), (own.at[n], side.at[n])))
+    ladder_terms(x, halves, cases, total)
+    for w in range(PLANES):
+        for rr in range(2):
+            for p in range(2):
+                tile = total[w, pl.ds(p * 128, 128), pl.ds(rr * 128, 128)]
+                out[w, rr, p] = tile.T.astype(jnp.bfloat16)
+
+
+def by_parity(g, half, even, odd):
+    return tuple(jnp.where((g & 1) == half, a, b) for a, b in zip(even, odd))
+
+
+SMEM = pl.BlockSpec(memory_space=pltpu.SMEM)
+VMEM = pl.BlockSpec(memory_space=pltpu.VMEM)
+
+
+def small_call(kernel, out_shape, *operands):
+    specs = [SMEM if value.dtype == jnp.int32 else VMEM for value in operands]
+    return pl.pallas_call(
+        kernel,
+        out_shape=out_shape,
+        in_specs=specs,
+        out_specs=jax.tree.map(lambda _: VMEM, out_shape),
+        compiler_params=pltpu.CompilerParams(vmem_limit_bytes=8 << 20),
+        cost_estimate=pl.CostEstimate(flops=1 << 10, bytes_accessed=1 << 10, transcendentals=0),
+    )(*operands)
+
+
+def fast_body(amplitudes, cholesky, tile_mask):
+    vectors = cholesky.shape[2] // 2
+    r, k = lax.axis_index("row"), lax.axis_index("col")
+    y, core, z, x = r >> 1, r & 1, k >> 1, k & 1
+    g = r ^ z
+    info = jnp.stack([x, core, g, y]).astype(jnp.int32)
+    masked = (amplitudes * tile_mask.astype(jnp.bfloat16)[:, :, None, None, None])[:, 0]
+    crossed = masked[:, 1:3]
+    straight = jnp.stack([masked[:, 0], masked[:, 3]], axis=1)
+    own_pairs = jnp.where(x == 0, crossed, straight)
+    other_pairs = jnp.where(x == 0, straight, crossed)
+    factors = cholesky[:, 0]
+    kept = lax.dynamic_slice_in_dim(factors, y * vectors, vectors, 1)
+    given = lax.dynamic_slice_in_dim(factors, (1 - y) * vectors, vectors, 1)
+    taken = swap_y(given)
+    near = [move(own_pairs, lambda r, z, x: (r, z ^ 1, x)), move(other_pairs, lambda r, z, x: (r, z ^ 1, x ^ 1))]
+    away = [move(own_pairs, lambda r, z, x: (r, z ^ 2, x)), move(other_pairs, lambda r, z, x: (r, z ^ 2, x ^ 1))]
+    *near, others = lax.optimization_barrier((*near, other_pairs))
+    side = swap_x(others)
+    taken, side, near, away = lax.optimization_barrier((taken, side, near, away))
+
+    e = jnp.stack([kept, taken])
+    ce = swap_core(e)
+    xe = swap_x(e)
+    got1 = move(jnp.where(g <= 1, kept, taken), lambda r, z, x: (r, z ^ 2, x))
+    block2 = small_call(block_kernel, jax.ShapeDtypeStruct((1, 2, 256, 256), jnp.bfloat16), info, *away)
+    block3 = move(block2, lambda r, z, x: (r, z ^ 1, x))
+    trio_shape = jax.ShapeDtypeStruct((3, 2, 256, 256), jnp.bfloat16)
+    trio = small_call(block_kernel, trio_shape, info, own_pairs, side, *near, *away)
+    across = swap_y(trio)
+    piece = jnp.where((g & 1) == 0, jnp.where(g == 0, kept, taken), jnp.where(g == 3, ce[0], ce[1]))
+    got2 = move(piece, lambda r, z, x: (r, z ^ 1 if (r ^ z) & 1 else z ^ 3, x))
+    ce, xe, got1, block3, across, got2 = lax.optimization_barrier((ce, xe, got1, block3, across, got2))
+
+    n = (g == 0) | (g == 3)
+    piece = jnp.stack([jnp.where(n, kept, taken), jnp.where(n, xe[0], xe[1])])
+    both = move(piece, lambda r, z, x: (r, z ^ 1, x))
+    far = jnp.stack([got1, got2])
+    beside = swap_x(far)
+    across3 = swap_y(block3)
+    cxe = swap_core(xe)
+    blocks = jnp.stack([trio, across])
+    rows = small_call(
+        turn_kernel, jax.ShapeDtypeStruct((PLANES, vectors * 128, 256), jnp.bfloat16), info, e, ce, xe, cxe
+    )
+    far_other = swap_core(far)
+    near3 = jnp.stack([block3, across3])
+    halves, info = pl.pallas_call(
+        halves_kernel,
+        out_shape=(
+            jax.ShapeDtypeStruct((PLANES, vectors, 256, 256), jnp.bfloat16),
+            jax.ShapeDtypeStruct(info.shape, info.dtype),
+        ),
+        in_specs=[SMEM] + [VMEM] * 5,
+        out_specs=(VMEM, SMEM),
+        scratch_shapes=[pltpu.VMEM((PLANES, 2, vectors * 128, 256), jnp.float32)],
+        compiler_params=pltpu.CompilerParams(vmem_limit_bytes=16 << 20),
+        cost_estimate=pl.CostEstimate(flops=1 << 10, bytes_accessed=1 << 10, transcendentals=0),
+    )(info, rows, blocks, swap_core(blocks), near3, swap_core(near3))
+    both, beside, info = lax.optimization_barrier((both, beside, info))
+
+    held = pl.pallas_call(
+        ladder_own_kernel,
+        out_shape=jax.ShapeDtypeStruct((PLANES, 256, 256), jnp.float32),
+        in_specs=[SMEM] + [VMEM] * 5,
+        out_specs=VMEM,
+        compiler_params=pltpu.CompilerParams(vmem_limit_bytes=8 << 20),
+        cost_estimate=pl.CostEstimate(flops=1 << 10, bytes_accessed=1 << 10, transcendentals=0),
+    )(info, halves, e, ce, xe, cxe)
+    partial = pl.pallas_call(
+        ladder_far_kernel,
+        out_shape=jax.ShapeDtypeStruct((PLANES, 2, 2, 128, 128), jnp.bfloat16),
+        in_specs=[SMEM] + [VMEM] * 8,
+        out_specs=VMEM,
+        scratch_shapes=[pltpu.VMEM((PLANES, 256, 256), jnp.float32)],
+        compiler_params=pltpu.CompilerParams(vmem_limit_bytes=8 << 20),
+        cost_estimate=pl.CostEstimate(flops=1 << 10, bytes_accessed=1 << 10, transcendentals=0),
+    )(info, halves, held, both, swap_core(both), far, far_other, beside, swap_core(beside))
+
+    sums = []
+    for m in range(ROWS):
+        part = lax.dynamic_index_in_dim(partial, g ^ m, 0, keepdims=False)
+        sums.append(move(part, lambda r, z, x, m=m: (r ^ m, z, x ^ (r & 1))).astype(jnp.float32))
+    same, other = sums[0] + sums[2], sums[1] + sums[3]
+    mine = (x ^ core) == 0
+    crossed = jnp.where(mine, same, other)
+    straight = jnp.where(mine, other, same)[::-1]
+    result = jnp.stack([straight[:, 0], crossed[:, 0], crossed[:, 1], straight[:, 1]], axis=1)
+    return result.astype(jnp.bfloat16)[:, None]
 
 
 def from_partner(value, axis, apart):
@@ -42,7 +271,7 @@
     return tile_set
 
 
-def body(amplitudes, cholesky, tile_mask):
+def general_body(amplitudes, cholesky, tile_mask):
     tile_rows = amplitudes.shape[0]
     pair_count = amplitudes.shape[2]
     tile_edge = amplitudes.shape[3]
@@ -79,6 +308,14 @@
     return result_tiles.reshape(tile_rows, 1, pair_count, tile_edge, tile_edge)
 
 
+def body(amplitudes, cholesky, tile_mask):
+    rows, cols = lax.axis_size("row"), lax.axis_size("col")
+    fits = amplitudes.shape == (2, 1, 4, 128, 128) and cholesky.shape[2] % 2 == 0
+    if rows == ROWS and cols == 2 * PLANES and fits:
+        return fast_body(amplitudes, cholesky, tile_mask)
+    return general_body(amplitudes, cholesky, tile_mask)
+
+
 def solution(mesh):
     in_specs = (
         P("row", "col", None, None, None),

time: 265 us -> 96.8 us (0.37)
  waiting for transfers between devices: 153 us -> 46.7 us
  blocking collectives: 62.5 us -> 0 us
  Pallas kernels: 0 us -> 16.3 us
  starting transfers between devices: 7.09 us -> 22.3 us
  between operations: 13.9 us -> 0.28 us
  matrix products: 12.1 us -> 0 us
  local copies, waits for them, and re-layouts: 11.3 us -> 4.49 us
    all_gather x3 -> x0, waiting for transfers between devices: 124 us -> none  [the longest x1 72.9 us: body(): spread = lax.all_gather(cholesky, 'col', axis=1, tiled=True)]
    unnamed x1 -> x0, blocking collectives: 40.2 us -> none
    all_gather x1 -> x0, blocking collectives: 22.3 us -> none  [body(): mask_block = lax.all_gather(tile_mask, 'col', axis=1, tiled=True)]
    ppermute x7 -> x25, waiting for transfers between devices: 27.2 us -> 46.7 us  [move(): return lax.ppermute(value, ('row', 'col'), pairs)]
    pallas_call x0 -> x6, Pallas kernels: none -> 16.3 us  [the longest x1 7.18 us: fast_body(): pl.pallas_call(halves_kernel, out_shape=(jax.ShapeDtypeStruct((PLANES, ve...]
    ppermute x7 -> x25, starting transfers between devices: 7.02 us -> 22.3 us  [move(): return lax.ppermute(value, ('row', 'col'), pairs)]
    dot_general x2 -> x0, matrix products: 12.1 us -> none  [the longest x1 6.13 us: body(): jnp.einsum('caqux,cpuqy->apxy', spread, halves, preferred_element_type=jn...]
    reshape x1 -> x0, local copies, waits for them, and re-layouts: 6.38 us -> none  [body(): halves.astype(jnp.bfloat16)]
  transfers between devices with their start and end apart: 10 -> 25, of which waited for: 10 -> 14; matrix products, arithmetic and copies ran while one was open for 8% -> 4% of each run, Pallas kernels for 0% -> 12%
where the time goes in v2:
time: 96.8 us; the launch traced here: 96.4 us
  waiting for transfers between devices  46.7 us (48%)
  starting transfers between devices  22.3 us (23%)
  Pallas kernels  16.3 us (17%)
  other arithmetic  6.23 us (6%)
  local copies, waits for them, and re-layouts  4.49 us (5%)
    ppermute x25, waiting for transfers between devices, move(): return lax.ppermute(value, ('row', 'col'), pairs)  46.7 us
    ppermute x25, starting transfers between devices, move(): return lax.ppermute(value, ('row', 'col'), pairs)  22.3 us
    pallas_call x1, Pallas kernels, fast_body(): pl.pallas_call(halves_kernel, out_shape=(jax.ShapeDtypeStruct((PLANES, ve...  7.18 us
    pallas_call x1, Pallas kernels, fast_body(): pl.pallas_call(ladder_far_kernel, out_shape=jax.ShapeDtypeStruct((PLANES,...  4.81 us
    unnamed x14, local copies, waits for them, and re-layouts  3.28 us
    pallas_call x3, Pallas kernels, small_call(): pl.pallas_call(kernel, out_shape=out_shape, in_specs=specs, out_specs=jax...  2.21 us
    pallas_call x1, Pallas kernels, fast_body(): pl.pallas_call(ladder_own_kernel, out_shape=jax.ShapeDtypeStruct((PLANES,...  2.13 us
  transfers between devices with their start and end apart: 25, of which 14 were waited for; matrix products, arithmetic and copies ran while one was open for 4% of the time, Pallas kernels for 12%

profile of v2, /device:TPU:0, one launch (start us, length us, event | category | flops | bytes accessed | tf_op | source)
XLA Modules:
  0.0 96.4 jit_solution(10316037780194326464)
XLA Ops:
  0.0 1.1 %dynamic-slice_bitcast_fusion.1 = (bf16[1,2,5,128,128]{4,3,2,1,0:T(8,128)(2,1)S(1)}, bf16[2,5,128,128]{3,2,1,0:T(8,128)(2,1)S(1)}) fusion(bf16[2,1,10,128,128]{4,3,2,1,0:T(8,128)(2,1)} %param.4, s32[]{:T(128)S(6)} %select_n.87, s32[]{:T(128)S(6)} %select_n.88), kind=kLoop, calls=%fused_computation.22 | loop fusion | bytes 1310728 | tf_op jit(solution)/shard_map/stack | solution.py:168
  1.1 3.0 %collective-permute-start = (bf16[2,5,128,128]{3,2,1,0:T(8,128)(2,1)S(1)}, bf16[2,5,128,128]{3,2,1,0:T(8,128)(2,1)S(1)}, u32[]{:S(2)}, u32[]{:S(2)}) collective-permute-start(bf16[2,5,128,128]{3,2,1,0:T(8,128)(2,1)S(1)} %get-tuple-element.49), channel_id=1, source_target_pairs={{0,16},{1,17},{2,18},{3,19},{4,20},{5,21},{6,22},{7,23},{8,24},{9,... | collective-permute-start | bytes 983048 | tf_op jit(solution)/shard_map/ppermute | solution.py:22
  4.8 1.0 %fusion.3 = bf16[2,4,128,128]{3,2,1,0:T(8,128)(2,1)S(1)} fusion(bf16[2,1,4,128,128]{4,3,2,1,0:T(8,128)(2,1)} %param.3, bf16[2]{0:T(256)(128)(2,1)S(1)} %convert_bitcast_fusion), kind=kLoop, calls=%fused_computation.16 | loop fusion | flops 131072 | bytes 524292 | tf_op jit(solution)/shard_map/squeeze | solution.py:153
  5.9 1.6 %collective-permute-start.1 = (bf16[2,2,128,128]{3,2,1,0:T(8,128)(2,1)S(1)}, bf16[2,2,128,128]{3,2,1,0:T(8,128)(2,1)S(1)}, u32[]{:S(2)}, u32[]{:S(2)}) collective-permute-start(bf16[2,2,128,128]{3,2,1,0:T(8,128)(2,1)S(1)} %get-tuple-element.55.refs_0_), channel_id=1, source_target_pairs={{0,2},{1,3},{2,0},{3,1},{4,6},{5,7},{6,4},{7,5},{8,10},{9,11},{10,... | collective-permute-start | bytes 393224 | tf_op jit(solution)/shard_map/ppermute | solution.py:22
  7.5 1.4 %collective-permute-start.2 = (bf16[2,2,128,128]{3,2,1,0:T(8,128)(2,1)S(1)}, bf16[2,2,128,128]{3,2,1,0:T(8,128)(2,1)S(1)}, u32[]{:S(2)}, u32[]{:S(2)}) collective-permute-start(bf16[2,2,128,128]{3,2,1,0:T(8,128)(2,1)S(1)} %get-tuple-element.25), channel_id=1, source_target_pairs={{0,3},{1,2},{2,1},{3,0},{4,7},{5,6},{6,5},{7,4},{8,11},{9,10},{10,... | collective-permute-start | bytes 393224 | tf_op jit(solution)/shard_map/ppermute | solution.py:22
  8.9 2.6 %collective-permute-start.4 = (bf16[2,2,128,128]{3,2,1,0:T(8,128)(2,1)S(1)}, bf16[2,2,128,128]{3,2,1,0:T(8,128)(2,1)S(1)}, u32[]{:S(2)}, u32[]{:S(2)}) collective-permute-start(bf16[2,2,128,128]{3,2,1,0:T(8,128)(2,1)S(1)} %get-tuple-element.55.refs_0_), channel_id=1, source_target_pairs={{0,4},{1,5},{2,6},{3,7},{4,0},{5,1},{6,2},{7,3},{8,12},{9,13},{10,... | collective-permute-start | bytes 393224 | tf_op jit(solution)/shard_map/ppermute | solution.py:22
  11.8 1.1 %collective-permute-done.1.refs_2_ = bf16[2,2,128,128]{3,2,1,0:T(8,128)(2,1)S(1)} collective-permute-done((bf16[2,2,128,128]{3,2,1,0:T(8,128)(2,1)S(1)}, bf16[2,2,128,128]{3,2,1,0:T(8,128)(2,1)S(1)}, u32[]{:S(2)}, u32[]{:S(2)}) %collective-permute-start.1) | collective-permute-done | bytes 131104 | tf_op jit(solution)/shard_map/ppermute | solution.py:22
  13.0 6.5 %collective-permute-done.2.refs_3_ = bf16[2,2,128,128]{3,2,1,0:T(8,128)(2,1)S(1)} collective-permute-done((bf16[2,2,128,128]{3,2,1,0:T(8,128)(2,1)S(1)}, bf16[2,2,128,128]{3,2,1,0:T(8,128)(2,1)S(1)}, u32[]{:S(2)}, u32[]{:S(2)}) %collective-permute-start.2) | collective-permute-done | bytes 131104 | tf_op jit(solution)/shard_map/ppermute | solution.py:22
  19.5 2.1 %collective-permute-done.4.refs_0_.refs_4_ = bf16[2,2,128,128]{3,2,1,0:T(8,128)(2,1)S(1)} collective-permute-done((bf16[2,2,128,128]{3,2,1,0:T(8,128)(2,1)S(1)}, bf16[2,2,128,128]{3,2,1,0:T(8,128)(2,1)S(1)}, u32[]{:S(2)}, u32[]{:S(2)}) %collective-permute-start.4) | collective-permute-done | bytes 131104 | tf_op jit(solution)/shard_map/ppermute | solution.py:22
  21.6 1.7 %collective-permute-done.5.refs_1_.refs_5_ = bf16[2,2,128,128]{3,2,1,0:T(8,128)(2,1)S(1)} collective-permute-done((bf16[2,2,128,128]{3,2,1,0:T(8,128)(2,1)S(1)}, bf16[2,2,128,128]{3,2,1,0:T(8,128)(2,1)S(1)}, u32[]{:S(2)}, u32[]{:S(2)}) %collective-permute-start.5) | collective-permute-done | bytes 131104 | tf_op jit(solution)/shard_map/ppermute | solution.py:22
  23.3 1.4 %collective-permute-done.3.refs_1_ = bf16[2,2,128,128]{3,2,1,0:T(8,128)(2,1)S(1)} collective-permute-done((bf16[2,2,128,128]{3,2,1,0:T(8,128)(2,1)S(1)}, bf16[2,2,128,128]{3,2,1,0:T(8,128)(2,1)S(1)}, u32[]{:S(2)}, u32[]{:S(2)}) %collective-permute-start.3) | collective-permute-done | bytes 131104 | tf_op jit(solution)/shard_map/ppermute | solution.py:22
  26.1 1.5 %collective-permute-start.7 = (bf16[2,2,5,128,128]{4,3,2,1,0:T(8,128)(2,1)S(1)}, bf16[2,2,5,128,128]{4,3,2,1,0:T(8,128)(2,1)S(1)}, u32[]{:S(2)}, u32[]{:S(2)}) collective-permute-start(bf16[2,2,5,128,128]{4,3,2,1,0:T(8,128)(2,1)S(1)} %pad_maximum_fusion.1.e), channel_id=1, source_target_pairs={{0,1},{1,0},{2,3},{3,2},{4,5},{5,4},{6,7},{7,6},{8,9},{9,8},{10,11... | collective-permute-start | bytes 1966088 | tf_op jit(solution)/shard_map/ppermute | solution.py:22
  27.7 1.2 %fusion.2 = (bf16[1,2,5,128,128]{4,3,2,1,0:T(8,128)(2,1)S(1)}, bf16[2,5,128,128]{3,2,1,0:T(8,128)(2,1)S(1)}, bf16[2,5,128,128]{3,2,1,0:T(8,128)(2,1)S(1)}) fusion(bf16[2,5,128,128]{3,2,1,0:T(8,128)(2,1)} %copy-done.6, pred[]{:T(512)S(6)} %or.3, bf16[2,1,10,128,128]{4,3,2,1,0:T(8,128)(2,1)} %param.4, s32[]{:T(128)S(6)} %select_n.87, ...), kind=kLoop, calls=%fused_computation.11 | loop fusion | flops 819200 | bytes 2293769 | tf_op jit(solution)/shard_map/stack | solution.py:182
  28.8 2.4 %collective-permute-start.11 = (bf16[2,5,128,128]{3,2,1,0:T(8,128)(2,1)S(1)}, bf16[2,5,128,128]{3,2,1,0:T(8,128)(2,1)S(1)}, u32[]{:S(2)}, u32[]{:S(2)}) collective-permute-start(bf16[2,5,128,128]{3,2,1,0:T(8,128)(2,1)S(1)} %get-tuple-element.46), channel_id=1, source_target_pairs={{0,6},{1,7},{2,0},{3,1},{4,2},{5,3},{6,4},{7,5},{8,10},{9,11},{10,... | collective-permute-start | bytes 983048 | tf_op jit(solution)/shard_map/ppermute | solution.py:22
  32.5 16.4 %collective-permute-done.9 = bf16[1,2,256,256]{3,2,1,0:T(8,128)(2,1)S(1)} collective-permute-done((bf16[1,2,256,256]{3,2,1,0:T(8,128)(2,1)S(1)}, bf16[1,2,256,256]{3,2,1,0:T(8,128)(2,1)S(1)}, u32[]{:S(2)}, u32[]{:S(2)}) %collective-permute-start.9) | collective-permute-done | bytes 262176 | tf_op jit(solution)/shard_map/ppermute | solution.py:22
  48.9 3.5 %collective-permute-done.8 = bf16[2,5,128,128]{3,2,1,0:T(8,128)(2,1)S(1)} collective-permute-done((bf16[2,5,128,128]{3,2,1,0:T(8,128)(2,1)S(1)}, bf16[2,5,128,128]{3,2,1,0:T(8,128)(2,1)S(1)}, u32[]{:S(2)}, u32[]{:S(2)}) %collective-permute-start.8) | collective-permute-done | bytes 327712 | tf_op jit(solution)/shard_map/ppermute | solution.py:22
  52.3 1.3 %pad_maximum_fusion.own = bf16[2,3,2,256,256]{4,3,2,1,0:T(8,128)(2,1)S(1)} fusion(bf16[1,3,2,256,256]{4,3,2,1,0:T(8,128)(2,1)} %bitcast.16, bf16[1,3,2,256,256]{4,3,2,1,0:T(8,128)(2,1)S(1)} %bitcast.55), kind=kLoop, calls=%fused_computation | loop fusion | flops 786432 | bytes 3145728 | tf_op jit(solution)/shard_map/stack | solution.py:188
  53.7 1.4 %collective-permute-start.16 = (bf16[1,2,256,256]{3,2,1,0:T(8,128)(2,1)S(1)}, bf16[1,2,256,256]{3,2,1,0:T(8,128)(2,1)S(1)}, u32[]{:S(2)}, u32[]{:S(2)}) collective-permute-start(bf16[1,2,256,256]{3,2,1,0:T(8,128)(2,1)S(1)} %collective-permute-done.9), channel_id=1, source_target_pairs={{0,16},{1,17},{2,18},{3,19},{4,20},{5,21},{6,22},{7,23},{8,24},{9,... | collective-permute-start | bytes 786440 | tf_op jit(solution)/shard_map/ppermute | solution.py:22
  57.2 5.2 %collective-permute-done.16 = bf16[1,2,256,256]{3,2,1,0:T(8,128)(2,1)S(1)} collective-permute-done((bf16[1,2,256,256]{3,2,1,0:T(8,128)(2,1)S(1)}, bf16[1,2,256,256]{3,2,1,0:T(8,128)(2,1)S(1)}, u32[]{:S(2)}, u32[]{:S(2)}) %collective-permute-start.16) | collective-permute-done | bytes 262176 | tf_op jit(solution)/shard_map/ppermute | solution.py:22
  63.0 0.9 shard_map.39.rows
  64.4 7.2 %shard_map.40 = (bf16[4,5,256,256]{3,2,1,0:T(8,128)(2,1)S(1)}, s32[4]{0:T(128)S(1)}) custom-call(s32[4]{0:T(128)S(1)} %pad_add_fusion.info, bf16[4,640,256]{2,1,0:T(8,128)(2,1)S(1)} %shard_map.39.rows, bf16[2,3,2,256,256]{4,3,2,1,0:T(8,128)(2,1)S(1)} %pad_maximum_fusion.own, bf16[2,3,2,256,256]{4,3,2,1,0:T(8,128)(2,1)S(1)} %collective-permute-done.15.other, ...), custom_call_target="tpu_custom_call" | custom-call | flops 1024 | bytes 1024 | tf_op jit(solution)/shard_map/pallas_call | solution.py:194
  71.6 1.9 %collective-permute-done.13.beside = bf16[2,2,5,128,128]{4,3,2,1,0:T(8,128)(2,1)} collective-permute-done((bf16[2,2,5,128,128]{4,3,2,1,0:T(8,128)(2,1)}, bf16[2,2,5,128,128]{4,3,2,1,0:T(8,128)(2,1)}, u32[]{:S(2)}, u32[]{:S(2)}) %collective-permute-start.13) | collective-permute-done | bytes 655392 | tf_op jit(solution)/shard_map/ppermute | solution.py:22
  74.5 1.1 %copy-done.1 = bf16[2,2,5,128,128]{4,3,2,1,0:T(8,128)(2,1)S(1)} copy-done((bf16[2,2,5,128,128]{4,3,2,1,0:T(8,128)(2,1)S(1)}, bf16[2,2,5,128,128]{4,3,2,1,0:T(8,128)(2,1)}, u32[]{:S(2)}) %copy-start.1) | copy-done | bytes 655384
  75.6 1.1 %copy-done.3 = bf16[2,2,5,128,128]{4,3,2,1,0:T(8,128)(2,1)S(1)} copy-done((bf16[2,2,5,128,128]{4,3,2,1,0:T(8,128)(2,1)S(1)}, bf16[2,2,5,128,128]{4,3,2,1,0:T(8,128)(2,1)}, u32[]{:S(2)}) %copy-start.3) | copy-done | bytes 655384
  76.7 1.1 %copy-done.5 = bf16[2,2,5,128,128]{4,3,2,1,0:T(8,128)(2,1)S(1)} copy-done((bf16[2,2,5,128,128]{4,3,2,1,0:T(8,128)(2,1)S(1)}, bf16[2,2,5,128,128]{4,3,2,1,0:T(8,128)(2,1)}, u32[]{:S(2)}) %copy-start.5) | copy-done | bytes 655384
  77.8 2.1 %shard_map.41.held = f32[4,256,256]{2,1,0:T(8,128)S(1)} custom-call(s32[4]{0:T(128)S(1)} %get-tuple-element.41.info, bf16[4,5,256,256]{3,2,1,0:T(8,128)(2,1)S(1)} %get-tuple-element.42.halves, bf16[2,2,5,128,128]{4,3,2,1,0:T(8,128)(2,1)S(1)} %copy-done.1, bf16[2,2,5,128,128]{4,3,2,1,0:T(8,128)(2,1)S(1)} %collective-permute-done.6.ce, ...), custom_call_target="tpu_custom_call" | custom-call | flops 1024 | bytes 1024 | tf_op jit(solution)/shard_map/pallas_call | solution.py:208
  80.0 4.8 %shard_map.42 = bf16[4,2,2,128,128]{4,3,2,1,0:T(8,128)(2,1)S(1)} custom-call(s32[4]{0:T(128)S(1)} %get-tuple-element.41.info, bf16[4,5,256,256]{3,2,1,0:T(8,128)(2,1)S(1)} %get-tuple-element.42.halves, f32[4,256,256]{2,1,0:T(8,128)S(1)} %shard_map.41.held, bf16[2,2,5,128,128]{4,3,2,1,0:T(8,128)(2,1)} %collective-permute-done.12.both, ...), custom_call_target="tpu_custom_call" | custom-call | flops 1024 | bytes 1024 | tf_op jit(solution)/shard_map/pallas_call | solution.py:216
  86.1 2.2 %collective-permute-start.21 = (bf16[2,2,128,128]{3,2,1,0:T(8,128)(2,1)S(1)}, bf16[2,2,128,128]{3,2,1,0:T(8,128)(2,1)S(1)}, u32[]{:S(2)}, u32[]{:S(2)}) collective-permute-start(bf16[2,2,128,128]{3,2,1,0:T(8,128)(2,1)S(1)} %get-tuple-element.53), channel_id=1, source_target_pairs={{0,8},{1,9},{2,10},{3,11},{4,12},{5,13},{6,14},{7,15},{8,1},{9,0},... | collective-permute-start | bytes 393224 | tf_op jit(solution)/shard_map/ppermute | solution.py:22
  88.3 1.1 %collective-permute-start.22 = (bf16[2,2,128,128]{3,2,1,0:T(8,128)(2,1)S(1)}, bf16[2,2,128,128]{3,2,1,0:T(8,128)(2,1)S(1)}, u32[]{:S(2)}, u32[]{:S(2)}) collective-permute-start(bf16[2,2,128,128]{3,2,1,0:T(8,128)(2,1)S(1)} %get-tuple-element.52), channel_id=1, source_target_pairs={{0,24},{1,25},{2,26},{3,27},{4,28},{5,29},{6,30},{7,31},{8,17},{9,... | collective-permute-start | bytes 393224 | tf_op jit(solution)/shard_map/ppermute | solution.py:22
  89.4 1.2 %collective-permute-done.24 = bf16[2,2,128,128]{3,2,0,1:T(8,128)(2,1)S(1)} collective-permute-done((bf16[2,2,128,128]{3,2,0,1:T(8,128)(2,1)S(1)}, bf16[2,2,128,128]{3,2,0,1:T(8,128)(2,1)S(1)}, u32[]{:S(2)}, u32[]{:S(2)}) %collective-permute-start.24) | collective-permute-done | bytes 131104 | tf_op jit(solution)/shard_map/ppermute | solution.py:22
  90.6 3.0 %collective-permute-done.21 = bf16[2,2,128,128]{3,2,1,0:T(8,128)(2,1)S(1)} collective-permute-done((bf16[2,2,128,128]{3,2,1,0:T(8,128)(2,1)S(1)}, bf16[2,2,128,128]{3,2,1,0:T(8,128)(2,1)S(1)}, u32[]{:S(2)}, u32[]{:S(2)}) %collective-permute-start.21) | collective-permute-done | bytes 131104 | tf_op jit(solution)/shard_map/ppermute | solution.py:22
  93.6 1.9 %collective-permute-done.22 = bf16[2,2,128,128]{3,2,1,0:T(8,128)(2,1)S(1)} collective-permute-done((bf16[2,2,128,128]{3,2,1,0:T(8,128)(2,1)S(1)}, bf16[2,2,128,128]{3,2,1,0:T(8,128)(2,1)S(1)}, u32[]{:S(2)}, u32[]{:S(2)}) %collective-permute-start.22) | collective-permute-done | bytes 131104 | tf_op jit(solution)/shard_map/ppermute | solution.py:22
  (59 shorter events, 10.2 us)
Async XLA Ops:
  1.1 23.5 %collective-permute-start = (bf16[2,5,128,128]{3,2,1,0:T(8,128)(2,1)S(1)}, bf16[2,5,128,128]{3,2,1,0:T(8,128)(2,1)S(1)}, u32[]{:S(2)}, u32[]{:S(2)}) collective-permute-start(bf16[2,5,128,128]{3,2,1,0:T(8,128)(2,1)S(1)} %get-tuple-element.49), channel_id=1, source_target_pairs={{0,16},{1,17},{2,18},{3,19},{4,20},{5,21},{6,22},{7,23},{8,24},{9,... | collective-permute-start | bytes 983048 | tf_op jit(solution)/shard_map/ppermute | solution.py:22
  5.9 7.1 %collective-permute-start.1 = (bf16[2,2,128,128]{3,2,1,0:T(8,128)(2,1)S(1)}, bf16[2,2,128,128]{3,2,1,0:T(8,128)(2,1)S(1)}, u32[]{:S(2)}, u32[]{:S(2)}) collective-permute-start(bf16[2,2,128,128]{3,2,1,0:T(8,128)(2,1)S(1)} %get-tuple-element.55.refs_0_), channel_id=1, source_target_pairs={{0,2},{1,3},{2,0},{3,1},{4,6},{5,7},{6,4},{7,5},{8,10},{9,11},{10,... | collective-permute-start | bytes 393224 | tf_op jit(solution)/shard_map/ppermute | solution.py:22
  7.5 11.9 %collective-permute-start.2 = (bf16[2,2,128,128]{3,2,1,0:T(8,128)(2,1)S(1)}, bf16[2,2,128,128]{3,2,1,0:T(8,128)(2,1)S(1)}, u32[]{:S(2)}, u32[]{:S(2)}) collective-permute-start(bf16[2,2,128,128]{3,2,1,0:T(8,128)(2,1)S(1)} %get-tuple-element.25), channel_id=1, source_target_pairs={{0,3},{1,2},{2,1},{3,0},{4,7},{5,6},{6,5},{7,4},{8,11},{9,10},{10,... | collective-permute-start | bytes 393224 | tf_op jit(solution)/shard_map/ppermute | solution.py:22
  8.9 12.6 %collective-permute-start.4 = (bf16[2,2,128,128]{3,2,1,0:T(8,128)(2,1)S(1)}, bf16[2,2,128,128]{3,2,1,0:T(8,128)(2,1)S(1)}, u32[]{:S(2)}, u32[]{:S(2)}) collective-permute-start(bf16[2,2,128,128]{3,2,1,0:T(8,128)(2,1)S(1)} %get-tuple-element.55.refs_0_), channel_id=1, source_target_pairs={{0,4},{1,5},{2,6},{3,7},{4,0},{5,1},{6,2},{7,3},{8,12},{9,13},{10,... | collective-permute-start | bytes 393224 | tf_op jit(solution)/shard_map/ppermute | solution.py:22
  11.5 11.7 %collective-permute-start.5 = (bf16[2,2,128,128]{3,2,1,0:T(8,128)(2,1)S(1)}, bf16[2,2,128,128]{3,2,1,0:T(8,128)(2,1)S(1)}, u32[]{:S(2)}, u32[]{:S(2)}) collective-permute-start(bf16[2,2,128,128]{3,2,1,0:T(8,128)(2,1)S(1)} %get-tuple-element.25), channel_id=1, source_target_pairs={{0,5},{1,4},{2,7},{3,6},{4,1},{5,0},{6,3},{7,2},{8,13},{9,12},{10,... | collective-permute-start | bytes 393224 | tf_op jit(solution)/shard_map/ppermute | solution.py:22
  19.5 5.2 %collective-permute-start.3 = (bf16[2,2,128,128]{3,2,1,0:T(8,128)(2,1)S(1)}, bf16[2,2,128,128]{3,2,1,0:T(8,128)(2,1)S(1)}, u32[]{:S(2)}, u32[]{:S(2)}) collective-permute-start(bf16[2,2,128,128]{3,2,1,0:T(8,128)(2,1)S(1)} %get-tuple-element.25), channel_id=1, source_target_pairs={{0,1},{1,0},{2,3},{3,2},{4,5},{5,4},{6,7},{7,6},{8,9},{9,8},{10,11... | collective-permute-start | bytes 393224 | tf_op jit(solution)/shard_map/ppermute | solution.py:22
  24.6 0.9 copy-start.6
  24.7 38.3 %copy-start = (bf16[2,2,5,128,128]{4,3,2,1,0:T(8,128)(2,1)}, bf16[2,2,5,128,128]{4,3,2,1,0:T(8,128)(2,1)S(1)}, u32[]{:S(2)}) copy-start(bf16[2,2,5,128,128]{4,3,2,1,0:T(8,128)(2,1)S(1)} %pad_maximum_fusion.1.e) | copy-start | bytes 1966084
  24.7 2.9 %collective-permute-start.6 = (bf16[2,2,5,128,128]{4,3,2,1,0:T(8,128)(2,1)S(1)}, bf16[2,2,5,128,128]{4,3,2,1,0:T(8,128)(2,1)S(1)}, u32[]{:S(2)}, u32[]{:S(2)}) collective-permute-start(bf16[2,2,5,128,128]{4,3,2,1,0:T(8,128)(2,1)S(1)} %pad_maximum_fusion.1.e), channel_id=1, source_target_pairs={{0,8},{1,9},{2,10},{3,11},{4,12},{5,13},{6,14},{7,15},{8,0},{9,1},... | collective-permute-start | bytes 1966088 | tf_op jit(solution)/shard_map/ppermute | solution.py:22
  25.6 23.3 %collective-permute-start.10 = (bf16[3,2,256,256]{3,2,1,0:T(8,128)(2,1)S(1)}, bf16[3,2,256,256]{3,2,1,0:T(8,128)(2,1)}, u32[]{:S(2)}, u32[]{:S(2)}) collective-permute-start(bf16[3,2,256,256]{3,2,1,0:T(8,128)(2,1)S(1)} %shard_map.38), channel_id=1, source_target_pairs={{0,16},{1,17},{2,18},{3,19},{4,20},{5,21},{6,22},{7,23},{8,24},{9,... | collective-permute-start | bytes 2359304 | tf_op jit(solution)/shard_map/ppermute | solution.py:22
  26.1 22.7 %collective-permute-start.7 = (bf16[2,2,5,128,128]{4,3,2,1,0:T(8,128)(2,1)S(1)}, bf16[2,2,5,128,128]{4,3,2,1,0:T(8,128)(2,1)S(1)}, u32[]{:S(2)}, u32[]{:S(2)}) collective-permute-start(bf16[2,2,5,128,128]{4,3,2,1,0:T(8,128)(2,1)S(1)} %pad_maximum_fusion.1.e), channel_id=1, source_target_pairs={{0,1},{1,0},{2,3},{3,2},{4,5},{5,4},{6,7},{7,6},{8,9},{9,8},{10,11... | collective-permute-start | bytes 1966088 | tf_op jit(solution)/shard_map/ppermute | solution.py:22
  28.8 20.0 %collective-permute-start.11 = (bf16[2,5,128,128]{3,2,1,0:T(8,128)(2,1)S(1)}, bf16[2,5,128,128]{3,2,1,0:T(8,128)(2,1)S(1)}, u32[]{:S(2)}, u32[]{:S(2)}) collective-permute-start(bf16[2,5,128,128]{3,2,1,0:T(8,128)(2,1)S(1)} %get-tuple-element.46), channel_id=1, source_target_pairs={{0,6},{1,7},{2,0},{3,1},{4,2},{5,3},{6,4},{7,5},{8,10},{9,11},{10,... | collective-permute-start | bytes 983048 | tf_op jit(solution)/shard_map/ppermute | solution.py:22
  31.2 21.1 %collective-permute-start.8 = (bf16[2,5,128,128]{3,2,1,0:T(8,128)(2,1)S(1)}, bf16[2,5,128,128]{3,2,1,0:T(8,128)(2,1)S(1)}, u32[]{:S(2)}, u32[]{:S(2)}) collective-permute-start(bf16[2,5,128,128]{3,2,1,0:T(8,128)(2,1)S(1)} %get-tuple-element.47), channel_id=1, source_target_pairs={{0,4},{1,5},{2,6},{3,7},{4,0},{5,1},{6,2},{7,3},{8,12},{9,13},{10,... | collective-permute-start | bytes 983048 | tf_op jit(solution)/shard_map/ppermute | solution.py:22
  31.8 17.1 %collective-permute-start.9 = (bf16[1,2,256,256]{3,2,1,0:T(8,128)(2,1)S(1)}, bf16[1,2,256,256]{3,2,1,0:T(8,128)(2,1)S(1)}, u32[]{:S(2)}, u32[]{:S(2)}) collective-permute-start(bf16[1,2,256,256]{3,2,1,0:T(8,128)(2,1)S(1)} %shard_map.37), channel_id=1, source_target_pairs={{0,2},{1,3},{2,0},{3,1},{4,6},{5,7},{6,4},{7,5},{8,10},{9,11},{10,... | collective-permute-start | bytes 786440 | tf_op jit(solution)/shard_map/ppermute | solution.py:22
  48.9 14.2 %copy-start.2 = (bf16[2,2,5,128,128]{4,3,2,1,0:T(8,128)(2,1)}, bf16[2,2,5,128,128]{4,3,2,1,0:T(8,128)(2,1)S(1)}, u32[]{:S(2)}) copy-start(bf16[2,2,5,128,128]{4,3,2,1,0:T(8,128)(2,1)S(1)} %collective-permute-done.7.xe) | copy-start | bytes 1966084
  53.6 10.8 %collective-permute-start.15 = (bf16[2,3,2,256,256]{4,3,2,1,0:T(8,128)(2,1)S(1)}, bf16[2,3,2,256,256]{4,3,2,1,0:T(8,128)(2,1)S(1)}, u32[]{:S(2)}, u32[]{:S(2)}) collective-permute-start(bf16[2,3,2,256,256]{4,3,2,1,0:T(8,128)(2,1)S(1)} %pad_maximum_fusion.own), channel_id=1, source_target_pairs={{0,8},{1,9},{2,10},{3,11},{4,12},{5,13},{6,14},{7,15},{8,0},{9,1},... | collective-permute-start | bytes 4718600 | tf_op jit(solution)/shard_map/ppermute | solution.py:22
  53.7 8.7 %collective-permute-start.16 = (bf16[1,2,256,256]{3,2,1,0:T(8,128)(2,1)S(1)}, bf16[1,2,256,256]{3,2,1,0:T(8,128)(2,1)S(1)}, u32[]{:S(2)}, u32[]{:S(2)}) collective-permute-start(bf16[1,2,256,256]{3,2,1,0:T(8,128)(2,1)S(1)} %collective-permute-done.9), channel_id=1, source_target_pairs={{0,16},{1,17},{2,18},{3,19},{4,20},{5,21},{6,22},{7,23},{8,24},{9,... | collective-permute-start | bytes 786440 | tf_op jit(solution)/shard_map/ppermute | solution.py:22
  55.1 7.4 %collective-permute-start.14 = (bf16[2,2,5,128,128]{4,3,2,1,0:T(8,128)(2,1)S(1)}, bf16[2,2,5,128,128]{4,3,2,1,0:T(8,128)(2,1)S(1)}, u32[]{:S(2)}, u32[]{:S(2)}) collective-permute-start(bf16[2,2,5,128,128]{4,3,2,1,0:T(8,128)(2,1)S(1)} %collective-permute-done.7.xe), channel_id=1, source_target_pairs={{0,8},{1,9},{2,10},{3,11},{4,12},{5,13},{6,14},{7,15},{8,0},{9,1},... | collective-permute-start | bytes 1966088 | tf_op jit(solution)/shard_map/ppermute | solution.py:22
  56.2 17.3 %collective-permute-start.13 = (bf16[2,2,5,128,128]{4,3,2,1,0:T(8,128)(2,1)}, bf16[2,2,5,128,128]{4,3,2,1,0:T(8,128)(2,1)}, u32[]{:S(2)}, u32[]{:S(2)}) collective-permute-start(bf16[2,2,5,128,128]{4,3,2,1,0:T(8,128)(2,1)} %pad_maximum_fusion.3.far), channel_id=1, source_target_pairs={{0,1},{1,0},{2,3},{3,2},{4,5},{5,4},{6,7},{7,6},{8,9},{9,8},{10,11... | collective-permute-start | bytes 1966088 | tf_op jit(solution)/shard_map/ppermute | solution.py:22
  57.2 16.9 %collective-permute-start.12 = (bf16[2,2,5,128,128]{4,3,2,1,0:T(8,128)(2,1)S(1)}, bf16[2,2,5,128,128]{4,3,2,1,0:T(8,128)(2,1)}, u32[]{:S(2)}, u32[]{:S(2)}) collective-permute-start(bf16[2,2,5,128,128]{4,3,2,1,0:T(8,128)(2,1)S(1)} %pad_maximum_fusion.2), channel_id=1, source_target_pairs={{0,2},{1,3},{2,0},{3,1},{4,6},{5,7},{6,4},{7,5},{8,10},{9,11},{10,... | collective-permute-start | bytes 1966088 | tf_op jit(solution)/shard_map/ppermute | solution.py:22
  62.5 2.0 %collective-permute-start.17 = (bf16[2,1,2,256,256]{4,3,2,1,0:T(8,128)(2,1)S(1)}, bf16[2,1,2,256,256]{4,3,2,1,0:T(8,128)(2,1)S(1)}, u32[]{:S(2)}, u32[]{:S(2)}) collective-permute-start(bf16[2,1,2,256,256]{4,3,2,1,0:T(8,128)(2,1)S(1)} %pad_maximum_fusion.4.own3), channel_id=1, source_target_pairs={{0,8},{1,9},{2,10},{3,11},{4,12},{5,13},{6,14},{7,15},{8,0},{9,1},... | collective-permute-start | bytes 1572872 | tf_op jit(solution)/shard_map/ppermute | solution.py:22
  62.5 1.4 %copy-start.4 = (bf16[2,2,5,128,128]{4,3,2,1,0:T(8,128)(2,1)}, bf16[2,2,5,128,128]{4,3,2,1,0:T(8,128)(2,1)S(1)}, u32[]{:S(2)}) copy-start(bf16[2,2,5,128,128]{4,3,2,1,0:T(8,128)(2,1)S(1)} %collective-permute-done.14.cxe) | copy-start | bytes 1966084
  62.5 17.4 %collective-permute-start.19 = (bf16[2,2,5,128,128]{4,3,2,1,0:T(8,128)(2,1)}, bf16[2,2,5,128,128]{4,3,2,1,0:T(8,128)(2,1)}, u32[]{:S(2)}, u32[]{:S(2)}) collective-permute-start(bf16[2,2,5,128,128]{4,3,2,1,0:T(8,128)(2,1)} %pad_maximum_fusion.3.far), channel_id=1, source_target_pairs={{0,8},{1,9},{2,10},{3,11},{4,12},{5,13},{6,14},{7,15},{8,0},{9,1},... | collective-permute-start | bytes 1966088 | tf_op jit(solution)/shard_map/ppermute | solution.py:22
  74.0 5.9 %collective-permute-start.18 = (bf16[2,2,5,128,128]{4,3,2,1,0:T(8,128)(2,1)}, bf16[2,2,5,128,128]{4,3,2,1,0:T(8,128)(2,1)}, u32[]{:S(2)}, u32[]{:S(2)}) collective-permute-start(bf16[2,2,5,128,128]{4,3,2,1,0:T(8,128)(2,1)} %collective-permute-done.12.both), channel_id=1, source_target_pairs={{0,8},{1,9},{2,10},{3,11},{4,12},{5,13},{6,14},{7,15},{8,0},{9,1},... | collective-permute-start | bytes 1966088 | tf_op jit(solution)/shard_map/ppermute | solution.py:22
  74.0 5.9 %collective-permute-start.20 = (bf16[2,2,5,128,128]{4,3,2,1,0:T(8,128)(2,1)}, bf16[2,2,5,128,128]{4,3,2,1,0:T(8,128)(2,1)}, u32[]{:S(2)}, u32[]{:S(2)}) collective-permute-start(bf16[2,2,5,128,128]{4,3,2,1,0:T(8,128)(2,1)} %collective-permute-done.13.beside), channel_id=1, source_target_pairs={{0,8},{1,9},{2,10},{3,11},{4,12},{5,13},{6,14},{7,15},{8,0},{9,1},... | collective-permute-start | bytes 1966088 | tf_op jit(solution)/shard_map/ppermute | solution.py:22
  74.5 1.1 %copy-start.1 = (bf16[2,2,5,128,128]{4,3,2,1,0:T(8,128)(2,1)S(1)}, bf16[2,2,5,128,128]{4,3,2,1,0:T(8,128)(2,1)}, u32[]{:S(2)}) copy-start(bf16[2,2,5,128,128]{4,3,2,1,0:T(8,128)(2,1)} %copy-done) | copy-start | bytes 1966084
  75.6 1.1 %copy-start.3 = (bf16[2,2,5,128,128]{4,3,2,1,0:T(8,128)(2,1)S(1)}, bf16[2,2,5,128,128]{4,3,2,1,0:T(8,128)(2,1)}, u32[]{:S(2)}) copy-start(bf16[2,2,5,128,128]{4,3,2,1,0:T(8,128)(2,1)} %copy-done.2) | copy-start | bytes 1966084
  76.7 1.1 %copy-start.5 = (bf16[2,2,5,128,128]{4,3,2,1,0:T(8,128)(2,1)S(1)}, bf16[2,2,5,128,128]{4,3,2,1,0:T(8,128)(2,1)}, u32[]{:S(2)}) copy-start(bf16[2,2,5,128,128]{4,3,2,1,0:T(8,128)(2,1)} %copy-done.4) | copy-start | bytes 1966084
  84.9 4.6 %collective-permute-start.23 = (bf16[2,2,128,128]{3,2,0,1:T(8,128)(2,1)S(1)}, bf16[2,2,128,128]{3,2,0,1:T(8,128)(2,1)S(1)}, u32[]{:S(2)}, u32[]{:S(2)}) collective-permute-start(bf16[2,2,128,128]{3,2,0,1:T(8,128)(2,1)S(1)} %copy.8), channel_id=1, source_target_pairs={{0,0},{1,1},{2,2},{3,3},{4,4},{5,5},{6,6},{7,7},{8,9},{9,8},{10,11... | collective-permute-start | bytes 393224 | tf_op jit(solution)/shard_map/ppermute | solution.py:22
  85.6 5.0 %collective-permute-start.24 = (bf16[2,2,128,128]{3,2,0,1:T(8,128)(2,1)S(1)}, bf16[2,2,128,128]{3,2,0,1:T(8,128)(2,1)S(1)}, u32[]{:S(2)}, u32[]{:S(2)}) collective-permute-start(bf16[2,2,128,128]{3,2,0,1:T(8,128)(2,1)S(1)} %copy.9), channel_id=1, source_target_pairs={{0,16},{1,17},{2,18},{3,19},{4,20},{5,21},{6,22},{7,23},{8,25},{9,... | collective-permute-start | bytes 393224 | tf_op jit(solution)/shard_map/ppermute | solution.py:22
  86.1 7.5 %collective-permute-start.21 = (bf16[2,2,128,128]{3,2,1,0:T(8,128)(2,1)S(1)}, bf16[2,2,128,128]{3,2,1,0:T(8,128)(2,1)S(1)}, u32[]{:S(2)}, u32[]{:S(2)}) collective-permute-start(bf16[2,2,128,128]{3,2,1,0:T(8,128)(2,1)S(1)} %get-tuple-element.53), channel_id=1, source_target_pairs={{0,8},{1,9},{2,10},{3,11},{4,12},{5,13},{6,14},{7,15},{8,1},{9,0},... | collective-permute-start | bytes 393224 | tf_op jit(solution)/shard_map/ppermute | solution.py:22
  88.3 7.2 %collective-permute-start.22 = (bf16[2,2,128,128]{3,2,1,0:T(8,128)(2,1)S(1)}, bf16[2,2,128,128]{3,2,1,0:T(8,128)(2,1)S(1)}, u32[]{:S(2)}, u32[]{:S(2)}) collective-permute-start(bf16[2,2,128,128]{3,2,1,0:T(8,128)(2,1)S(1)} %get-tuple-element.52), channel_id=1, source_target_pairs={{0,24},{1,25},{2,26},{3,27},{4,28},{5,29},{6,30},{7,31},{8,17},{9,... | collective-permute-start | bytes 393224 | tf_op jit(solution)/shard_map/ppermute | solution.py:22

commit v3 on v2

--- a/solution.py
+++ b/solution.py
@@ -44,18 +44,22 @@
                     out[n, p, pl.ds(rr * 128, 128), pl.ds(cc * 128, 128)] = refs[2 * n + cc][rr ^ x, p]
 
 
-def turn_kernel(info, e, ce, xe, cxe, out):
+def turn_kernel(info, e, ce, xe, cxe, out, blocks):
     x, core, g = info[0], info[1], info[2]
     vectors = e.shape[2]
     for half in range(2):
         for t in range(2):
+            slot = g ^ (half + 2 * t)
             for rr in range(2):
                 for q in range(vectors):
-                    tile = jnp.where(core == 0, (e, ce)[half][t, rr ^ x, q], (xe, cxe)[half][t, rr ^ x, q])
-                    out[g ^ (half + 2 * t), pl.ds(q * 128, 128), pl.ds(rr * 128, 128)] = tile.T
-
-
-def halves_kernel(info, rows, own, other, own3, other3, out, after, total):
+                    tiles = [ref[t, rr ^ x, q] for ref in ((e, ce)[half], (xe, cxe)[half])]
+                    for cc in range(2):
+                        blocks[slot, q, pl.ds(rr * 128, 128), pl.ds(cc * 128, 128)] = tiles[cc]
+                    tile = jnp.where(core == 0, tiles[0], tiles[1])
+                    out[slot, pl.ds(q * 128, 128), pl.ds(rr * 128, 128)] = tile.T
+
+
+def halves_kernel(info, rows, mine, own, other, own3, other3, out, after, total):
     x, g = info[0], info[2]
     for n in range(info.shape[0]):
         after[n] = info[n]
@@ -80,14 +84,12 @@
                 out[w, q, pl.ds(p * 128, 128), :] = value[q * 128 : (q + 1) * 128]
 
 
-def ladder_terms(x, halves, cases, total):
+def ladder_terms(halves, cases, total):
     vectors = halves.shape[1]
-    for i, j, columns in cases:
+    for i, j, factors in cases:
         direct, mirror = None, None
         for q in range(vectors):
-            factor = jnp.concatenate(
-                [jnp.concatenate([columns[cc][rr ^ x, q] for cc in range(2)], axis=1) for rr in range(2)], axis=0
-            )
+            factor = factors(q)
             term = lax.dot_general(halves[j, q], factor, (((1,), (1,)), ((), ())), preferred_element_type=jnp.float32)
             direct = term if direct is None else direct + term
             term = jnp.dot(halves[i, q], factor, preferred_element_type=jnp.float32)
@@ -96,27 +98,41 @@
         total[j] = total[j] + jnp.where(i == j, jnp.zeros_like(mirror), mirror)
 
 
-def ladder_own_kernel(info, halves, e, ce, xe, cxe, total):
-    x, g = info[0], info[2]
+def ladder_own_kernel(info, halves, mine, total):
+    vectors = halves.shape[1]
+    first = None
     for w in range(PLANES):
-        total[w] = jnp.zeros(total.shape[1:], jnp.float32)
-    cases = []
-    for half, (own, side) in enumerate(((e, xe), (ce, cxe))):
-        for t in range(2):
-            cases.append((g ^ (half + 2 * t), 0, (own.at[t], side.at[t])))
-    ladder_terms(x, halves, cases, total)
+        direct = None
+        for q in range(vectors):
+            term = lax.dot_general(
+                halves[0, q], mine[w, q], (((1,), (1,)), ((), ())), preferred_element_type=jnp.float32
+            )
+            direct = term if direct is None else direct + term
+            if w:
+                first = first + jnp.dot(halves[w, q], mine[w, q], preferred_element_type=jnp.float32)
+        if w:
+            total[w] = direct
+        else:
+            first = direct
+    total[0] = first
 
 
 def ladder_far_kernel(info, halves, held, both, both_other, far, far_other, beside, beside_other, out, total):
     x, g = info[0], info[2]
     total[...] = held[...]
+
+    def factors(columns):
+        return lambda q: jnp.concatenate(
+            [jnp.concatenate([columns[cc][rr ^ x, q] for cc in range(2)], axis=1) for rr in range(2)], axis=0
+        )
+
     cases = []
     for half, ref in enumerate((both, both_other)):
-        cases.append((*by_parity(g, half, (2, 1), (1, 1)), (ref.at[0], ref.at[1])))
+        cases.append((*by_parity(g, half, (2, 1), (1, 1)), factors((ref.at[0], ref.at[1]))))
     for n, pairs in enumerate((((2, 2), (3, 2)), ((3, 1), (3, 3)))):
         for half, (own, side) in enumerate(((far, beside), (far_other, beside_other))):
-            cases.append((*by_parity(g, half, *pairs), (own.at[n], side.at[n])))
-    ladder_terms(x, halves, cases, total)
+            cases.append((*by_parity(g, half, *pairs), factors((own.at[n], side.at[n]))))
+    ladder_terms(halves, cases, total)
     for w in range(PLANES):
         for rr in range(2):
             for p in range(2):
@@ -168,26 +184,32 @@
     e = jnp.stack([kept, taken])
     ce = swap_core(e)
     xe = swap_x(e)
-    got1 = move(jnp.where(g <= 1, kept, taken), lambda r, z, x: (r, z ^ 2, x))
     block2 = small_call(block_kernel, jax.ShapeDtypeStruct((1, 2, 256, 256), jnp.bfloat16), info, *away)
     block3 = move(block2, lambda r, z, x: (r, z ^ 1, x))
     trio_shape = jax.ShapeDtypeStruct((3, 2, 256, 256), jnp.bfloat16)
     trio = small_call(block_kernel, trio_shape, info, own_pairs, side, *near, *away)
     across = swap_y(trio)
-    piece = jnp.where((g & 1) == 0, jnp.where(g == 0, kept, taken), jnp.where(g == 3, ce[0], ce[1]))
-    got2 = move(piece, lambda r, z, x: (r, z ^ 1 if (r ^ z) & 1 else z ^ 3, x))
-    ce, xe, got1, block3, across, got2 = lax.optimization_barrier((ce, xe, got1, block3, across, got2))
-
+    piece1, ce, kept_again, taken_again = (jnp.where(g <= 1, kept, taken), *lax.optimization_barrier((ce, kept, taken)))
+    piece2 = jnp.where((g & 1) == 0, jnp.where(g == 0, kept_again, taken_again), jnp.where(g == 3, ce[0], ce[1]))
+    got1 = move(piece1, lambda r, z, x: (r, z ^ 2, x))
+    got2 = move(piece2, lambda r, z, x: (r, z ^ 1 if (r ^ z) & 1 else z ^ 3, x))
     n = (g == 0) | (g == 3)
     piece = jnp.stack([jnp.where(n, kept, taken), jnp.where(n, xe[0], xe[1])])
+    blocks = jnp.stack([trio, across])
+    ce, xe, got1, block3, blocks, got2, piece = lax.optimization_barrier((ce, xe, got1, block3, blocks, got2, piece))
+
     both = move(piece, lambda r, z, x: (r, z ^ 1, x))
     far = jnp.stack([got1, got2])
     beside = swap_x(far)
     across3 = swap_y(block3)
     cxe = swap_core(xe)
-    blocks = jnp.stack([trio, across])
-    rows = small_call(
-        turn_kernel, jax.ShapeDtypeStruct((PLANES, vectors * 128, 256), jnp.bfloat16), info, e, ce, xe, cxe
+    rows, mine = small_call(
+        turn_kernel,
+        (
+            jax.ShapeDtypeStruct((PLANES, vectors * 128, 256), jnp.bfloat16),
+            jax.ShapeDtypeStruct((PLANES, vectors, 256, 256), jnp.bfloat16),
+        ),
+        info, e, ce, xe, cxe,
     )
     far_other = swap_core(far)
     near3 = jnp.stack([block3, across3])
@@ -197,22 +219,22 @@
             jax.ShapeDtypeStruct((PLANES, vectors, 256, 256), jnp.bfloat16),
             jax.ShapeDtypeStruct(info.shape, info.dtype),
         ),
-        in_specs=[SMEM] + [VMEM] * 5,
+        in_specs=[SMEM] + [VMEM] * 6,
         out_specs=(VMEM, SMEM),
         scratch_shapes=[pltpu.VMEM((PLANES, 2, vectors * 128, 256), jnp.float32)],
         compiler_params=pltpu.CompilerParams(vmem_limit_bytes=16 << 20),
         cost_estimate=pl.CostEstimate(flops=1 << 10, bytes_accessed=1 << 10, transcendentals=0),
-    )(info, rows, blocks, swap_core(blocks), near3, swap_core(near3))
+    )(info, rows, mine, blocks, swap_core(blocks), near3, swap_core(near3))
     both, beside, info = lax.optimization_barrier((both, beside, info))
 
     held = pl.pallas_call(
         ladder_own_kernel,
         out_shape=jax.ShapeDtypeStruct((PLANES, 256, 256), jnp.float32),
-        in_specs=[SMEM] + [VMEM] * 5,
+        in_specs=[SMEM] + [VMEM] * 2,
         out_specs=VMEM,
         compiler_params=pltpu.CompilerParams(vmem_limit_bytes=8 << 20),
         cost_estimate=pl.CostEstimate(flops=1 << 10, bytes_accessed=1 << 10, transcendentals=0),
-    )(info, halves, e, ce, xe, cxe)
+    )(info, halves, mine)
     partial = pl.pallas_call(
         ladder_far_kernel,
         out_shape=jax.ShapeDtypeStruct((PLANES, 2, 2, 128, 128), jnp.bfloat16),

time: 96.8 us -> 92.6 us (0.957)
  waiting for transfers between devices: 46.7 us -> 43.1 us
  starting transfers between devices: 22.3 us -> 25.6 us
  other arithmetic: 6.23 us -> 4.2 us
  local copies, waits for them, and re-layouts: 4.49 us -> 2.96 us
    ppermute x25, waiting for transfers between devices: 46.7 us -> 43.1 us  [move(): return lax.ppermute(value, ('row', 'col'), pairs)]
    ppermute x25, starting transfers between devices: 22.3 us -> 25.6 us  [move(): return lax.ppermute(value, ('row', 'col'), pairs)]
    unnamed x14 -> x4, local copies, waits for them, and re-layouts: 3.28 us -> 1.74 us
    another operation x1, other arithmetic: 1.28 us -> 0.15 us  [fast_body(): blocks = jnp.stack([trio, across])]
  transfers between devices with their start and end apart: 25 -> 25, of which waited for: 14 -> 16; matrix products, arithmetic and copies ran while one was open for 4% -> 4% of each run, Pallas kernels for 12% -> 13%
where the time goes in v3:
time: 92.6 us; the launch traced here: 92.3 us
  waiting for transfers between devices  43.1 us (47%)
  starting transfers between devices  25.6 us (28%)
  Pallas kernels  16.2 us (17%)
  other arithmetic  4.2 us (5%)
  local copies, waits for them, and re-layouts  2.96 us (3%)
    ppermute x25, waiting for transfers between devices, move(): return lax.ppermute(value, ('row', 'col'), pairs)  43.1 us
    ppermute x25, starting transfers between devices, move(): return lax.ppermute(value, ('row', 'col'), pairs)  25.6 us
    pallas_call x1, Pallas kernels, fast_body(): pl.pallas_call(halves_kernel, out_shape=(jax.ShapeDtypeStruct((PLANES, ve...  7.18 us
    pallas_call x1, Pallas kernels, fast_body(): pl.pallas_call(ladder_far_kernel, out_shape=jax.ShapeDtypeStruct((PLANES,...  4.61 us
    pallas_call x3, Pallas kernels, small_call(): pl.pallas_call(kernel, out_shape=out_shape, in_specs=specs, out_specs=jax...  2.49 us
    pallas_call x1, Pallas kernels, fast_body(): pl.pallas_call(ladder_own_kernel, out_shape=jax.ShapeDtypeStruct((PLANES,...  1.92 us
  transfers between devices with their start and end apart: 25, of which 16 were waited for; matrix products, arithmetic and copies ran while one was open for 4% of the time, Pallas kernels for 13%

profile of v3, /device:TPU:0, one launch (start us, length us, event | category | flops | bytes accessed | tf_op | source)
XLA Modules:
  0.0 92.3 jit_solution(6142367551095627541)
XLA Ops:
  0.0 1.1 %dynamic-slice_bitcast_fusion.2 = (bf16[1,2,5,128,128]{4,3,2,1,0:T(8,128)(2,1)S(1)}, bf16[2,5,128,128]{3,2,1,0:T(8,128)(2,1)S(1)}) fusion(bf16[2,1,10,128,128]{4,3,2,1,0:T(8,128)(2,1)} %param.4, s32[]{:T(128)S(6)} %select_n.86, s32[]{:T(128)S(6)} %select_n.87), kind=kLoop, calls=%fused_computation.11 | loop fusion | bytes 1310728 | tf_op jit(solution)/shard_map/stack | solution.py:184
  1.1 3.0 %collective-permute-start = (bf16[2,5,128,128]{3,2,1,0:T(8,128)(2,1)S(1)}, bf16[2,5,128,128]{3,2,1,0:T(8,128)(2,1)S(1)}, u32[]{:S(2)}, u32[]{:S(2)}) collective-permute-start(bf16[2,5,128,128]{3,2,1,0:T(8,128)(2,1)S(1)} %get-tuple-element.60), channel_id=1, source_target_pairs={{0,16},{1,17},{2,18},{3,19},{4,20},{5,21},{6,22},{7,23},{8,24},{9,... | collective-permute-start | bytes 983048 | tf_op jit(solution)/shard_map/ppermute | solution.py:22
  4.8 1.0 %fusion = bf16[2,4,128,128]{3,2,1,0:T(8,128)(2,1)S(1)} fusion(bf16[2,1,4,128,128]{4,3,2,1,0:T(8,128)(2,1)} %param.3, bf16[2]{0:T(256)(128)(2,1)S(1)} %convert_bitcast_fusion), kind=kLoop, calls=%fused_computation.14 | loop fusion | flops 131072 | bytes 524292 | tf_op jit(solution)/shard_map/squeeze | solution.py:169
  5.9 1.6 %collective-permute-start.1 = (bf16[2,2,128,128]{3,2,1,0:T(8,128)(2,1)S(1)}, bf16[2,2,128,128]{3,2,1,0:T(8,128)(2,1)S(1)}, u32[]{:S(2)}, u32[]{:S(2)}) collective-permute-start(bf16[2,2,128,128]{3,2,1,0:T(8,128)(2,1)S(1)} %get-tuple-element.66.refs_0_), channel_id=1, source_target_pairs={{0,2},{1,3},{2,0},{3,1},{4,6},{5,7},{6,4},{7,5},{8,10},{9,11},{10,... | collective-permute-start | bytes 393224 | tf_op jit(solution)/shard_map/ppermute | solution.py:22
  7.5 1.4 %collective-permute-start.2 = (bf16[2,2,128,128]{3,2,1,0:T(8,128)(2,1)S(1)}, bf16[2,2,128,128]{3,2,1,0:T(8,128)(2,1)S(1)}, u32[]{:S(2)}, u32[]{:S(2)}) collective-permute-start(bf16[2,2,128,128]{3,2,1,0:T(8,128)(2,1)S(1)} %get-tuple-element.31), channel_id=1, source_target_pairs={{0,3},{1,2},{2,1},{3,0},{4,7},{5,6},{6,5},{7,4},{8,11},{9,10},{10,... | collective-permute-start | bytes 393224 | tf_op jit(solution)/shard_map/ppermute | solution.py:22
  8.9 2.6 %collective-permute-start.4 = (bf16[2,2,128,128]{3,2,1,0:T(8,128)(2,1)S(1)}, bf16[2,2,128,128]{3,2,1,0:T(8,128)(2,1)S(1)}, u32[]{:S(2)}, u32[]{:S(2)}) collective-permute-start(bf16[2,2,128,128]{3,2,1,0:T(8,128)(2,1)S(1)} %get-tuple-element.66.refs_0_), channel_id=1, source_target_pairs={{0,4},{1,5},{2,6},{3,7},{4,0},{5,1},{6,2},{7,3},{8,12},{9,13},{10,... | collective-permute-start | bytes 393224 | tf_op jit(solution)/shard_map/ppermute | solution.py:22
  11.8 1.1 %collective-permute-done.1.refs_2_ = bf16[2,2,128,128]{3,2,1,0:T(8,128)(2,1)S(1)} collective-permute-done((bf16[2,2,128,128]{3,2,1,0:T(8,128)(2,1)S(1)}, bf16[2,2,128,128]{3,2,1,0:T(8,128)(2,1)S(1)}, u32[]{:S(2)}, u32[]{:S(2)}) %collective-permute-start.1) | collective-permute-done | bytes 131104 | tf_op jit(solution)/shard_map/ppermute | solution.py:22
  13.0 6.5 %collective-permute-done.2.refs_3_ = bf16[2,2,128,128]{3,2,1,0:T(8,128)(2,1)S(1)} collective-permute-done((bf16[2,2,128,128]{3,2,1,0:T(8,128)(2,1)S(1)}, bf16[2,2,128,128]{3,2,1,0:T(8,128)(2,1)S(1)}, u32[]{:S(2)}, u32[]{:S(2)}) %collective-permute-start.2) | collective-permute-done | bytes 131104 | tf_op jit(solution)/shard_map/ppermute | solution.py:22
  19.5 2.1 %collective-permute-done.4.refs_0_.refs_4_ = bf16[2,2,128,128]{3,2,1,0:T(8,128)(2,1)S(1)} collective-permute-done((bf16[2,2,128,128]{3,2,1,0:T(8,128)(2,1)S(1)}, bf16[2,2,128,128]{3,2,1,0:T(8,128)(2,1)S(1)}, u32[]{:S(2)}, u32[]{:S(2)}) %collective-permute-start.4) | collective-permute-done | bytes 131104 | tf_op jit(solution)/shard_map/ppermute | solution.py:22
  21.6 1.7 %collective-permute-done.5.refs_1_.refs_5_ = bf16[2,2,128,128]{3,2,1,0:T(8,128)(2,1)S(1)} collective-permute-done((bf16[2,2,128,128]{3,2,1,0:T(8,128)(2,1)S(1)}, bf16[2,2,128,128]{3,2,1,0:T(8,128)(2,1)S(1)}, u32[]{:S(2)}, u32[]{:S(2)}) %collective-permute-start.5) | collective-permute-done | bytes 131104 | tf_op jit(solution)/shard_map/ppermute | solution.py:22
  23.3 1.4 %collective-permute-done.3.refs_1_ = bf16[2,2,128,128]{3,2,1,0:T(8,128)(2,1)S(1)} collective-permute-done((bf16[2,2,128,128]{3,2,1,0:T(8,128)(2,1)S(1)}, bf16[2,2,128,128]{3,2,1,0:T(8,128)(2,1)S(1)}, u32[]{:S(2)}, u32[]{:S(2)}) %collective-permute-start.3) | collective-permute-done | bytes 131104 | tf_op jit(solution)/shard_map/ppermute | solution.py:22
  24.9 1.5 %collective-permute-start.7 = (bf16[2,2,5,128,128]{4,3,2,1,0:T(8,128)(2,1)S(1)}, bf16[2,2,5,128,128]{4,3,2,1,0:T(8,128)(2,1)S(1)}, u32[]{:S(2)}, u32[]{:S(2)}) collective-permute-start(bf16[2,2,5,128,128]{4,3,2,1,0:T(8,128)(2,1)S(1)} %pad_maximum_fusion.1.e), channel_id=1, source_target_pairs={{0,1},{1,0},{2,3},{3,2},{4,5},{5,4},{6,7},{7,6},{8,9},{9,8},{10,11... | collective-permute-start | bytes 1966088 | tf_op jit(solution)/shard_map/ppermute | solution.py:22
  28.2 1.0 %select_bitcast_fusion = (bf16[1,2,5,128,128]{4,3,2,1,0:T(8,128)(2,1)S(1)}, bf16[2,5,128,128]{3,2,1,0:T(8,128)(2,1)S(1)}) fusion(bf16[2,5,128,128]{3,2,1,0:T(8,128)(2,1)S(1)} %collective-permute-done, pred[]{:T(512)S(6)} %or.3, bf16[2,1,10,128,128]{4,3,2,1,0:T(8,128)(2,1)} %param.4, s32[]{:T(128)S(6)} %select_n.86), kind=kLoop, calls=%fused_computation.7 | loop fusion | flops 163840 | bytes 1310725 | tf_op jit(solution)/shard_map/stack | solution.py:197
  29.4 2.9 %collective-permute-start.9 = (bf16[1,2,256,256]{3,2,1,0:T(8,128)(2,1)S(1)}, bf16[1,2,256,256]{3,2,1,0:T(8,128)(2,1)S(1)}, u32[]{:S(2)}, u32[]{:S(2)}) collective-permute-start(bf16[1,2,256,256]{3,2,1,0:T(8,128)(2,1)S(1)} %shard_map.37), channel_id=1, source_target_pairs={{0,2},{1,3},{2,0},{3,1},{4,6},{5,7},{6,4},{7,5},{8,10},{9,11},{10,... | collective-permute-start | bytes 786440 | tf_op jit(solution)/shard_map/ppermute | solution.py:22
  32.3 1.6 %collective-permute-start.11 = (bf16[2,5,128,128]{3,2,1,0:T(8,128)(2,1)S(1)}, bf16[2,5,128,128]{3,2,1,0:T(8,128)(2,1)S(1)}, u32[]{:S(2)}, u32[]{:S(2)}) collective-permute-start(bf16[2,5,128,128]{3,2,1,0:T(8,128)(2,1)S(1)} %bitcast_select_fusion), channel_id=1, source_target_pairs={{0,6},{1,7},{2,0},{3,1},{4,2},{5,3},{6,4},{7,5},{8,10},{9,11},{10,... | collective-permute-start | bytes 983048 | tf_op jit(solution)/shard_map/ppermute | solution.py:22
  33.9 8.1 %collective-permute-done.7.xe = bf16[2,2,5,128,128]{4,3,2,1,0:T(8,128)(2,1)S(1)} collective-permute-done((bf16[2,2,5,128,128]{4,3,2,1,0:T(8,128)(2,1)S(1)}, bf16[2,2,5,128,128]{4,3,2,1,0:T(8,128)(2,1)S(1)}, u32[]{:S(2)}, u32[]{:S(2)}) %collective-permute-start.7) | collective-permute-done | bytes 655392 | tf_op jit(solution)/shard_map/ppermute | solution.py:22
  42.1 5.3 %collective-permute-done.10 = bf16[3,2,256,256]{3,2,1,0:T(8,128)(2,1)S(1)} collective-permute-done((bf16[3,2,256,256]{3,2,1,0:T(8,128)(2,1)S(1)}, bf16[3,2,256,256]{3,2,1,0:T(8,128)(2,1)S(1)}, u32[]{:S(2)}, u32[]{:S(2)}) %collective-permute-start.10) | collective-permute-done | bytes 786464 | tf_op jit(solution)/shard_map/ppermute | solution.py:22
  47.5 1.2 %collective-permute-done.8 = bf16[2,5,128,128]{3,2,1,0:T(8,128)(2,1)S(1)} collective-permute-done((bf16[2,5,128,128]{3,2,1,0:T(8,128)(2,1)S(1)}, bf16[2,5,128,128]{3,2,1,0:T(8,128)(2,1)S(1)}, u32[]{:S(2)}, u32[]{:S(2)}) %collective-permute-start.8) | collective-permute-done | bytes 327712 | tf_op jit(solution)/shard_map/ppermute | solution.py:22
  48.7 3.6 %collective-permute-done.11 = bf16[2,5,128,128]{3,2,1,0:T(8,128)(2,1)S(1)} collective-permute-done((bf16[2,5,128,128]{3,2,1,0:T(8,128)(2,1)S(1)}, bf16[2,5,128,128]{3,2,1,0:T(8,128)(2,1)S(1)}, u32[]{:S(2)}, u32[]{:S(2)}) %collective-permute-start.11) | collective-permute-done | bytes 327712 | tf_op jit(solution)/shard_map/ppermute | solution.py:22
  52.4 1.5 %collective-permute-start.16 = (bf16[1,2,256,256]{3,2,1,0:T(8,128)(2,1)S(1)}, bf16[1,2,256,256]{3,2,1,0:T(8,128)(2,1)S(1)}, u32[]{:S(2)}, u32[]{:S(2)}) collective-permute-start(bf16[1,2,256,256]{3,2,1,0:T(8,128)(2,1)S(1)} %collective-permute-done.9), channel_id=1, source_target_pairs={{0,16},{1,17},{2,18},{3,19},{4,20},{5,21},{6,22},{7,23},{8,24},{9,... | collective-permute-start | bytes 786440 | tf_op jit(solution)/shard_map/ppermute | solution.py:22
  55.0 1.8 %collective-permute-start.12 = (bf16[2,2,5,128,128]{4,3,2,1,0:T(8,128)(2,1)S(1)}, bf16[2,2,5,128,128]{4,3,2,1,0:T(8,128)(2,1)}, u32[]{:S(2)}, u32[]{:S(2)}) collective-permute-start(bf16[2,2,5,128,128]{4,3,2,1,0:T(8,128)(2,1)S(1)} %pad_maximum_fusion.2), channel_id=1, source_target_pairs={{0,2},{1,3},{2,0},{3,1},{4,6},{5,7},{6,4},{7,5},{8,10},{9,11},{10,... | collective-permute-start | bytes 1966088 | tf_op jit(solution)/shard_map/ppermute | solution.py:22
  56.9 4.2 %collective-permute-done.16 = bf16[1,2,256,256]{3,2,1,0:T(8,128)(2,1)S(1)} collective-permute-done((bf16[1,2,256,256]{3,2,1,0:T(8,128)(2,1)S(1)}, bf16[1,2,256,256]{3,2,1,0:T(8,128)(2,1)S(1)}, u32[]{:S(2)}, u32[]{:S(2)}) %collective-permute-start.16) | collective-permute-done | bytes 262176 | tf_op jit(solution)/shard_map/ppermute | solution.py:22
  61.8 1.2 %shard_map.39 = (bf16[4,640,256]{2,1,0:T(8,128)(2,1)S(1)}, bf16[4,5,256,256]{3,2,1,0:T(8,128)(2,1)S(1)}) custom-call(s32[4]{0:T(128)S(1)} %pad_add_fusion.info, bf16[2,2,5,128,128]{4,3,2,1,0:T(8,128)(2,1)S(1)} %pad_maximum_fusion.1.e, bf16[2,2,5,128,128]{4,3,2,1,0:T(8,128)(2,1)S(1)} %collective-permute-done.6.ce, ...), custom_call_target="tpu_custom_call" | custom-call | flops 1024 | bytes 1024 | tf_op jit(solution)/shard_map/pallas_call | solution.py:153
  63.2 7.2 %shard_map.40 = (bf16[4,5,256,256]{3,2,1,0:T(8,128)(2,1)S(1)}, s32[4]{0:T(128)S(1)}) custom-call(s32[4]{0:T(128)S(1)} %pad_add_fusion.info, bf16[4,640,256]{2,1,0:T(8,128)(2,1)S(1)} %get-tuple-element.48.rows, bf16[4,5,256,256]{3,2,1,0:T(8,128)(2,1)S(1)} %get-tuple-element.49.mine, bf16[2,3,2,256,256]{4,3,2,1,0:T(8,128)(2,1)S(1)} %pad_maximum_fusion.own, ...), custom_call_target="tpu_custom_call" | custom-call | flops 1024 | bytes 1024 | tf_op jit(solution)/shard_map/pallas_call | solution.py:216
  72.4 1.7 %copy-done.1 = bf16[4,5,256,256]{3,2,1,0:T(8,128)(2,1)S(1)} copy-done((bf16[4,5,256,256]{3,2,1,0:T(8,128)(2,1)S(1)}, bf16[4,5,256,256]{3,2,1,0:T(8,128)(2,1)}, u32[]{:S(2)}) %copy-start.1) | copy-done | bytes 2621464
  74.1 1.9 %shard_map.41.held = f32[4,256,256]{2,1,0:T(8,128)S(1)} custom-call(s32[4]{0:T(128)S(1)} %get-tuple-element.53.info, bf16[4,5,256,256]{3,2,1,0:T(8,128)(2,1)S(1)} %get-tuple-element.54.halves, bf16[4,5,256,256]{3,2,1,0:T(8,128)(2,1)S(1)} %copy-done.1), custom_call_target="tpu_custom_call" | custom-call | flops 1024 | bytes 1024 | tf_op jit(solution)/shard_map/pallas_call | solution.py:230
  76.1 4.6 %shard_map.42 = bf16[4,2,2,128,128]{4,3,2,1,0:T(8,128)(2,1)S(1)} custom-call(s32[4]{0:T(128)S(1)} %get-tuple-element.53.info, bf16[4,5,256,256]{3,2,1,0:T(8,128)(2,1)S(1)} %get-tuple-element.54.halves, f32[4,256,256]{2,1,0:T(8,128)S(1)} %shard_map.41.held, bf16[2,2,5,128,128]{4,3,2,1,0:T(8,128)(2,1)} %collective-permute-done.12.both, ...), custom_call_target="tpu_custom_call" | custom-call | flops 1024 | bytes 1024 | tf_op jit(solution)/shard_map/pallas_call | solution.py:238
  82.0 2.2 %collective-permute-start.21 = (bf16[2,2,128,128]{3,2,1,0:T(8,128)(2,1)S(1)}, bf16[2,2,128,128]{3,2,1,0:T(8,128)(2,1)S(1)}, u32[]{:S(2)}, u32[]{:S(2)}) collective-permute-start(bf16[2,2,128,128]{3,2,1,0:T(8,128)(2,1)S(1)} %get-tuple-element.64), channel_id=1, source_target_pairs={{0,8},{1,9},{2,10},{3,11},{4,12},{5,13},{6,14},{7,15},{8,1},{9,0},... | collective-permute-start | bytes 393224 | tf_op jit(solution)/shard_map/ppermute | solution.py:22
  84.1 1.2 %collective-permute-start.22 = (bf16[2,2,128,128]{3,2,1,0:T(8,128)(2,1)S(1)}, bf16[2,2,128,128]{3,2,1,0:T(8,128)(2,1)S(1)}, u32[]{:S(2)}, u32[]{:S(2)}) collective-permute-start(bf16[2,2,128,128]{3,2,1,0:T(8,128)(2,1)S(1)} %get-tuple-element.63), channel_id=1, source_target_pairs={{0,24},{1,25},{2,26},{3,27},{4,28},{5,29},{6,30},{7,31},{8,17},{9,... | collective-permute-start | bytes 393224 | tf_op jit(solution)/shard_map/ppermute | solution.py:22
  85.3 1.2 %collective-permute-done.24 = bf16[2,2,128,128]{3,2,0,1:T(8,128)(2,1)S(1)} collective-permute-done((bf16[2,2,128,128]{3,2,0,1:T(8,128)(2,1)S(1)}, bf16[2,2,128,128]{3,2,0,1:T(8,128)(2,1)S(1)}, u32[]{:S(2)}, u32[]{:S(2)}) %collective-permute-start.24) | collective-permute-done | bytes 131104 | tf_op jit(solution)/shard_map/ppermute | solution.py:22
  86.5 3.0 %collective-permute-done.21 = bf16[2,2,128,128]{3,2,1,0:T(8,128)(2,1)S(1)} collective-permute-done((bf16[2,2,128,128]{3,2,1,0:T(8,128)(2,1)S(1)}, bf16[2,2,128,128]{3,2,1,0:T(8,128)(2,1)S(1)}, u32[]{:S(2)}, u32[]{:S(2)}) %collective-permute-start.21) | collective-permute-done | bytes 131104 | tf_op jit(solution)/shard_map/ppermute | solution.py:22
  89.5 1.9 %collective-permute-done.22 = bf16[2,2,128,128]{3,2,1,0:T(8,128)(2,1)S(1)} collective-permute-done((bf16[2,2,128,128]{3,2,1,0:T(8,128)(2,1)S(1)}, bf16[2,2,128,128]{3,2,1,0:T(8,128)(2,1)S(1)}, u32[]{:S(2)}, u32[]{:S(2)}) %collective-permute-start.22) | collective-permute-done | bytes 131104 | tf_op jit(solution)/shard_map/ppermute | solution.py:22
  (51 shorter events, 9.6 us)
Async XLA Ops:
  1.1 23.5 %collective-permute-start = (bf16[2,5,128,128]{3,2,1,0:T(8,128)(2,1)S(1)}, bf16[2,5,128,128]{3,2,1,0:T(8,128)(2,1)S(1)}, u32[]{:S(2)}, u32[]{:S(2)}) collective-permute-start(bf16[2,5,128,128]{3,2,1,0:T(8,128)(2,1)S(1)} %get-tuple-element.60), channel_id=1, source_target_pairs={{0,16},{1,17},{2,18},{3,19},{4,20},{5,21},{6,22},{7,23},{8,24},{9,... | collective-permute-start | bytes 983048 | tf_op jit(solution)/shard_map/ppermute | solution.py:22
  5.9 7.1 %collective-permute-start.1 = (bf16[2,2,128,128]{3,2,1,0:T(8,128)(2,1)S(1)}, bf16[2,2,128,128]{3,2,1,0:T(8,128)(2,1)S(1)}, u32[]{:S(2)}, u32[]{:S(2)}) collective-permute-start(bf16[2,2,128,128]{3,2,1,0:T(8,128)(2,1)S(1)} %get-tuple-element.66.refs_0_), channel_id=1, source_target_pairs={{0,2},{1,3},{2,0},{3,1},{4,6},{5,7},{6,4},{7,5},{8,10},{9,11},{10,... | collective-permute-start | bytes 393224 | tf_op jit(solution)/shard_map/ppermute | solution.py:22
  7.5 11.9 %collective-permute-start.2 = (bf16[2,2,128,128]{3,2,1,0:T(8,128)(2,1)S(1)}, bf16[2,2,128,128]{3,2,1,0:T(8,128)(2,1)S(1)}, u32[]{:S(2)}, u32[]{:S(2)}) collective-permute-start(bf16[2,2,128,128]{3,2,1,0:T(8,128)(2,1)S(1)} %get-tuple-element.31), channel_id=1, source_target_pairs={{0,3},{1,2},{2,1},{3,0},{4,7},{5,6},{6,5},{7,4},{8,11},{9,10},{10,... | collective-permute-start | bytes 393224 | tf_op jit(solution)/shard_map/ppermute | solution.py:22
  8.9 12.6 %collective-permute-start.4 = (bf16[2,2,128,128]{3,2,1,0:T(8,128)(2,1)S(1)}, bf16[2,2,128,128]{3,2,1,0:T(8,128)(2,1)S(1)}, u32[]{:S(2)}, u32[]{:S(2)}) collective-permute-start(bf16[2,2,128,128]{3,2,1,0:T(8,128)(2,1)S(1)} %get-tuple-element.66.refs_0_), channel_id=1, source_target_pairs={{0,4},{1,5},{2,6},{3,7},{4,0},{5,1},{6,2},{7,3},{8,12},{9,13},{10,... | collective-permute-start | bytes 393224 | tf_op jit(solution)/shard_map/ppermute | solution.py:22
  11.5 11.7 %collective-permute-start.5 = (bf16[2,2,128,128]{3,2,1,0:T(8,128)(2,1)S(1)}, bf16[2,2,128,128]{3,2,1,0:T(8,128)(2,1)S(1)}, u32[]{:S(2)}, u32[]{:S(2)}) collective-permute-start(bf16[2,2,128,128]{3,2,1,0:T(8,128)(2,1)S(1)} %get-tuple-element.31), channel_id=1, source_target_pairs={{0,5},{1,4},{2,7},{3,6},{4,1},{5,0},{6,3},{7,2},{8,13},{9,12},{10,... | collective-permute-start | bytes 393224 | tf_op jit(solution)/shard_map/ppermute | solution.py:22
  19.5 5.2 %collective-permute-start.3 = (bf16[2,2,128,128]{3,2,1,0:T(8,128)(2,1)S(1)}, bf16[2,2,128,128]{3,2,1,0:T(8,128)(2,1)S(1)}, u32[]{:S(2)}, u32[]{:S(2)}) collective-permute-start(bf16[2,2,128,128]{3,2,1,0:T(8,128)(2,1)S(1)} %get-tuple-element.31), channel_id=1, source_target_pairs={{0,1},{1,0},{2,3},{3,2},{4,5},{5,4},{6,7},{7,6},{8,9},{9,8},{10,11... | collective-permute-start | bytes 393224 | tf_op jit(solution)/shard_map/ppermute | solution.py:22
  24.7 7.5 %collective-permute-start.6 = (bf16[2,2,5,128,128]{4,3,2,1,0:T(8,128)(2,1)S(1)}, bf16[2,2,5,128,128]{4,3,2,1,0:T(8,128)(2,1)S(1)}, u32[]{:S(2)}, u32[]{:S(2)}) collective-permute-start(bf16[2,2,5,128,128]{4,3,2,1,0:T(8,128)(2,1)S(1)} %pad_maximum_fusion.1.e), channel_id=1, source_target_pairs={{0,8},{1,9},{2,10},{3,11},{4,12},{5,13},{6,14},{7,15},{8,0},{9,1},... | collective-permute-start | bytes 1966088 | tf_op jit(solution)/shard_map/ppermute | solution.py:22
  24.9 17.1 %collective-permute-start.7 = (bf16[2,2,5,128,128]{4,3,2,1,0:T(8,128)(2,1)S(1)}, bf16[2,2,5,128,128]{4,3,2,1,0:T(8,128)(2,1)S(1)}, u32[]{:S(2)}, u32[]{:S(2)}) collective-permute-start(bf16[2,2,5,128,128]{4,3,2,1,0:T(8,128)(2,1)S(1)} %pad_maximum_fusion.1.e), channel_id=1, source_target_pairs={{0,1},{1,0},{2,3},{3,2},{4,5},{5,4},{6,7},{7,6},{8,9},{9,8},{10,11... | collective-permute-start | bytes 1966088 | tf_op jit(solution)/shard_map/ppermute | solution.py:22
  27.7 19.7 %collective-permute-start.10 = (bf16[3,2,256,256]{3,2,1,0:T(8,128)(2,1)S(1)}, bf16[3,2,256,256]{3,2,1,0:T(8,128)(2,1)S(1)}, u32[]{:S(2)}, u32[]{:S(2)}) collective-permute-start(bf16[3,2,256,256]{3,2,1,0:T(8,128)(2,1)S(1)} %shard_map.38), channel_id=1, source_target_pairs={{0,16},{1,17},{2,18},{3,19},{4,20},{5,21},{6,22},{7,23},{8,24},{9,... | collective-permute-start | bytes 2359304 | tf_op jit(solution)/shard_map/ppermute | solution.py:22
  29.3 19.4 %collective-permute-start.8 = (bf16[2,5,128,128]{3,2,1,0:T(8,128)(2,1)S(1)}, bf16[2,5,128,128]{3,2,1,0:T(8,128)(2,1)S(1)}, u32[]{:S(2)}, u32[]{:S(2)}) collective-permute-start(bf16[2,5,128,128]{3,2,1,0:T(8,128)(2,1)S(1)} %broadcast_select_fusion), channel_id=1, source_target_pairs={{0,4},{1,5},{2,6},{3,7},{4,0},{5,1},{6,2},{7,3},{8,12},{9,13},{10,... | collective-permute-start | bytes 983048 | tf_op jit(solution)/shard_map/ppermute | solution.py:22
  29.4 18.1 %collective-permute-start.9 = (bf16[1,2,256,256]{3,2,1,0:T(8,128)(2,1)S(1)}, bf16[1,2,256,256]{3,2,1,0:T(8,128)(2,1)S(1)}, u32[]{:S(2)}, u32[]{:S(2)}) collective-permute-start(bf16[1,2,256,256]{3,2,1,0:T(8,128)(2,1)S(1)} %shard_map.37), channel_id=1, source_target_pairs={{0,2},{1,3},{2,0},{3,1},{4,6},{5,7},{6,4},{7,5},{8,10},{9,11},{10,... | collective-permute-start | bytes 786440 | tf_op jit(solution)/shard_map/ppermute | solution.py:22
  32.3 20.1 %collective-permute-start.11 = (bf16[2,5,128,128]{3,2,1,0:T(8,128)(2,1)S(1)}, bf16[2,5,128,128]{3,2,1,0:T(8,128)(2,1)S(1)}, u32[]{:S(2)}, u32[]{:S(2)}) collective-permute-start(bf16[2,5,128,128]{3,2,1,0:T(8,128)(2,1)S(1)} %bitcast_select_fusion), channel_id=1, source_target_pairs={{0,6},{1,7},{2,0},{3,1},{4,2},{5,3},{6,4},{7,5},{8,10},{9,11},{10,... | collective-permute-start | bytes 983048 | tf_op jit(solution)/shard_map/ppermute | solution.py:22
  52.4 10.8 %collective-permute-start.15 = (bf16[2,3,2,256,256]{4,3,2,1,0:T(8,128)(2,1)S(1)}, bf16[2,3,2,256,256]{4,3,2,1,0:T(8,128)(2,1)S(1)}, u32[]{:S(2)}, u32[]{:S(2)}) collective-permute-start(bf16[2,3,2,256,256]{4,3,2,1,0:T(8,128)(2,1)S(1)} %pad_maximum_fusion.own), channel_id=1, source_target_pairs={{0,8},{1,9},{2,10},{3,11},{4,12},{5,13},{6,14},{7,15},{8,0},{9,1},... | collective-permute-start | bytes 4718600 | tf_op jit(solution)/shard_map/ppermute | solution.py:22
  52.4 8.7 %collective-permute-start.16 = (bf16[1,2,256,256]{3,2,1,0:T(8,128)(2,1)S(1)}, bf16[1,2,256,256]{3,2,1,0:T(8,128)(2,1)S(1)}, u32[]{:S(2)}, u32[]{:S(2)}) collective-permute-start(bf16[1,2,256,256]{3,2,1,0:T(8,128)(2,1)S(1)} %collective-permute-done.9), channel_id=1, source_target_pairs={{0,16},{1,17},{2,18},{3,19},{4,20},{5,21},{6,22},{7,23},{8,24},{9,... | collective-permute-start | bytes 786440 | tf_op jit(solution)/shard_map/ppermute | solution.py:22
  53.9 7.3 %collective-permute-start.14 = (bf16[2,2,5,128,128]{4,3,2,1,0:T(8,128)(2,1)S(1)}, bf16[2,2,5,128,128]{4,3,2,1,0:T(8,128)(2,1)S(1)}, u32[]{:S(2)}, u32[]{:S(2)}) collective-permute-start(bf16[2,2,5,128,128]{4,3,2,1,0:T(8,128)(2,1)S(1)} %collective-permute-done.7.xe), channel_id=1, source_target_pairs={{0,8},{1,9},{2,10},{3,11},{4,12},{5,13},{6,14},{7,15},{8,0},{9,1},... | collective-permute-start | bytes 1966088 | tf_op jit(solution)/shard_map/ppermute | solution.py:22
  54.2 17.1 %collective-permute-start.13 = (bf16[2,2,5,128,128]{4,3,2,1,0:T(8,128)(2,1)S(1)}, bf16[2,2,5,128,128]{4,3,2,1,0:T(8,128)(2,1)}, u32[]{:S(2)}, u32[]{:S(2)}) collective-permute-start(bf16[2,2,5,128,128]{4,3,2,1,0:T(8,128)(2,1)S(1)} %pad_maximum_fusion.3.far), channel_id=1, source_target_pairs={{0,1},{1,0},{2,3},{3,2},{4,5},{5,4},{6,7},{7,6},{8,9},{9,8},{10,11... | collective-permute-start | bytes 1966088 | tf_op jit(solution)/shard_map/ppermute | solution.py:22
  55.0 16.8 %collective-permute-start.12 = (bf16[2,2,5,128,128]{4,3,2,1,0:T(8,128)(2,1)S(1)}, bf16[2,2,5,128,128]{4,3,2,1,0:T(8,128)(2,1)}, u32[]{:S(2)}, u32[]{:S(2)}) collective-permute-start(bf16[2,2,5,128,128]{4,3,2,1,0:T(8,128)(2,1)S(1)} %pad_maximum_fusion.2), channel_id=1, source_target_pairs={{0,2},{1,3},{2,0},{3,1},{4,6},{5,7},{6,4},{7,5},{8,10},{9,11},{10,... | collective-permute-start | bytes 1966088 | tf_op jit(solution)/shard_map/ppermute | solution.py:22
  61.2 2.0 %collective-permute-start.17 = (bf16[2,1,2,256,256]{4,3,2,1,0:T(8,128)(2,1)S(1)}, bf16[2,1,2,256,256]{4,3,2,1,0:T(8,128)(2,1)S(1)}, u32[]{:S(2)}, u32[]{:S(2)}) collective-permute-start(bf16[2,1,2,256,256]{4,3,2,1,0:T(8,128)(2,1)S(1)} %pad_maximum_fusion.4.own3), channel_id=1, source_target_pairs={{0,8},{1,9},{2,10},{3,11},{4,12},{5,13},{6,14},{7,15},{8,0},{9,1},... | collective-permute-start | bytes 1572872 | tf_op jit(solution)/shard_map/ppermute | solution.py:22
  61.3 14.8 %collective-permute-start.19 = (bf16[2,2,5,128,128]{4,3,2,1,0:T(8,128)(2,1)S(1)}, bf16[2,2,5,128,128]{4,3,2,1,0:T(8,128)(2,1)}, u32[]{:S(2)}, u32[]{:S(2)}) collective-permute-start(bf16[2,2,5,128,128]{4,3,2,1,0:T(8,128)(2,1)S(1)} %pad_maximum_fusion.3.far), channel_id=1, source_target_pairs={{0,8},{1,9},{2,10},{3,11},{4,12},{5,13},{6,14},{7,15},{8,0},{9,1},... | collective-permute-start | bytes 1966088 | tf_op jit(solution)/shard_map/ppermute | solution.py:22
  63.0 7.4 %copy-start = (bf16[4,5,256,256]{3,2,1,0:T(8,128)(2,1)}, bf16[4,5,256,256]{3,2,1,0:T(8,128)(2,1)S(1)}, u32[]{:S(2)}) copy-start(bf16[4,5,256,256]{3,2,1,0:T(8,128)(2,1)S(1)} %get-tuple-element.49.mine) | copy-start | bytes 7864324
  71.9 4.2 %collective-permute-start.18 = (bf16[2,2,5,128,128]{4,3,2,1,0:T(8,128)(2,1)}, bf16[2,2,5,128,128]{4,3,2,1,0:T(8,128)(2,1)}, u32[]{:S(2)}, u32[]{:S(2)}) collective-permute-start(bf16[2,2,5,128,128]{4,3,2,1,0:T(8,128)(2,1)} %collective-permute-done.12.both), channel_id=1, source_target_pairs={{0,8},{1,9},{2,10},{3,11},{4,12},{5,13},{6,14},{7,15},{8,0},{9,1},... | collective-permute-start | bytes 1966088 | tf_op jit(solution)/shard_map/ppermute | solution.py:22
  71.9 4.2 %collective-permute-start.20 = (bf16[2,2,5,128,128]{4,3,2,1,0:T(8,128)(2,1)}, bf16[2,2,5,128,128]{4,3,2,1,0:T(8,128)(2,1)}, u32[]{:S(2)}, u32[]{:S(2)}) collective-permute-start(bf16[2,2,5,128,128]{4,3,2,1,0:T(8,128)(2,1)} %collective-permute-done.13.beside), channel_id=1, source_target_pairs={{0,8},{1,9},{2,10},{3,11},{4,12},{5,13},{6,14},{7,15},{8,0},{9,1},... | collective-permute-start | bytes 1966088 | tf_op jit(solution)/shard_map/ppermute | solution.py:22
  72.4 1.7 %copy-start.1 = (bf16[4,5,256,256]{3,2,1,0:T(8,128)(2,1)S(1)}, bf16[4,5,256,256]{3,2,1,0:T(8,128)(2,1)}, u32[]{:S(2)}) copy-start(bf16[4,5,256,256]{3,2,1,0:T(8,128)(2,1)} %copy-done) | copy-start | bytes 7864324
  80.8 4.6 %collective-permute-start.23 = (bf16[2,2,128,128]{3,2,0,1:T(8,128)(2,1)S(1)}, bf16[2,2,128,128]{3,2,0,1:T(8,128)(2,1)S(1)}, u32[]{:S(2)}, u32[]{:S(2)}) collective-permute-start(bf16[2,2,128,128]{3,2,0,1:T(8,128)(2,1)S(1)} %copy.8), channel_id=1, source_target_pairs={{0,0},{1,1},{2,2},{3,3},{4,4},{5,5},{6,6},{7,7},{8,9},{9,8},{10,11... | collective-permute-start | bytes 393224 | tf_op jit(solution)/shard_map/ppermute | solution.py:22
  81.5 5.0 %collective-permute-start.24 = (bf16[2,2,128,128]{3,2,0,1:T(8,128)(2,1)S(1)}, bf16[2,2,128,128]{3,2,0,1:T(8,128)(2,1)S(1)}, u32[]{:S(2)}, u32[]{:S(2)}) collective-permute-start(bf16[2,2,128,128]{3,2,0,1:T(8,128)(2,1)S(1)} %copy.9), channel_id=1, source_target_pairs={{0,16},{1,17},{2,18},{3,19},{4,20},{5,21},{6,22},{7,23},{8,25},{9,... | collective-permute-start | bytes 393224 | tf_op jit(solution)/shard_map/ppermute | solution.py:22
  82.0 7.5 %collective-permute-start.21 = (bf16[2,2,128,128]{3,2,1,0:T(8,128)(2,1)S(1)}, bf16[2,2,128,128]{3,2,1,0:T(8,128)(2,1)S(1)}, u32[]{:S(2)}, u32[]{:S(2)}) collective-permute-start(bf16[2,2,128,128]{3,2,1,0:T(8,128)(2,1)S(1)} %get-tuple-element.64), channel_id=1, source_target_pairs={{0,8},{1,9},{2,10},{3,11},{4,12},{5,13},{6,14},{7,15},{8,1},{9,0},... | collective-permute-start | bytes 393224 | tf_op jit(solution)/shard_map/ppermute | solution.py:22
  84.1 7.3 %collective-permute-start.22 = (bf16[2,2,128,128]{3,2,1,0:T(8,128)(2,1)S(1)}, bf16[2,2,128,128]{3,2,1,0:T(8,128)(2,1)S(1)}, u32[]{:S(2)}, u32[]{:S(2)}) collective-permute-start(bf16[2,2,128,128]{3,2,1,0:T(8,128)(2,1)S(1)} %get-tuple-element.63), channel_id=1, source_target_pairs={{0,24},{1,25},{2,26},{3,27},{4,28},{5,29},{6,30},{7,31},{8,17},{9,... | collective-permute-start | bytes 393224 | tf_op jit(solution)/shard_map/ppermute | solution.py:22

commit v4 on v3

--- a/solution.py
+++ b/solution.py
@@ -137,7 +137,7 @@
         for rr in range(2):
             for p in range(2):
                 tile = total[w, pl.ds(p * 128, 128), pl.ds(rr * 128, 128)]
-                out[w, rr, p] = tile.T.astype(jnp.bfloat16)
+                out[w, rr, p] = tile.astype(jnp.bfloat16).T
 
 
 def by_parity(g, half, even, odd):
@@ -171,14 +171,15 @@
     straight = jnp.stack([masked[:, 0], masked[:, 3]], axis=1)
     own_pairs = jnp.where(x == 0, crossed, straight)
     other_pairs = jnp.where(x == 0, straight, crossed)
-    factors = cholesky[:, 0]
+    factors, own_pairs, other_pairs = lax.optimization_barrier((cholesky, own_pairs, other_pairs))
+    factors = factors[:, 0]
     kept = lax.dynamic_slice_in_dim(factors, y * vectors, vectors, 1)
     given = lax.dynamic_slice_in_dim(factors, (1 - y) * vectors, vectors, 1)
     taken = swap_y(given)
-    near = [move(own_pairs, lambda r, z, x: (r, z ^ 1, x)), move(other_pairs, lambda r, z, x: (r, z ^ 1, x ^ 1))]
     away = [move(own_pairs, lambda r, z, x: (r, z ^ 2, x)), move(other_pairs, lambda r, z, x: (r, z ^ 2, x ^ 1))]
-    *near, others = lax.optimization_barrier((*near, other_pairs))
-    side = swap_x(others)
+    side = swap_x(other_pairs)
+    side, own_again, other_again = lax.optimization_barrier((side, own_pairs, other_pairs))
+    near = [move(own_again, lambda r, z, x: (r, z ^ 1, x)), move(other_again, lambda r, z, x: (r, z ^ 1, x ^ 1))]
     taken, side, near, away = lax.optimization_barrier((taken, side, near, away))
 
     e = jnp.stack([kept, taken])
@@ -212,6 +213,7 @@
         info, e, ce, xe, cxe,
     )
     far_other = swap_core(far)
+    across3, rows, mine = lax.optimization_barrier((across3, rows, mine))
     near3 = jnp.stack([block3, across3])
     halves, info = pl.pallas_call(
         halves_kernel,

time: 92.6 us -> 90 us (0.972)
  waiting for transfers between devices: 43.1 us -> 37 us
  starting transfers between devices: 25.6 us -> 29.4 us
    ppermute x25, waiting for transfers between devices: 43.1 us -> 37 us  [move(): return lax.ppermute(value, ('row', 'col'), pairs)]
    ppermute x25, starting transfers between devices: 25.6 us -> 29.4 us  [move(): return lax.ppermute(value, ('row', 'col'), pairs)]
    unnamed x4 -> x14, local copies, waits for them, and re-layouts: 1.74 us -> 3.23 us
    another operation x1, local copies, waits for them, and re-layouts: 1.12 us -> 0.06 us  [fast_body(): e = jnp.stack([kept, taken])]
    another operation x2, other arithmetic: 1.08 us -> 0.11 us  [fast_body(): piece = jnp.stack([jnp.where(n, kept, taken), jnp.where(n, xe[0], xe[1])])]
  transfers between devices with their start and end apart: 25 -> 25, of which waited for: 16 -> 12; matrix products, arithmetic and copies ran while one was open for 4% -> 1% of each run, Pallas kernels for 13% -> 13%
where the time goes in v4:
time: 90 us; the launch traced here: 89.8 us
  waiting for transfers between devices  37 us (41%)
  starting transfers between devices  29.4 us (33%)
  Pallas kernels  16.3 us (18%)
  local copies, waits for them, and re-layouts  3.4 us (4%)
  other arithmetic  3.3 us (4%)
    ppermute x25, waiting for transfers between devices, move(): return lax.ppermute(value, ('row', 'col'), pairs)  37 us
    ppermute x25, starting transfers between devices, move(): return lax.ppermute(value, ('row', 'col'), pairs)  29.4 us
    pallas_call x1, Pallas kernels, fast_body(): pl.pallas_call(halves_kernel, out_shape=(jax.ShapeDtypeStruct((PLANES, ve...  7.24 us
    pallas_call x1, Pallas kernels, fast_body(): pl.pallas_call(ladder_far_kernel, out_shape=jax.ShapeDtypeStruct((PLANES,...  4.61 us
    unnamed x14, local copies, waits for them, and re-layouts  3.23 us
    pallas_call x3, Pallas kernels, small_call(): pl.pallas_call(kernel, out_shape=out_shape, in_specs=specs, out_specs=jax...  2.51 us
    pallas_call x1, Pallas kernels, fast_body(): pl.pallas_call(ladder_own_kernel, out_shape=jax.ShapeDtypeStruct((PLANES,...  1.92 us
  transfers between devices with their start and end apart: 25, of which 12 were waited for; matrix products, arithmetic and copies ran while one was open for 1% of the time, Pallas kernels for 13%

profile of v4, /device:TPU:0, one launch (start us, length us, event | category | flops | bytes accessed | tf_op | source)
XLA Modules:
  0.0 89.8 jit_solution(1794844187897254739)
XLA Ops:
  0.0 0.7 convert_bitcast_fusion
  0.7 1.0 %fusion = bf16[2,4,128,128]{3,2,1,0:T(8,128)(2,1)S(1)} fusion(bf16[2,1,4,128,128]{4,3,2,1,0:T(8,128)(2,1)} %param.3, bf16[2]{0:T(256)(128)(2,1)S(1)} %convert_bitcast_fusion), kind=kLoop, calls=%fused_computation.14 | loop fusion | flops 131072 | bytes 524292 | tf_op jit(solution)/shard_map/squeeze | solution.py:169
  1.9 3.0 %collective-permute-start = (bf16[2,5,128,128]{3,2,1,0:T(8,128)(2,1)S(1)}, bf16[2,5,128,128]{3,2,1,0:T(8,128)(2,1)S(1)}, u32[]{:S(2)}, u32[]{:S(2)}) collective-permute-start(bf16[2,5,128,128]{3,2,1,0:T(8,128)(2,1)S(1)} %get-tuple-element.72), channel_id=1, source_target_pairs={{0,16},{1,17},{2,18},{3,19},{4,20},{5,21},{6,22},{7,23},{8,24},{9,... | collective-permute-start | bytes 983048 | tf_op jit(solution)/shard_map/ppermute | solution.py:22
  4.9 1.5 %collective-permute-start.1 = (bf16[2,2,128,128]{3,2,1,0:T(8,128)(2,1)S(1)}, bf16[2,2,128,128]{3,2,1,0:T(8,128)(2,1)S(1)}, u32[]{:S(2)}, u32[]{:S(2)}) collective-permute-start(bf16[2,2,128,128]{3,2,1,0:T(8,128)(2,1)S(1)} %get-tuple-element.42), channel_id=1, source_target_pairs={{0,1},{1,0},{2,3},{3,2},{4,5},{5,4},{6,7},{7,6},{8,9},{9,8},{10,11... | collective-permute-start | bytes 393224 | tf_op jit(solution)/shard_map/ppermute | solution.py:22
  6.4 2.6 %collective-permute-start.5 = (bf16[2,2,128,128]{3,2,1,0:T(8,128)(2,1)S(1)}, bf16[2,2,128,128]{3,2,1,0:T(8,128)(2,1)S(1)}, u32[]{:S(2)}, u32[]{:S(2)}) collective-permute-start(bf16[2,2,128,128]{3,2,1,0:T(8,128)(2,1)S(1)} %get-tuple-element.42), channel_id=1, source_target_pairs={{0,5},{1,4},{2,7},{3,6},{4,1},{5,0},{6,3},{7,2},{8,13},{9,12},{10,... | collective-permute-start | bytes 393224 | tf_op jit(solution)/shard_map/ppermute | solution.py:22
  9.3 0.7 collective-permute-done.1.refs_1_
  10.0 2.8 %collective-permute-start.2 = (bf16[2,2,128,128]{3,2,1,0:T(8,128)(2,1)S(1)}, bf16[2,2,128,128]{3,2,1,0:T(8,128)(2,1)S(1)}, u32[]{:S(2)}, u32[]{:S(2)}) collective-permute-start(bf16[2,2,128,128]{3,2,1,0:T(8,128)(2,1)S(1)} %get-tuple-element.41.refs_0_), channel_id=1, source_target_pairs={{0,2},{1,3},{2,0},{3,1},{4,6},{5,7},{6,4},{7,5},{8,10},{9,11},{10,... | collective-permute-start | bytes 393224 | tf_op jit(solution)/shard_map/ppermute | solution.py:22
  12.8 2.1 %collective-permute-start.3 = (bf16[2,2,128,128]{3,2,1,0:T(8,128)(2,1)S(1)}, bf16[2,2,128,128]{3,2,1,0:T(8,128)(2,1)S(1)}, u32[]{:S(2)}, u32[]{:S(2)}) collective-permute-start(bf16[2,2,128,128]{3,2,1,0:T(8,128)(2,1)S(1)} %get-tuple-element.42), channel_id=1, source_target_pairs={{0,3},{1,2},{2,1},{3,0},{4,7},{5,6},{6,5},{7,4},{8,11},{9,10},{10,... | collective-permute-start | bytes 393224 | tf_op jit(solution)/shard_map/ppermute | solution.py:22
  14.8 5.7 %collective-permute-done.4.refs_0_.refs_4_ = bf16[2,2,128,128]{3,2,1,0:T(8,128)(2,1)S(1)} collective-permute-done((bf16[2,2,128,128]{3,2,1,0:T(8,128)(2,1)S(1)}, bf16[2,2,128,128]{3,2,1,0:T(8,128)(2,1)S(1)}, u32[]{:S(2)}, u32[]{:S(2)}) %collective-permute-start.4) | collective-permute-done | bytes 131104 | tf_op jit(solution)/shard_map/ppermute | solution.py:22
  20.5 2.6 %collective-permute-done.3.refs_3_ = bf16[2,2,128,128]{3,2,1,0:T(8,128)(2,1)S(1)} collective-permute-done((bf16[2,2,128,128]{3,2,1,0:T(8,128)(2,1)S(1)}, bf16[2,2,128,128]{3,2,1,0:T(8,128)(2,1)S(1)}, u32[]{:S(2)}, u32[]{:S(2)}) %collective-permute-start.3) | collective-permute-done | bytes 131104 | tf_op jit(solution)/shard_map/ppermute | solution.py:22
  25.6 2.2 %collective-permute-start.8 = (bf16[2,5,128,128]{3,2,1,0:T(8,128)(2,1)S(1)}, bf16[2,5,128,128]{3,2,1,0:T(8,128)(2,1)S(1)}, u32[]{:S(2)}, u32[]{:S(2)}) collective-permute-start(bf16[2,5,128,128]{3,2,1,0:T(8,128)(2,1)S(1)} %broadcast_select_fusion), channel_id=1, source_target_pairs={{0,4},{1,5},{2,6},{3,7},{4,0},{5,1},{6,2},{7,3},{8,12},{9,13},{10,... | collective-permute-start | bytes 983048 | tf_op jit(solution)/shard_map/ppermute | solution.py:22
  27.8 2.5 %collective-permute-start.9 = (bf16[1,2,256,256]{3,2,1,0:T(8,128)(2,1)S(1)}, bf16[1,2,256,256]{3,2,1,0:T(8,128)(2,1)S(1)}, u32[]{:S(2)}, u32[]{:S(2)}) collective-permute-start(bf16[1,2,256,256]{3,2,1,0:T(8,128)(2,1)S(1)} %shard_map.37), channel_id=1, source_target_pairs={{0,2},{1,3},{2,0},{3,1},{4,6},{5,7},{6,4},{7,5},{8,10},{9,11},{10,... | collective-permute-start | bytes 786440 | tf_op jit(solution)/shard_map/ppermute | solution.py:22
  30.4 10.2 %collective-permute-done.7.xe = bf16[2,2,5,128,128]{4,3,2,1,0:T(8,128)(2,1)S(1)} collective-permute-done((bf16[2,2,5,128,128]{4,3,2,1,0:T(8,128)(2,1)S(1)}, bf16[2,2,5,128,128]{4,3,2,1,0:T(8,128)(2,1)S(1)}, u32[]{:S(2)}, u32[]{:S(2)}) %collective-permute-start.7) | collective-permute-done | bytes 655392 | tf_op jit(solution)/shard_map/ppermute | solution.py:22
  40.7 4.1 %collective-permute-done.10 = bf16[3,2,256,256]{3,2,1,0:T(8,128)(2,1)S(1)} collective-permute-done((bf16[3,2,256,256]{3,2,1,0:T(8,128)(2,1)S(1)}, bf16[3,2,256,256]{3,2,1,0:T(8,128)(2,1)S(1)}, u32[]{:S(2)}, u32[]{:S(2)}) %collective-permute-start.10) | collective-permute-done | bytes 786464 | tf_op jit(solution)/shard_map/ppermute | solution.py:22
  44.9 3.7 %collective-permute-done.11 = bf16[2,5,128,128]{3,2,1,0:T(8,128)(2,1)S(1)} collective-permute-done((bf16[2,5,128,128]{3,2,1,0:T(8,128)(2,1)S(1)}, bf16[2,5,128,128]{3,2,1,0:T(8,128)(2,1)S(1)}, u32[]{:S(2)}, u32[]{:S(2)}) %collective-permute-start.11) | collective-permute-done | bytes 327712 | tf_op jit(solution)/shard_map/ppermute | solution.py:22
  49.2 1.5 %collective-permute-start.14 = (bf16[1,2,256,256]{3,2,1,0:T(8,128)(2,1)S(1)}, bf16[1,2,256,256]{3,2,1,0:T(8,128)(2,1)S(1)}, u32[]{:S(2)}, u32[]{:S(2)}) collective-permute-start(bf16[1,2,256,256]{3,2,1,0:T(8,128)(2,1)S(1)} %collective-permute-done.9), channel_id=1, source_target_pairs={{0,16},{1,17},{2,18},{3,19},{4,20},{5,21},{6,22},{7,23},{8,24},{9,... | collective-permute-start | bytes 786440 | tf_op jit(solution)/shard_map/ppermute | solution.py:22
  50.8 1.9 %collective-permute-start.13 = (bf16[2,2,5,128,128]{4,3,2,1,0:T(8,128)(2,1)S(1)}, bf16[2,2,5,128,128]{4,3,2,1,0:T(8,128)(2,1)}, u32[]{:S(2)}, u32[]{:S(2)}) collective-permute-start(bf16[2,2,5,128,128]{4,3,2,1,0:T(8,128)(2,1)S(1)} %pad_maximum_fusion.3.far), channel_id=1, source_target_pairs={{0,1},{1,0},{2,3},{3,2},{4,5},{5,4},{6,7},{7,6},{8,9},{9,8},{10,11... | collective-permute-start | bytes 1966088 | tf_op jit(solution)/shard_map/ppermute | solution.py:22
  52.8 2.0 %collective-permute-start.12 = (bf16[2,2,5,128,128]{4,3,2,1,0:T(8,128)(2,1)S(1)}, bf16[2,2,5,128,128]{4,3,2,1,0:T(8,128)(2,1)}, u32[]{:S(2)}, u32[]{:S(2)}) collective-permute-start(bf16[2,2,5,128,128]{4,3,2,1,0:T(8,128)(2,1)S(1)} %pad_maximum_fusion.2), channel_id=1, source_target_pairs={{0,2},{1,3},{2,0},{3,1},{4,6},{5,7},{6,4},{7,5},{8,10},{9,11},{10,... | collective-permute-start | bytes 1966088 | tf_op jit(solution)/shard_map/ppermute | solution.py:22
  54.8 1.2 %shard_map.39 = (bf16[4,640,256]{2,1,0:T(8,128)(2,1)S(1)}, bf16[4,5,256,256]{3,2,1,0:T(8,128)(2,1)S(1)}) custom-call(s32[4]{0:T(128)S(1)} %pad_add_fusion.info, bf16[2,2,5,128,128]{4,3,2,1,0:T(8,128)(2,1)S(1)} %copy-done.3, bf16[2,2,5,128,128]{4,3,2,1,0:T(8,128)(2,1)S(1)} %copy-done.5, bf16[2,2,5,128,128]{4,3,2,1,0:T(8,128)(2,1)S(1)} %collective-permute-done.7.xe, ...), custom_call_target="tpu_custom_call" | custom-call | flops 1024 | bytes 1024 | tf_op jit(solution)/shard_map/pallas_call | solution.py:153
  56.0 2.0 %collective-permute-done.14 = bf16[1,2,256,256]{3,2,1,0:T(8,128)(2,1)S(1)} collective-permute-done((bf16[1,2,256,256]{3,2,1,0:T(8,128)(2,1)S(1)}, bf16[1,2,256,256]{3,2,1,0:T(8,128)(2,1)S(1)}, u32[]{:S(2)}, u32[]{:S(2)}) %collective-permute-start.14) | collective-permute-done | bytes 262176 | tf_op jit(solution)/shard_map/ppermute | solution.py:22
  58.6 1.4 %collective-permute-done.17.other3 = bf16[2,1,2,256,256]{4,3,2,1,0:T(8,128)(2,1)S(1)} collective-permute-done((bf16[2,1,2,256,256]{4,3,2,1,0:T(8,128)(2,1)S(1)}, bf16[2,1,2,256,256]{4,3,2,1,0:T(8,128)(2,1)S(1)}, u32[]{:S(2)}, u32[]{:S(2)}) %collective-permute-start.17) | collective-permute-done | bytes 524320 | tf_op jit(solution)/shard_map/ppermute | solution.py:22
  60.0 7.2 %shard_map.40 = (bf16[4,5,256,256]{3,2,1,0:T(8,128)(2,1)S(1)}, s32[4]{0:T(128)S(1)}) custom-call(s32[4]{0:T(128)S(1)} %pad_add_fusion.info, bf16[4,640,256]{2,1,0:T(8,128)(2,1)S(1)} %get-tuple-element.60.rows, bf16[4,5,256,256]{3,2,1,0:T(8,128)(2,1)S(1)} %get-tuple-element.61.mine, bf16[2,3,2,256,256]{4,3,2,1,0:T(8,128)(2,1)S(1)} %pad_maximum_fusion.own, ...), custom_call_target="tpu_custom_call" | custom-call | flops 1024 | bytes 1024 | tf_op jit(solution)/shard_map/pallas_call | solution.py:218
  67.2 1.5 %copy-done = bf16[4,5,256,256]{3,2,1,0:T(8,128)(2,1)} copy-done((bf16[4,5,256,256]{3,2,1,0:T(8,128)(2,1)}, bf16[4,5,256,256]{3,2,1,0:T(8,128)(2,1)S(1)}, u32[]{:S(2)}) %copy-start) | copy-done | bytes 2621464
  69.7 1.7 %copy-done.1 = bf16[4,5,256,256]{3,2,1,0:T(8,128)(2,1)S(1)} copy-done((bf16[4,5,256,256]{3,2,1,0:T(8,128)(2,1)S(1)}, bf16[4,5,256,256]{3,2,1,0:T(8,128)(2,1)}, u32[]{:S(2)}) %copy-start.1) | copy-done | bytes 2621464
  71.4 1.9 %shard_map.41.held = f32[4,256,256]{2,1,0:T(8,128)S(1)} custom-call(s32[4]{0:T(128)S(1)} %get-tuple-element.65.info, bf16[4,5,256,256]{3,2,1,0:T(8,128)(2,1)S(1)} %copy-done.1, bf16[4,5,256,256]{3,2,1,0:T(8,128)(2,1)S(1)} %get-tuple-element.61.mine), custom_call_target="tpu_custom_call" | custom-call | flops 1024 | bytes 1024 | tf_op jit(solution)/shard_map/pallas_call | solution.py:232
  73.4 4.6 %shard_map.42 = bf16[4,2,2,128,128]{4,3,2,1,0:T(8,128)(2,1)S(1)} custom-call(s32[4]{0:T(128)S(1)} %get-tuple-element.65.info, bf16[4,5,256,256]{3,2,1,0:T(8,128)(2,1)S(1)} %copy-done.1, f32[4,256,256]{2,1,0:T(8,128)S(1)} %shard_map.41.held, bf16[2,2,5,128,128]{4,3,2,1,0:T(8,128)(2,1)} %collective-permute-done.12.both, ...), custom_call_target="tpu_custom_call" | custom-call | flops 1024 | bytes 1024 | tf_op jit(solution)/shard_map/pallas_call | solution.py:240
  78.8 1.1 %collective-permute-start.24 = (bf16[2,2,128,128]{3,2,0,1:T(8,128)(2,1)S(1)}, bf16[2,2,128,128]{3,2,0,1:T(8,128)(2,1)S(1)}, u32[]{:S(2)}, u32[]{:S(2)}) collective-permute-start(bf16[2,2,128,128]{3,2,0,1:T(8,128)(2,1)S(1)} %copy.9), channel_id=1, source_target_pairs={{0,16},{1,17},{2,18},{3,19},{4,20},{5,21},{6,22},{7,23},{8,25},{9,... | collective-permute-start | bytes 393224 | tf_op jit(solution)/shard_map/ppermute | solution.py:22
  79.9 2.3 %collective-permute-start.21 = (bf16[2,2,128,128]{3,2,1,0:T(8,128)(2,1)S(1)}, bf16[2,2,128,128]{3,2,1,0:T(8,128)(2,1)S(1)}, u32[]{:S(2)}, u32[]{:S(2)}) collective-permute-start(bf16[2,2,128,128]{3,2,1,0:T(8,128)(2,1)S(1)} %get-tuple-element.76), channel_id=1, source_target_pairs={{0,8},{1,9},{2,10},{3,11},{4,12},{5,13},{6,14},{7,15},{8,1},{9,0},... | collective-permute-start | bytes 393224 | tf_op jit(solution)/shard_map/ppermute | solution.py:22
  82.6 1.2 %collective-permute-done.24 = bf16[2,2,128,128]{3,2,0,1:T(8,128)(2,1)S(1)} collective-permute-done((bf16[2,2,128,128]{3,2,0,1:T(8,128)(2,1)S(1)}, bf16[2,2,128,128]{3,2,0,1:T(8,128)(2,1)S(1)}, u32[]{:S(2)}, u32[]{:S(2)}) %collective-permute-start.24) | collective-permute-done | bytes 131104 | tf_op jit(solution)/shard_map/ppermute | solution.py:22
  83.8 3.5 %collective-permute-done.21 = bf16[2,2,128,128]{3,2,1,0:T(8,128)(2,1)S(1)} collective-permute-done((bf16[2,2,128,128]{3,2,1,0:T(8,128)(2,1)S(1)}, bf16[2,2,128,128]{3,2,1,0:T(8,128)(2,1)S(1)}, u32[]{:S(2)}, u32[]{:S(2)}) %collective-permute-start.21) | collective-permute-done | bytes 131104 | tf_op jit(solution)/shard_map/ppermute | solution.py:22
  87.3 1.5 %collective-permute-done.22 = bf16[2,2,128,128]{3,2,1,0:T(8,128)(2,1)S(1)} collective-permute-done((bf16[2,2,128,128]{3,2,1,0:T(8,128)(2,1)S(1)}, bf16[2,2,128,128]{3,2,1,0:T(8,128)(2,1)S(1)}, u32[]{:S(2)}, u32[]{:S(2)}) %collective-permute-start.22) | collective-permute-done | bytes 131104 | tf_op jit(solution)/shard_map/ppermute | solution.py:22
  89.0 0.7 maximum_bitcast_fusion
  (61 shorter events, 6.8 us)
Async XLA Ops:
  0.0 1.8 %copy-start.6 = (bf16[2,1,10,128,128]{4,3,2,1,0:T(8,128)(2,1)S(1)}, bf16[2,1,10,128,128]{4,3,2,1,0:T(8,128)(2,1)}, u32[]{:S(2)}) copy-start(bf16[2,1,10,128,128]{4,3,2,1,0:T(8,128)(2,1)} %param.4) | copy-start | bytes 1966084
  1.9 21.3 %collective-permute-start = (bf16[2,5,128,128]{3,2,1,0:T(8,128)(2,1)S(1)}, bf16[2,5,128,128]{3,2,1,0:T(8,128)(2,1)S(1)}, u32[]{:S(2)}, u32[]{:S(2)}) collective-permute-start(bf16[2,5,128,128]{3,2,1,0:T(8,128)(2,1)S(1)} %get-tuple-element.72), channel_id=1, source_target_pairs={{0,16},{1,17},{2,18},{3,19},{4,20},{5,21},{6,22},{7,23},{8,24},{9,... | collective-permute-start | bytes 983048 | tf_op jit(solution)/shard_map/ppermute | solution.py:22
  4.9 5.1 %collective-permute-start.1 = (bf16[2,2,128,128]{3,2,1,0:T(8,128)(2,1)S(1)}, bf16[2,2,128,128]{3,2,1,0:T(8,128)(2,1)S(1)}, u32[]{:S(2)}, u32[]{:S(2)}) collective-permute-start(bf16[2,2,128,128]{3,2,1,0:T(8,128)(2,1)S(1)} %get-tuple-element.42), channel_id=1, source_target_pairs={{0,1},{1,0},{2,3},{3,2},{4,5},{5,4},{6,7},{7,6},{8,9},{9,8},{10,11... | collective-permute-start | bytes 393224 | tf_op jit(solution)/shard_map/ppermute | solution.py:22
  6.4 14.1 %collective-permute-start.5 = (bf16[2,2,128,128]{3,2,1,0:T(8,128)(2,1)S(1)}, bf16[2,2,128,128]{3,2,1,0:T(8,128)(2,1)S(1)}, u32[]{:S(2)}, u32[]{:S(2)}) collective-permute-start(bf16[2,2,128,128]{3,2,1,0:T(8,128)(2,1)S(1)} %get-tuple-element.42), channel_id=1, source_target_pairs={{0,5},{1,4},{2,7},{3,6},{4,1},{5,0},{6,3},{7,2},{8,13},{9,12},{10,... | collective-permute-start | bytes 393224 | tf_op jit(solution)/shard_map/ppermute | solution.py:22
  9.0 11.5 %collective-permute-start.4 = (bf16[2,2,128,128]{3,2,1,0:T(8,128)(2,1)S(1)}, bf16[2,2,128,128]{3,2,1,0:T(8,128)(2,1)S(1)}, u32[]{:S(2)}, u32[]{:S(2)}) collective-permute-start(bf16[2,2,128,128]{3,2,1,0:T(8,128)(2,1)S(1)} %get-tuple-element.41.refs_0_), channel_id=1, source_target_pairs={{0,4},{1,5},{2,6},{3,7},{4,0},{5,1},{6,2},{7,3},{8,12},{9,13},{10,... | collective-permute-start | bytes 393224 | tf_op jit(solution)/shard_map/ppermute | solution.py:22
  10.0 10.5 %collective-permute-start.2 = (bf16[2,2,128,128]{3,2,1,0:T(8,128)(2,1)S(1)}, bf16[2,2,128,128]{3,2,1,0:T(8,128)(2,1)S(1)}, u32[]{:S(2)}, u32[]{:S(2)}) collective-permute-start(bf16[2,2,128,128]{3,2,1,0:T(8,128)(2,1)S(1)} %get-tuple-element.41.refs_0_), channel_id=1, source_target_pairs={{0,2},{1,3},{2,0},{3,1},{4,6},{5,7},{6,4},{7,5},{8,10},{9,11},{10,... | collective-permute-start | bytes 393224 | tf_op jit(solution)/shard_map/ppermute | solution.py:22
  12.8 10.4 %collective-permute-start.3 = (bf16[2,2,128,128]{3,2,1,0:T(8,128)(2,1)S(1)}, bf16[2,2,128,128]{3,2,1,0:T(8,128)(2,1)S(1)}, u32[]{:S(2)}, u32[]{:S(2)}) collective-permute-start(bf16[2,2,128,128]{3,2,1,0:T(8,128)(2,1)S(1)} %get-tuple-element.42), channel_id=1, source_target_pairs={{0,3},{1,2},{2,1},{3,0},{4,7},{5,6},{6,5},{7,4},{8,11},{9,10},{10,... | collective-permute-start | bytes 393224 | tf_op jit(solution)/shard_map/ppermute | solution.py:22
  23.3 2.3 %copy-start.2 = (bf16[2,2,5,128,128]{4,3,2,1,0:T(8,128)(2,1)}, bf16[2,2,5,128,128]{4,3,2,1,0:T(8,128)(2,1)S(1)}, u32[]{:S(2)}) copy-start(bf16[2,2,5,128,128]{4,3,2,1,0:T(8,128)(2,1)S(1)} %pad_maximum_fusion.1.e) | copy-start | bytes 1966084
  23.3 7.0 %collective-permute-start.6 = (bf16[2,2,5,128,128]{4,3,2,1,0:T(8,128)(2,1)S(1)}, bf16[2,2,5,128,128]{4,3,2,1,0:T(8,128)(2,1)S(1)}, u32[]{:S(2)}, u32[]{:S(2)}) collective-permute-start(bf16[2,2,5,128,128]{4,3,2,1,0:T(8,128)(2,1)S(1)} %pad_maximum_fusion.1.e), channel_id=1, source_target_pairs={{0,8},{1,9},{2,10},{3,11},{4,12},{5,13},{6,14},{7,15},{8,0},{9,1},... | collective-permute-start | bytes 1966088 | tf_op jit(solution)/shard_map/ppermute | solution.py:22
  23.4 17.1 %collective-permute-start.7 = (bf16[2,2,5,128,128]{4,3,2,1,0:T(8,128)(2,1)S(1)}, bf16[2,2,5,128,128]{4,3,2,1,0:T(8,128)(2,1)S(1)}, u32[]{:S(2)}, u32[]{:S(2)}) collective-permute-start(bf16[2,2,5,128,128]{4,3,2,1,0:T(8,128)(2,1)S(1)} %pad_maximum_fusion.1.e), channel_id=1, source_target_pairs={{0,1},{1,0},{2,3},{3,2},{4,5},{5,4},{6,7},{7,6},{8,9},{9,8},{10,11... | collective-permute-start | bytes 1966088 | tf_op jit(solution)/shard_map/ppermute | solution.py:22
  25.0 19.8 %collective-permute-start.10 = (bf16[3,2,256,256]{3,2,1,0:T(8,128)(2,1)S(1)}, bf16[3,2,256,256]{3,2,1,0:T(8,128)(2,1)S(1)}, u32[]{:S(2)}, u32[]{:S(2)}) collective-permute-start(bf16[3,2,256,256]{3,2,1,0:T(8,128)(2,1)S(1)} %shard_map.38), channel_id=1, source_target_pairs={{0,16},{1,17},{2,18},{3,19},{4,20},{5,21},{6,22},{7,23},{8,24},{9,... | collective-permute-start | bytes 2359304 | tf_op jit(solution)/shard_map/ppermute | solution.py:22
  25.6 19.3 %collective-permute-start.8 = (bf16[2,5,128,128]{3,2,1,0:T(8,128)(2,1)S(1)}, bf16[2,5,128,128]{3,2,1,0:T(8,128)(2,1)S(1)}, u32[]{:S(2)}, u32[]{:S(2)}) collective-permute-start(bf16[2,5,128,128]{3,2,1,0:T(8,128)(2,1)S(1)} %broadcast_select_fusion), channel_id=1, source_target_pairs={{0,4},{1,5},{2,6},{3,7},{4,0},{5,1},{6,2},{7,3},{8,12},{9,13},{10,... | collective-permute-start | bytes 983048 | tf_op jit(solution)/shard_map/ppermute | solution.py:22
  27.8 17.1 %collective-permute-start.9 = (bf16[1,2,256,256]{3,2,1,0:T(8,128)(2,1)S(1)}, bf16[1,2,256,256]{3,2,1,0:T(8,128)(2,1)S(1)}, u32[]{:S(2)}, u32[]{:S(2)}) collective-permute-start(bf16[1,2,256,256]{3,2,1,0:T(8,128)(2,1)S(1)} %shard_map.37), channel_id=1, source_target_pairs={{0,2},{1,3},{2,0},{3,1},{4,6},{5,7},{6,4},{7,5},{8,10},{9,11},{10,... | collective-permute-start | bytes 786440 | tf_op jit(solution)/shard_map/ppermute | solution.py:22
  30.3 10.4 %copy-start.4 = (bf16[2,2,5,128,128]{4,3,2,1,0:T(8,128)(2,1)}, bf16[2,2,5,128,128]{4,3,2,1,0:T(8,128)(2,1)S(1)}, u32[]{:S(2)}) copy-start(bf16[2,2,5,128,128]{4,3,2,1,0:T(8,128)(2,1)S(1)} %collective-permute-done.6.ce) | copy-start | bytes 1966084
  30.3 18.3 %collective-permute-start.11 = (bf16[2,5,128,128]{3,2,1,0:T(8,128)(2,1)S(1)}, bf16[2,5,128,128]{3,2,1,0:T(8,128)(2,1)S(1)}, u32[]{:S(2)}, u32[]{:S(2)}) collective-permute-start(bf16[2,5,128,128]{3,2,1,0:T(8,128)(2,1)S(1)} %bitcast_select_fusion), channel_id=1, source_target_pairs={{0,6},{1,7},{2,0},{3,1},{4,2},{5,3},{6,4},{7,5},{8,10},{9,11},{10,... | collective-permute-start | bytes 983048 | tf_op jit(solution)/shard_map/ppermute | solution.py:22
  44.7 10.0 %copy-start.3 = (bf16[2,2,5,128,128]{4,3,2,1,0:T(8,128)(2,1)S(1)}, bf16[2,2,5,128,128]{4,3,2,1,0:T(8,128)(2,1)}, u32[]{:S(2)}) copy-start(bf16[2,2,5,128,128]{4,3,2,1,0:T(8,128)(2,1)} %copy-done.2) | copy-start | bytes 1966084
  44.7 10.0 %copy-start.5 = (bf16[2,2,5,128,128]{4,3,2,1,0:T(8,128)(2,1)S(1)}, bf16[2,2,5,128,128]{4,3,2,1,0:T(8,128)(2,1)}, u32[]{:S(2)}) copy-start(bf16[2,2,5,128,128]{4,3,2,1,0:T(8,128)(2,1)} %copy-done.4) | copy-start | bytes 1966084
  48.6 11.4 %collective-permute-start.16 = (bf16[2,3,2,256,256]{4,3,2,1,0:T(8,128)(2,1)S(1)}, bf16[2,3,2,256,256]{4,3,2,1,0:T(8,128)(2,1)S(1)}, u32[]{:S(2)}, u32[]{:S(2)}) collective-permute-start(bf16[2,3,2,256,256]{4,3,2,1,0:T(8,128)(2,1)S(1)} %pad_maximum_fusion.own), channel_id=1, source_target_pairs={{0,8},{1,9},{2,10},{3,11},{4,12},{5,13},{6,14},{7,15},{8,0},{9,1},... | collective-permute-start | bytes 4718600 | tf_op jit(solution)/shard_map/ppermute | solution.py:22
  49.2 5.5 %collective-permute-start.15 = (bf16[2,2,5,128,128]{4,3,2,1,0:T(8,128)(2,1)S(1)}, bf16[2,2,5,128,128]{4,3,2,1,0:T(8,128)(2,1)S(1)}, u32[]{:S(2)}, u32[]{:S(2)}) collective-permute-start(bf16[2,2,5,128,128]{4,3,2,1,0:T(8,128)(2,1)S(1)} %collective-permute-done.7.xe), channel_id=1, source_target_pairs={{0,8},{1,9},{2,10},{3,11},{4,12},{5,13},{6,14},{7,15},{8,0},{9,1},... | collective-permute-start | bytes 1966088 | tf_op jit(solution)/shard_map/ppermute | solution.py:22
  49.2 8.7 %collective-permute-start.14 = (bf16[1,2,256,256]{3,2,1,0:T(8,128)(2,1)S(1)}, bf16[1,2,256,256]{3,2,1,0:T(8,128)(2,1)S(1)}, u32[]{:S(2)}, u32[]{:S(2)}) collective-permute-start(bf16[1,2,256,256]{3,2,1,0:T(8,128)(2,1)S(1)} %collective-permute-done.9), channel_id=1, source_target_pairs={{0,16},{1,17},{2,18},{3,19},{4,20},{5,21},{6,22},{7,23},{8,24},{9,... | collective-permute-start | bytes 786440 | tf_op jit(solution)/shard_map/ppermute | solution.py:22
  50.8 17.9 %collective-permute-start.13 = (bf16[2,2,5,128,128]{4,3,2,1,0:T(8,128)(2,1)S(1)}, bf16[2,2,5,128,128]{4,3,2,1,0:T(8,128)(2,1)}, u32[]{:S(2)}, u32[]{:S(2)}) collective-permute-start(bf16[2,2,5,128,128]{4,3,2,1,0:T(8,128)(2,1)S(1)} %pad_maximum_fusion.3.far), channel_id=1, source_target_pairs={{0,1},{1,0},{2,3},{3,2},{4,5},{5,4},{6,7},{7,6},{8,9},{9,8},{10,11... | collective-permute-start | bytes 1966088 | tf_op jit(solution)/shard_map/ppermute | solution.py:22
  52.8 16.4 %collective-permute-start.12 = (bf16[2,2,5,128,128]{4,3,2,1,0:T(8,128)(2,1)S(1)}, bf16[2,2,5,128,128]{4,3,2,1,0:T(8,128)(2,1)}, u32[]{:S(2)}, u32[]{:S(2)}) collective-permute-start(bf16[2,2,5,128,128]{4,3,2,1,0:T(8,128)(2,1)S(1)} %pad_maximum_fusion.2), channel_id=1, source_target_pairs={{0,2},{1,3},{2,0},{3,1},{4,6},{5,7},{6,4},{7,5},{8,10},{9,11},{10,... | collective-permute-start | bytes 1966088 | tf_op jit(solution)/shard_map/ppermute | solution.py:22
  58.0 2.0 %collective-permute-start.17 = (bf16[2,1,2,256,256]{4,3,2,1,0:T(8,128)(2,1)S(1)}, bf16[2,1,2,256,256]{4,3,2,1,0:T(8,128)(2,1)S(1)}, u32[]{:S(2)}, u32[]{:S(2)}) collective-permute-start(bf16[2,1,2,256,256]{4,3,2,1,0:T(8,128)(2,1)S(1)} %pad_maximum_fusion.4.own3), channel_id=1, source_target_pairs={{0,8},{1,9},{2,10},{3,11},{4,12},{5,13},{6,14},{7,15},{8,0},{9,1},... | collective-permute-start | bytes 1572872 | tf_op jit(solution)/shard_map/ppermute | solution.py:22
  58.1 15.3 %collective-permute-start.19 = (bf16[2,2,5,128,128]{4,3,2,1,0:T(8,128)(2,1)S(1)}, bf16[2,2,5,128,128]{4,3,2,1,0:T(8,128)(2,1)}, u32[]{:S(2)}, u32[]{:S(2)}) collective-permute-start(bf16[2,2,5,128,128]{4,3,2,1,0:T(8,128)(2,1)S(1)} %pad_maximum_fusion.3.far), channel_id=1, source_target_pairs={{0,8},{1,9},{2,10},{3,11},{4,12},{5,13},{6,14},{7,15},{8,0},{9,1},... | collective-permute-start | bytes 1966088 | tf_op jit(solution)/shard_map/ppermute | solution.py:22
  67.2 1.5 %copy-start = (bf16[4,5,256,256]{3,2,1,0:T(8,128)(2,1)}, bf16[4,5,256,256]{3,2,1,0:T(8,128)(2,1)S(1)}, u32[]{:S(2)}) copy-start(bf16[4,5,256,256]{3,2,1,0:T(8,128)(2,1)S(1)} %get-tuple-element.66.halves) | copy-start | bytes 7864324
  69.2 4.2 %collective-permute-start.18 = (bf16[2,2,5,128,128]{4,3,2,1,0:T(8,128)(2,1)}, bf16[2,2,5,128,128]{4,3,2,1,0:T(8,128)(2,1)}, u32[]{:S(2)}, u32[]{:S(2)}) collective-permute-start(bf16[2,2,5,128,128]{4,3,2,1,0:T(8,128)(2,1)} %collective-permute-done.12.both), channel_id=1, source_target_pairs={{0,8},{1,9},{2,10},{3,11},{4,12},{5,13},{6,14},{7,15},{8,0},{9,1},... | collective-permute-start | bytes 1966088 | tf_op jit(solution)/shard_map/ppermute | solution.py:22
  69.2 4.2 %collective-permute-start.20 = (bf16[2,2,5,128,128]{4,3,2,1,0:T(8,128)(2,1)}, bf16[2,2,5,128,128]{4,3,2,1,0:T(8,128)(2,1)}, u32[]{:S(2)}, u32[]{:S(2)}) collective-permute-start(bf16[2,2,5,128,128]{4,3,2,1,0:T(8,128)(2,1)} %collective-permute-done.13.beside), channel_id=1, source_target_pairs={{0,8},{1,9},{2,10},{3,11},{4,12},{5,13},{6,14},{7,15},{8,0},{9,1},... | collective-permute-start | bytes 1966088 | tf_op jit(solution)/shard_map/ppermute | solution.py:22
  69.7 1.7 %copy-start.1 = (bf16[4,5,256,256]{3,2,1,0:T(8,128)(2,1)S(1)}, bf16[4,5,256,256]{3,2,1,0:T(8,128)(2,1)}, u32[]{:S(2)}) copy-start(bf16[4,5,256,256]{3,2,1,0:T(8,128)(2,1)} %copy-done) | copy-start | bytes 7864324
  78.1 4.6 %collective-permute-start.23 = (bf16[2,2,128,128]{3,2,0,1:T(8,128)(2,1)S(1)}, bf16[2,2,128,128]{3,2,0,1:T(8,128)(2,1)S(1)}, u32[]{:S(2)}, u32[]{:S(2)}) collective-permute-start(bf16[2,2,128,128]{3,2,0,1:T(8,128)(2,1)S(1)} %copy.8), channel_id=1, source_target_pairs={{0,0},{1,1},{2,2},{3,3},{4,4},{5,5},{6,6},{7,7},{8,9},{9,8},{10,11... | collective-permute-start | bytes 393224 | tf_op jit(solution)/shard_map/ppermute | solution.py:22
  78.8 5.0 %collective-permute-start.24 = (bf16[2,2,128,128]{3,2,0,1:T(8,128)(2,1)S(1)}, bf16[2,2,128,128]{3,2,0,1:T(8,128)(2,1)S(1)}, u32[]{:S(2)}, u32[]{:S(2)}) collective-permute-start(bf16[2,2,128,128]{3,2,0,1:T(8,128)(2,1)S(1)} %copy.9), channel_id=1, source_target_pairs={{0,16},{1,17},{2,18},{3,19},{4,20},{5,21},{6,22},{7,23},{8,25},{9,... | collective-permute-start | bytes 393224 | tf_op jit(solution)/shard_map/ppermute | solution.py:22
  79.9 7.4 %collective-permute-start.21 = (bf16[2,2,128,128]{3,2,1,0:T(8,128)(2,1)S(1)}, bf16[2,2,128,128]{3,2,1,0:T(8,128)(2,1)S(1)}, u32[]{:S(2)}, u32[]{:S(2)}) collective-permute-start(bf16[2,2,128,128]{3,2,1,0:T(8,128)(2,1)S(1)} %get-tuple-element.76), channel_id=1, source_target_pairs={{0,8},{1,9},{2,10},{3,11},{4,12},{5,13},{6,14},{7,15},{8,1},{9,0},... | collective-permute-start | bytes 393224 | tf_op jit(solution)/shard_map/ppermute | solution.py:22
  82.2 6.6 %collective-permute-start.22 = (bf16[2,2,128,128]{3,2,1,0:T(8,128)(2,1)S(1)}, bf16[2,2,128,128]{3,2,1,0:T(8,128)(2,1)S(1)}, u32[]{:S(2)}, u32[]{:S(2)}) collective-permute-start(bf16[2,2,128,128]{3,2,1,0:T(8,128)(2,1)S(1)} %get-tuple-element.75), channel_id=1, source_target_pairs={{0,24},{1,25},{2,26},{3,27},{4,28},{5,29},{6,30},{7,31},{8,17},{9,... | collective-permute-start | bytes 393224 | tf_op jit(solution)/shard_map/ppermute | solution.py:22

commit v5 on v4

--- a/solution.py
+++ b/solution.py
@@ -248,10 +248,10 @@
     )(info, halves, held, both, swap_core(both), far, far_other, beside, swap_core(beside))
 
     sums = []
-    for m in range(ROWS):
+    for m in reversed(range(ROWS)):
         part = lax.dynamic_index_in_dim(partial, g ^ m, 0, keepdims=False)
         sums.append(move(part, lambda r, z, x, m=m: (r ^ m, z, x ^ (r & 1))).astype(jnp.float32))
-    same, other = sums[0] + sums[2], sums[1] + sums[3]
+    same, other = sums[3] + sums[1], sums[2] + sums[0]
     mine = (x ^ core) == 0
     crossed = jnp.where(mine, same, other)
     straight = jnp.where(mine, other, same)[::-1]

time: 90 us -> 90 us (level)
  no operation moved by 1% of the time
where the time goes in v5:
time: 90 us; the launch traced here: 89.8 us
  waiting for transfers between devices  37 us (41%)
  starting transfers between devices  29.4 us (33%)
  Pallas kernels  16.3 us (18%)
  local copies, waits for them, and re-layouts  3.4 us (4%)
  other arithmetic  3.3 us (4%)
    ppermute x25, waiting for transfers between devices, move(): return lax.ppermute(value, ('row', 'col'), pairs)  37 us
    ppermute x25, starting transfers between devices, move(): return lax.ppermute(value, ('row', 'col'), pairs)  29.4 us
    pallas_call x1, Pallas kernels, fast_body(): pl.pallas_call(halves_kernel, out_shape=(jax.ShapeDtypeStruct((PLANES, ve...  7.24 us
    pallas_call x1, Pallas kernels, fast_body(): pl.pallas_call(ladder_far_kernel, out_shape=jax.ShapeDtypeStruct((PLANES,...  4.61 us
    unnamed x14, local copies, waits for them, and re-layouts  3.23 us
    pallas_call x3, Pallas kernels, small_call(): pl.pallas_call(kernel, out_shape=out_shape, in_specs=specs, out_specs=jax...  2.51 us
    pallas_call x1, Pallas kernels, fast_body(): pl.pallas_call(ladder_own_kernel, out_shape=jax.ShapeDtypeStruct((PLANES,...  1.92 us
  transfers between devices with their start and end apart: 25, of which 12 were waited for; matrix products, arithmetic and copies ran while one was open for 1% of the time, Pallas kernels for 13%

profile of v5, /device:TPU:0, one launch (start us, length us, event | category | flops | bytes accessed | tf_op | source)
XLA Modules:
  0.0 89.8 jit_solution(1794844187897254739)
XLA Ops:
  0.0 0.7 convert_bitcast_fusion
  0.7 1.0 %fusion = bf16[2,4,128,128]{3,2,1,0:T(8,128)(2,1)S(1)} fusion(bf16[2,1,4,128,128]{4,3,2,1,0:T(8,128)(2,1)} %param.3, bf16[2]{0:T(256)(128)(2,1)S(1)} %convert_bitcast_fusion), kind=kLoop, calls=%fused_computation.14 | loop fusion | flops 131072 | bytes 524292 | tf_op jit(solution)/shard_map/squeeze | solution.py:169
  1.9 3.0 %collective-permute-start = (bf16[2,5,128,128]{3,2,1,0:T(8,128)(2,1)S(1)}, bf16[2,5,128,128]{3,2,1,0:T(8,128)(2,1)S(1)}, u32[]{:S(2)}, u32[]{:S(2)}) collective-permute-start(bf16[2,5,128,128]{3,2,1,0:T(8,128)(2,1)S(1)} %get-tuple-element.72), channel_id=1, source_target_pairs={{0,16},{1,17},{2,18},{3,19},{4,20},{5,21},{6,22},{7,23},{8,24},{9,... | collective-permute-start | bytes 983048 | tf_op jit(solution)/shard_map/ppermute | solution.py:22
  4.9 1.5 %collective-permute-start.1 = (bf16[2,2,128,128]{3,2,1,0:T(8,128)(2,1)S(1)}, bf16[2,2,128,128]{3,2,1,0:T(8,128)(2,1)S(1)}, u32[]{:S(2)}, u32[]{:S(2)}) collective-permute-start(bf16[2,2,128,128]{3,2,1,0:T(8,128)(2,1)S(1)} %get-tuple-element.42), channel_id=1, source_target_pairs={{0,1},{1,0},{2,3},{3,2},{4,5},{5,4},{6,7},{7,6},{8,9},{9,8},{10,11... | collective-permute-start | bytes 393224 | tf_op jit(solution)/shard_map/ppermute | solution.py:22
  6.4 2.6 %collective-permute-start.5 = (bf16[2,2,128,128]{3,2,1,0:T(8,128)(2,1)S(1)}, bf16[2,2,128,128]{3,2,1,0:T(8,128)(2,1)S(1)}, u32[]{:S(2)}, u32[]{:S(2)}) collective-permute-start(bf16[2,2,128,128]{3,2,1,0:T(8,128)(2,1)S(1)} %get-tuple-element.42), channel_id=1, source_target_pairs={{0,5},{1,4},{2,7},{3,6},{4,1},{5,0},{6,3},{7,2},{8,13},{9,12},{10,... | collective-permute-start | bytes 393224 | tf_op jit(solution)/shard_map/ppermute | solution.py:22
  9.3 0.7 collective-permute-done.1.refs_1_
  10.0 2.8 %collective-permute-start.2 = (bf16[2,2,128,128]{3,2,1,0:T(8,128)(2,1)S(1)}, bf16[2,2,128,128]{3,2,1,0:T(8,128)(2,1)S(1)}, u32[]{:S(2)}, u32[]{:S(2)}) collective-permute-start(bf16[2,2,128,128]{3,2,1,0:T(8,128)(2,1)S(1)} %get-tuple-element.41.refs_0_), channel_id=1, source_target_pairs={{0,2},{1,3},{2,0},{3,1},{4,6},{5,7},{6,4},{7,5},{8,10},{9,11},{10,... | collective-permute-start | bytes 393224 | tf_op jit(solution)/shard_map/ppermute | solution.py:22
  12.8 2.1 %collective-permute-start.3 = (bf16[2,2,128,128]{3,2,1,0:T(8,128)(2,1)S(1)}, bf16[2,2,128,128]{3,2,1,0:T(8,128)(2,1)S(1)}, u32[]{:S(2)}, u32[]{:S(2)}) collective-permute-start(bf16[2,2,128,128]{3,2,1,0:T(8,128)(2,1)S(1)} %get-tuple-element.42), channel_id=1, source_target_pairs={{0,3},{1,2},{2,1},{3,0},{4,7},{5,6},{6,5},{7,4},{8,11},{9,10},{10,... | collective-permute-start | bytes 393224 | tf_op jit(solution)/shard_map/ppermute | solution.py:22
  14.8 5.7 %collective-permute-done.4.refs_0_.refs_4_ = bf16[2,2,128,128]{3,2,1,0:T(8,128)(2,1)S(1)} collective-permute-done((bf16[2,2,128,128]{3,2,1,0:T(8,128)(2,1)S(1)}, bf16[2,2,128,128]{3,2,1,0:T(8,128)(2,1)S(1)}, u32[]{:S(2)}, u32[]{:S(2)}) %collective-permute-start.4) | collective-permute-done | bytes 131104 | tf_op jit(solution)/shard_map/ppermute | solution.py:22
  20.5 2.6 %collective-permute-done.3.refs_3_ = bf16[2,2,128,128]{3,2,1,0:T(8,128)(2,1)S(1)} collective-permute-done((bf16[2,2,128,128]{3,2,1,0:T(8,128)(2,1)S(1)}, bf16[2,2,128,128]{3,2,1,0:T(8,128)(2,1)S(1)}, u32[]{:S(2)}, u32[]{:S(2)}) %collective-permute-start.3) | collective-permute-done | bytes 131104 | tf_op jit(solution)/shard_map/ppermute | solution.py:22
  25.6 2.2 %collective-permute-start.8 = (bf16[2,5,128,128]{3,2,1,0:T(8,128)(2,1)S(1)}, bf16[2,5,128,128]{3,2,1,0:T(8,128)(2,1)S(1)}, u32[]{:S(2)}, u32[]{:S(2)}) collective-permute-start(bf16[2,5,128,128]{3,2,1,0:T(8,128)(2,1)S(1)} %broadcast_select_fusion), channel_id=1, source_target_pairs={{0,4},{1,5},{2,6},{3,7},{4,0},{5,1},{6,2},{7,3},{8,12},{9,13},{10,... | collective-permute-start | bytes 983048 | tf_op jit(solution)/shard_map/ppermute | solution.py:22
  27.8 2.5 %collective-permute-start.9 = (bf16[1,2,256,256]{3,2,1,0:T(8,128)(2,1)S(1)}, bf16[1,2,256,256]{3,2,1,0:T(8,128)(2,1)S(1)}, u32[]{:S(2)}, u32[]{:S(2)}) collective-permute-start(bf16[1,2,256,256]{3,2,1,0:T(8,128)(2,1)S(1)} %shard_map.37), channel_id=1, source_target_pairs={{0,2},{1,3},{2,0},{3,1},{4,6},{5,7},{6,4},{7,5},{8,10},{9,11},{10,... | collective-permute-start | bytes 786440 | tf_op jit(solution)/shard_map/ppermute | solution.py:22
  30.4 10.2 %collective-permute-done.7.xe = bf16[2,2,5,128,128]{4,3,2,1,0:T(8,128)(2,1)S(1)} collective-permute-done((bf16[2,2,5,128,128]{4,3,2,1,0:T(8,128)(2,1)S(1)}, bf16[2,2,5,128,128]{4,3,2,1,0:T(8,128)(2,1)S(1)}, u32[]{:S(2)}, u32[]{:S(2)}) %collective-permute-start.7) | collective-permute-done | bytes 655392 | tf_op jit(solution)/shard_map/ppermute | solution.py:22
  40.7 4.1 %collective-permute-done.10 = bf16[3,2,256,256]{3,2,1,0:T(8,128)(2,1)S(1)} collective-permute-done((bf16[3,2,256,256]{3,2,1,0:T(8,128)(2,1)S(1)}, bf16[3,2,256,256]{3,2,1,0:T(8,128)(2,1)S(1)}, u32[]{:S(2)}, u32[]{:S(2)}) %collective-permute-start.10) | collective-permute-done | bytes 786464 | tf_op jit(solution)/shard_map/ppermute | solution.py:22
  44.9 3.7 %collective-permute-done.11 = bf16[2,5,128,128]{3,2,1,0:T(8,128)(2,1)S(1)} collective-permute-done((bf16[2,5,128,128]{3,2,1,0:T(8,128)(2,1)S(1)}, bf16[2,5,128,128]{3,2,1,0:T(8,128)(2,1)S(1)}, u32[]{:S(2)}, u32[]{:S(2)}) %collective-permute-start.11) | collective-permute-done | bytes 327712 | tf_op jit(solution)/shard_map/ppermute | solution.py:22
  49.2 1.5 %collective-permute-start.14 = (bf16[1,2,256,256]{3,2,1,0:T(8,128)(2,1)S(1)}, bf16[1,2,256,256]{3,2,1,0:T(8,128)(2,1)S(1)}, u32[]{:S(2)}, u32[]{:S(2)}) collective-permute-start(bf16[1,2,256,256]{3,2,1,0:T(8,128)(2,1)S(1)} %collective-permute-done.9), channel_id=1, source_target_pairs={{0,16},{1,17},{2,18},{3,19},{4,20},{5,21},{6,22},{7,23},{8,24},{9,... | collective-permute-start | bytes 786440 | tf_op jit(solution)/shard_map/ppermute | solution.py:22
  50.8 1.9 %collective-permute-start.13 = (bf16[2,2,5,128,128]{4,3,2,1,0:T(8,128)(2,1)S(1)}, bf16[2,2,5,128,128]{4,3,2,1,0:T(8,128)(2,1)}, u32[]{:S(2)}, u32[]{:S(2)}) collective-permute-start(bf16[2,2,5,128,128]{4,3,2,1,0:T(8,128)(2,1)S(1)} %pad_maximum_fusion.3.far), channel_id=1, source_target_pairs={{0,1},{1,0},{2,3},{3,2},{4,5},{5,4},{6,7},{7,6},{8,9},{9,8},{10,11... | collective-permute-start | bytes 1966088 | tf_op jit(solution)/shard_map/ppermute | solution.py:22
  52.8 2.0 %collective-permute-start.12 = (bf16[2,2,5,128,128]{4,3,2,1,0:T(8,128)(2,1)S(1)}, bf16[2,2,5,128,128]{4,3,2,1,0:T(8,128)(2,1)}, u32[]{:S(2)}, u32[]{:S(2)}) collective-permute-start(bf16[2,2,5,128,128]{4,3,2,1,0:T(8,128)(2,1)S(1)} %pad_maximum_fusion.2), channel_id=1, source_target_pairs={{0,2},{1,3},{2,0},{3,1},{4,6},{5,7},{6,4},{7,5},{8,10},{9,11},{10,... | collective-permute-start | bytes 1966088 | tf_op jit(solution)/shard_map/ppermute | solution.py:22
  54.8 1.2 %shard_map.39 = (bf16[4,640,256]{2,1,0:T(8,128)(2,1)S(1)}, bf16[4,5,256,256]{3,2,1,0:T(8,128)(2,1)S(1)}) custom-call(s32[4]{0:T(128)S(1)} %pad_add_fusion.info, bf16[2,2,5,128,128]{4,3,2,1,0:T(8,128)(2,1)S(1)} %copy-done.3, bf16[2,2,5,128,128]{4,3,2,1,0:T(8,128)(2,1)S(1)} %copy-done.5, bf16[2,2,5,128,128]{4,3,2,1,0:T(8,128)(2,1)S(1)} %collective-permute-done.7.xe, ...), custom_call_target="tpu_custom_call" | custom-call | flops 1024 | bytes 1024 | tf_op jit(solution)/shard_map/pallas_call | solution.py:153
  56.0 2.0 %collective-permute-done.14 = bf16[1,2,256,256]{3,2,1,0:T(8,128)(2,1)S(1)} collective-permute-done((bf16[1,2,256,256]{3,2,1,0:T(8,128)(2,1)S(1)}, bf16[1,2,256,256]{3,2,1,0:T(8,128)(2,1)S(1)}, u32[]{:S(2)}, u32[]{:S(2)}) %collective-permute-start.14) | collective-permute-done | bytes 262176 | tf_op jit(solution)/shard_map/ppermute | solution.py:22
  58.6 1.4 %collective-permute-done.17.other3 = bf16[2,1,2,256,256]{4,3,2,1,0:T(8,128)(2,1)S(1)} collective-permute-done((bf16[2,1,2,256,256]{4,3,2,1,0:T(8,128)(2,1)S(1)}, bf16[2,1,2,256,256]{4,3,2,1,0:T(8,128)(2,1)S(1)}, u32[]{:S(2)}, u32[]{:S(2)}) %collective-permute-start.17) | collective-permute-done | bytes 524320 | tf_op jit(solution)/shard_map/ppermute | solution.py:22
  60.0 7.2 %shard_map.40 = (bf16[4,5,256,256]{3,2,1,0:T(8,128)(2,1)S(1)}, s32[4]{0:T(128)S(1)}) custom-call(s32[4]{0:T(128)S(1)} %pad_add_fusion.info, bf16[4,640,256]{2,1,0:T(8,128)(2,1)S(1)} %get-tuple-element.60.rows, bf16[4,5,256,256]{3,2,1,0:T(8,128)(2,1)S(1)} %get-tuple-element.61.mine, bf16[2,3,2,256,256]{4,3,2,1,0:T(8,128)(2,1)S(1)} %pad_maximum_fusion.own, ...), custom_call_target="tpu_custom_call" | custom-call | flops 1024 | bytes 1024 | tf_op jit(solution)/shard_map/pallas_call | solution.py:218
  67.2 1.5 %copy-done = bf16[4,5,256,256]{3,2,1,0:T(8,128)(2,1)} copy-done((bf16[4,5,256,256]{3,2,1,0:T(8,128)(2,1)}, bf16[4,5,256,256]{3,2,1,0:T(8,128)(2,1)S(1)}, u32[]{:S(2)}) %copy-start) | copy-done | bytes 2621464
  69.7 1.7 %copy-done.1 = bf16[4,5,256,256]{3,2,1,0:T(8,128)(2,1)S(1)} copy-done((bf16[4,5,256,256]{3,2,1,0:T(8,128)(2,1)S(1)}, bf16[4,5,256,256]{3,2,1,0:T(8,128)(2,1)}, u32[]{:S(2)}) %copy-start.1) | copy-done | bytes 2621464
  71.4 1.9 %shard_map.41.held = f32[4,256,256]{2,1,0:T(8,128)S(1)} custom-call(s32[4]{0:T(128)S(1)} %get-tuple-element.65.info, bf16[4,5,256,256]{3,2,1,0:T(8,128)(2,1)S(1)} %copy-done.1, bf16[4,5,256,256]{3,2,1,0:T(8,128)(2,1)S(1)} %get-tuple-element.61.mine), custom_call_target="tpu_custom_call" | custom-call | flops 1024 | bytes 1024 | tf_op jit(solution)/shard_map/pallas_call | solution.py:232
  73.4 4.6 %shard_map.42 = bf16[4,2,2,128,128]{4,3,2,1,0:T(8,128)(2,1)S(1)} custom-call(s32[4]{0:T(128)S(1)} %get-tuple-element.65.info, bf16[4,5,256,256]{3,2,1,0:T(8,128)(2,1)S(1)} %copy-done.1, f32[4,256,256]{2,1,0:T(8,128)S(1)} %shard_map.41.held, bf16[2,2,5,128,128]{4,3,2,1,0:T(8,128)(2,1)} %collective-permute-done.12.both, ...), custom_call_target="tpu_custom_call" | custom-call | flops 1024 | bytes 1024 | tf_op jit(solution)/shard_map/pallas_call | solution.py:240
  78.8 1.1 %collective-permute-start.24 = (bf16[2,2,128,128]{3,2,0,1:T(8,128)(2,1)S(1)}, bf16[2,2,128,128]{3,2,0,1:T(8,128)(2,1)S(1)}, u32[]{:S(2)}, u32[]{:S(2)}) collective-permute-start(bf16[2,2,128,128]{3,2,0,1:T(8,128)(2,1)S(1)} %copy.9), channel_id=1, source_target_pairs={{0,16},{1,17},{2,18},{3,19},{4,20},{5,21},{6,22},{7,23},{8,25},{9,... | collective-permute-start | bytes 393224 | tf_op jit(solution)/shard_map/ppermute | solution.py:22
  79.9 2.3 %collective-permute-start.21 = (bf16[2,2,128,128]{3,2,1,0:T(8,128)(2,1)S(1)}, bf16[2,2,128,128]{3,2,1,0:T(8,128)(2,1)S(1)}, u32[]{:S(2)}, u32[]{:S(2)}) collective-permute-start(bf16[2,2,128,128]{3,2,1,0:T(8,128)(2,1)S(1)} %get-tuple-element.76), channel_id=1, source_target_pairs={{0,8},{1,9},{2,10},{3,11},{4,12},{5,13},{6,14},{7,15},{8,1},{9,0},... | collective-permute-start | bytes 393224 | tf_op jit(solution)/shard_map/ppermute | solution.py:22
  82.6 1.2 %collective-permute-done.24 = bf16[2,2,128,128]{3,2,0,1:T(8,128)(2,1)S(1)} collective-permute-done((bf16[2,2,128,128]{3,2,0,1:T(8,128)(2,1)S(1)}, bf16[2,2,128,128]{3,2,0,1:T(8,128)(2,1)S(1)}, u32[]{:S(2)}, u32[]{:S(2)}) %collective-permute-start.24) | collective-permute-done | bytes 131104 | tf_op jit(solution)/shard_map/ppermute | solution.py:22
  83.8 3.5 %collective-permute-done.21 = bf16[2,2,128,128]{3,2,1,0:T(8,128)(2,1)S(1)} collective-permute-done((bf16[2,2,128,128]{3,2,1,0:T(8,128)(2,1)S(1)}, bf16[2,2,128,128]{3,2,1,0:T(8,128)(2,1)S(1)}, u32[]{:S(2)}, u32[]{:S(2)}) %collective-permute-start.21) | collective-permute-done | bytes 131104 | tf_op jit(solution)/shard_map/ppermute | solution.py:22
  87.3 1.5 %collective-permute-done.22 = bf16[2,2,128,128]{3,2,1,0:T(8,128)(2,1)S(1)} collective-permute-done((bf16[2,2,128,128]{3,2,1,0:T(8,128)(2,1)S(1)}, bf16[2,2,128,128]{3,2,1,0:T(8,128)(2,1)S(1)}, u32[]{:S(2)}, u32[]{:S(2)}) %collective-permute-start.22) | collective-permute-done | bytes 131104 | tf_op jit(solution)/shard_map/ppermute | solution.py:22
  89.0 0.7 maximum_bitcast_fusion
  (61 shorter events, 6.8 us)
Async XLA Ops:
  0.0 1.8 %copy-start.6 = (bf16[2,1,10,128,128]{4,3,2,1,0:T(8,128)(2,1)S(1)}, bf16[2,1,10,128,128]{4,3,2,1,0:T(8,128)(2,1)}, u32[]{:S(2)}) copy-start(bf16[2,1,10,128,128]{4,3,2,1,0:T(8,128)(2,1)} %param.4) | copy-start | bytes 1966084
  1.9 21.3 %collective-permute-start = (bf16[2,5,128,128]{3,2,1,0:T(8,128)(2,1)S(1)}, bf16[2,5,128,128]{3,2,1,0:T(8,128)(2,1)S(1)}, u32[]{:S(2)}, u32[]{:S(2)}) collective-permute-start(bf16[2,5,128,128]{3,2,1,0:T(8,128)(2,1)S(1)} %get-tuple-element.72), channel_id=1, source_target_pairs={{0,16},{1,17},{2,18},{3,19},{4,20},{5,21},{6,22},{7,23},{8,24},{9,... | collective-permute-start | bytes 983048 | tf_op jit(solution)/shard_map/ppermute | solution.py:22
  4.9 5.1 %collective-permute-start.1 = (bf16[2,2,128,128]{3,2,1,0:T(8,128)(2,1)S(1)}, bf16[2,2,128,128]{3,2,1,0:T(8,128)(2,1)S(1)}, u32[]{:S(2)}, u32[]{:S(2)}) collective-permute-start(bf16[2,2,128,128]{3,2,1,0:T(8,128)(2,1)S(1)} %get-tuple-element.42), channel_id=1, source_target_pairs={{0,1},{1,0},{2,3},{3,2},{4,5},{5,4},{6,7},{7,6},{8,9},{9,8},{10,11... | collective-permute-start | bytes 393224 | tf_op jit(solution)/shard_map/ppermute | solution.py:22
  6.4 14.1 %collective-permute-start.5 = (bf16[2,2,128,128]{3,2,1,0:T(8,128)(2,1)S(1)}, bf16[2,2,128,128]{3,2,1,0:T(8,128)(2,1)S(1)}, u32[]{:S(2)}, u32[]{:S(2)}) collective-permute-start(bf16[2,2,128,128]{3,2,1,0:T(8,128)(2,1)S(1)} %get-tuple-element.42), channel_id=1, source_target_pairs={{0,5},{1,4},{2,7},{3,6},{4,1},{5,0},{6,3},{7,2},{8,13},{9,12},{10,... | collective-permute-start | bytes 393224 | tf_op jit(solution)/shard_map/ppermute | solution.py:22
  9.0 11.5 %collective-permute-start.4 = (bf16[2,2,128,128]{3,2,1,0:T(8,128)(2,1)S(1)}, bf16[2,2,128,128]{3,2,1,0:T(8,128)(2,1)S(1)}, u32[]{:S(2)}, u32[]{:S(2)}) collective-permute-start(bf16[2,2,128,128]{3,2,1,0:T(8,128)(2,1)S(1)} %get-tuple-element.41.refs_0_), channel_id=1, source_target_pairs={{0,4},{1,5},{2,6},{3,7},{4,0},{5,1},{6,2},{7,3},{8,12},{9,13},{10,... | collective-permute-start | bytes 393224 | tf_op jit(solution)/shard_map/ppermute | solution.py:22
  10.0 10.5 %collective-permute-start.2 = (bf16[2,2,128,128]{3,2,1,0:T(8,128)(2,1)S(1)}, bf16[2,2,128,128]{3,2,1,0:T(8,128)(2,1)S(1)}, u32[]{:S(2)}, u32[]{:S(2)}) collective-permute-start(bf16[2,2,128,128]{3,2,1,0:T(8,128)(2,1)S(1)} %get-tuple-element.41.refs_0_), channel_id=1, source_target_pairs={{0,2},{1,3},{2,0},{3,1},{4,6},{5,7},{6,4},{7,5},{8,10},{9,11},{10,... | collective-permute-start | bytes 393224 | tf_op jit(solution)/shard_map/ppermute | solution.py:22
  12.8 10.4 %collective-permute-start.3 = (bf16[2,2,128,128]{3,2,1,0:T(8,128)(2,1)S(1)}, bf16[2,2,128,128]{3,2,1,0:T(8,128)(2,1)S(1)}, u32[]{:S(2)}, u32[]{:S(2)}) collective-permute-start(bf16[2,2,128,128]{3,2,1,0:T(8,128)(2,1)S(1)} %get-tuple-element.42), channel_id=1, source_target_pairs={{0,3},{1,2},{2,1},{3,0},{4,7},{5,6},{6,5},{7,4},{8,11},{9,10},{10,... | collective-permute-start | bytes 393224 | tf_op jit(solution)/shard_map/ppermute | solution.py:22
  23.3 2.3 %copy-start.2 = (bf16[2,2,5,128,128]{4,3,2,1,0:T(8,128)(2,1)}, bf16[2,2,5,128,128]{4,3,2,1,0:T(8,128)(2,1)S(1)}, u32[]{:S(2)}) copy-start(bf16[2,2,5,128,128]{4,3,2,1,0:T(8,128)(2,1)S(1)} %pad_maximum_fusion.1.e) | copy-start | bytes 1966084
  23.3 7.0 %collective-permute-start.6 = (bf16[2,2,5,128,128]{4,3,2,1,0:T(8,128)(2,1)S(1)}, bf16[2,2,5,128,128]{4,3,2,1,0:T(8,128)(2,1)S(1)}, u32[]{:S(2)}, u32[]{:S(2)}) collective-permute-start(bf16[2,2,5,128,128]{4,3,2,1,0:T(8,128)(2,1)S(1)} %pad_maximum_fusion.1.e), channel_id=1, source_target_pairs={{0,8},{1,9},{2,10},{3,11},{4,12},{5,13},{6,14},{7,15},{8,0},{9,1},... | collective-permute-start | bytes 1966088 | tf_op jit(solution)/shard_map/ppermute | solution.py:22
  23.4 17.1 %collective-permute-start.7 = (bf16[2,2,5,128,128]{4,3,2,1,0:T(8,128)(2,1)S(1)}, bf16[2,2,5,128,128]{4,3,2,1,0:T(8,128)(2,1)S(1)}, u32[]{:S(2)}, u32[]{:S(2)}) collective-permute-start(bf16[2,2,5,128,128]{4,3,2,1,0:T(8,128)(2,1)S(1)} %pad_maximum_fusion.1.e), channel_id=1, source_target_pairs={{0,1},{1,0},{2,3},{3,2},{4,5},{5,4},{6,7},{7,6},{8,9},{9,8},{10,11... | collective-permute-start | bytes 1966088 | tf_op jit(solution)/shard_map/ppermute | solution.py:22
  25.0 19.8 %collective-permute-start.10 = (bf16[3,2,256,256]{3,2,1,0:T(8,128)(2,1)S(1)}, bf16[3,2,256,256]{3,2,1,0:T(8,128)(2,1)S(1)}, u32[]{:S(2)}, u32[]{:S(2)}) collective-permute-start(bf16[3,2,256,256]{3,2,1,0:T(8,128)(2,1)S(1)} %shard_map.38), channel_id=1, source_target_pairs={{0,16},{1,17},{2,18},{3,19},{4,20},{5,21},{6,22},{7,23},{8,24},{9,... | collective-permute-start | bytes 2359304 | tf_op jit(solution)/shard_map/ppermute | solution.py:22
  25.6 19.3 %collective-permute-start.8 = (bf16[2,5,128,128]{3,2,1,0:T(8,128)(2,1)S(1)}, bf16[2,5,128,128]{3,2,1,0:T(8,128)(2,1)S(1)}, u32[]{:S(2)}, u32[]{:S(2)}) collective-permute-start(bf16[2,5,128,128]{3,2,1,0:T(8,128)(2,1)S(1)} %broadcast_select_fusion), channel_id=1, source_target_pairs={{0,4},{1,5},{2,6},{3,7},{4,0},{5,1},{6,2},{7,3},{8,12},{9,13},{10,... | collective-permute-start | bytes 983048 | tf_op jit(solution)/shard_map/ppermute | solution.py:22
  27.8 17.1 %collective-permute-start.9 = (bf16[1,2,256,256]{3,2,1,0:T(8,128)(2,1)S(1)}, bf16[1,2,256,256]{3,2,1,0:T(8,128)(2,1)S(1)}, u32[]{:S(2)}, u32[]{:S(2)}) collective-permute-start(bf16[1,2,256,256]{3,2,1,0:T(8,128)(2,1)S(1)} %shard_map.37), channel_id=1, source_target_pairs={{0,2},{1,3},{2,0},{3,1},{4,6},{5,7},{6,4},{7,5},{8,10},{9,11},{10,... | collective-permute-start | bytes 786440 | tf_op jit(solution)/shard_map/ppermute | solution.py:22
  30.3 10.4 %copy-start.4 = (bf16[2,2,5,128,128]{4,3,2,1,0:T(8,128)(2,1)}, bf16[2,2,5,128,128]{4,3,2,1,0:T(8,128)(2,1)S(1)}, u32[]{:S(2)}) copy-start(bf16[2,2,5,128,128]{4,3,2,1,0:T(8,128)(2,1)S(1)} %collective-permute-done.6.ce) | copy-start | bytes 1966084
  30.3 18.3 %collective-permute-start.11 = (bf16[2,5,128,128]{3,2,1,0:T(8,128)(2,1)S(1)}, bf16[2,5,128,128]{3,2,1,0:T(8,128)(2,1)S(1)}, u32[]{:S(2)}, u32[]{:S(2)}) collective-permute-start(bf16[2,5,128,128]{3,2,1,0:T(8,128)(2,1)S(1)} %bitcast_select_fusion), channel_id=1, source_target_pairs={{0,6},{1,7},{2,0},{3,1},{4,2},{5,3},{6,4},{7,5},{8,10},{9,11},{10,... | collective-permute-start | bytes 983048 | tf_op jit(solution)/shard_map/ppermute | solution.py:22
  44.7 10.0 %copy-start.3 = (bf16[2,2,5,128,128]{4,3,2,1,0:T(8,128)(2,1)S(1)}, bf16[2,2,5,128,128]{4,3,2,1,0:T(8,128)(2,1)}, u32[]{:S(2)}) copy-start(bf16[2,2,5,128,128]{4,3,2,1,0:T(8,128)(2,1)} %copy-done.2) | copy-start | bytes 1966084
  44.7 10.0 %copy-start.5 = (bf16[2,2,5,128,128]{4,3,2,1,0:T(8,128)(2,1)S(1)}, bf16[2,2,5,128,128]{4,3,2,1,0:T(8,128)(2,1)}, u32[]{:S(2)}) copy-start(bf16[2,2,5,128,128]{4,3,2,1,0:T(8,128)(2,1)} %copy-done.4) | copy-start | bytes 1966084
  48.6 11.4 %collective-permute-start.16 = (bf16[2,3,2,256,256]{4,3,2,1,0:T(8,128)(2,1)S(1)}, bf16[2,3,2,256,256]{4,3,2,1,0:T(8,128)(2,1)S(1)}, u32[]{:S(2)}, u32[]{:S(2)}) collective-permute-start(bf16[2,3,2,256,256]{4,3,2,1,0:T(8,128)(2,1)S(1)} %pad_maximum_fusion.own), channel_id=1, source_target_pairs={{0,8},{1,9},{2,10},{3,11},{4,12},{5,13},{6,14},{7,15},{8,0},{9,1},... | collective-permute-start | bytes 4718600 | tf_op jit(solution)/shard_map/ppermute | solution.py:22
  49.2 5.5 %collective-permute-start.15 = (bf16[2,2,5,128,128]{4,3,2,1,0:T(8,128)(2,1)S(1)}, bf16[2,2,5,128,128]{4,3,2,1,0:T(8,128)(2,1)S(1)}, u32[]{:S(2)}, u32[]{:S(2)}) collective-permute-start(bf16[2,2,5,128,128]{4,3,2,1,0:T(8,128)(2,1)S(1)} %collective-permute-done.7.xe), channel_id=1, source_target_pairs={{0,8},{1,9},{2,10},{3,11},{4,12},{5,13},{6,14},{7,15},{8,0},{9,1},... | collective-permute-start | bytes 1966088 | tf_op jit(solution)/shard_map/ppermute | solution.py:22
  49.2 8.7 %collective-permute-start.14 = (bf16[1,2,256,256]{3,2,1,0:T(8,128)(2,1)S(1)}, bf16[1,2,256,256]{3,2,1,0:T(8,128)(2,1)S(1)}, u32[]{:S(2)}, u32[]{:S(2)}) collective-permute-start(bf16[1,2,256,256]{3,2,1,0:T(8,128)(2,1)S(1)} %collective-permute-done.9), channel_id=1, source_target_pairs={{0,16},{1,17},{2,18},{3,19},{4,20},{5,21},{6,22},{7,23},{8,24},{9,... | collective-permute-start | bytes 786440 | tf_op jit(solution)/shard_map/ppermute | solution.py:22
  50.8 17.9 %collective-permute-start.13 = (bf16[2,2,5,128,128]{4,3,2,1,0:T(8,128)(2,1)S(1)}, bf16[2,2,5,128,128]{4,3,2,1,0:T(8,128)(2,1)}, u32[]{:S(2)}, u32[]{:S(2)}) collective-permute-start(bf16[2,2,5,128,128]{4,3,2,1,0:T(8,128)(2,1)S(1)} %pad_maximum_fusion.3.far), channel_id=1, source_target_pairs={{0,1},{1,0},{2,3},{3,2},{4,5},{5,4},{6,7},{7,6},{8,9},{9,8},{10,11... | collective-permute-start | bytes 1966088 | tf_op jit(solution)/shard_map/ppermute | solution.py:22
  52.8 16.4 %collective-permute-start.12 = (bf16[2,2,5,128,128]{4,3,2,1,0:T(8,128)(2,1)S(1)}, bf16[2,2,5,128,128]{4,3,2,1,0:T(8,128)(2,1)}, u32[]{:S(2)}, u32[]{:S(2)}) collective-permute-start(bf16[2,2,5,128,128]{4,3,2,1,0:T(8,128)(2,1)S(1)} %pad_maximum_fusion.2), channel_id=1, source_target_pairs={{0,2},{1,3},{2,0},{3,1},{4,6},{5,7},{6,4},{7,5},{8,10},{9,11},{10,... | collective-permute-start | bytes 1966088 | tf_op jit(solution)/shard_map/ppermute | solution.py:22
  58.0 2.0 %collective-permute-start.17 = (bf16[2,1,2,256,256]{4,3,2,1,0:T(8,128)(2,1)S(1)}, bf16[2,1,2,256,256]{4,3,2,1,0:T(8,128)(2,1)S(1)}, u32[]{:S(2)}, u32[]{:S(2)}) collective-permute-start(bf16[2,1,2,256,256]{4,3,2,1,0:T(8,128)(2,1)S(1)} %pad_maximum_fusion.4.own3), channel_id=1, source_target_pairs={{0,8},{1,9},{2,10},{3,11},{4,12},{5,13},{6,14},{7,15},{8,0},{9,1},... | collective-permute-start | bytes 1572872 | tf_op jit(solution)/shard_map/ppermute | solution.py:22
  58.1 15.3 %collective-permute-start.19 = (bf16[2,2,5,128,128]{4,3,2,1,0:T(8,128)(2,1)S(1)}, bf16[2,2,5,128,128]{4,3,2,1,0:T(8,128)(2,1)}, u32[]{:S(2)}, u32[]{:S(2)}) collective-permute-start(bf16[2,2,5,128,128]{4,3,2,1,0:T(8,128)(2,1)S(1)} %pad_maximum_fusion.3.far), channel_id=1, source_target_pairs={{0,8},{1,9},{2,10},{3,11},{4,12},{5,13},{6,14},{7,15},{8,0},{9,1},... | collective-permute-start | bytes 1966088 | tf_op jit(solution)/shard_map/ppermute | solution.py:22
  67.2 1.5 %copy-start = (bf16[4,5,256,256]{3,2,1,0:T(8,128)(2,1)}, bf16[4,5,256,256]{3,2,1,0:T(8,128)(2,1)S(1)}, u32[]{:S(2)}) copy-start(bf16[4,5,256,256]{3,2,1,0:T(8,128)(2,1)S(1)} %get-tuple-element.66.halves) | copy-start | bytes 7864324
  69.2 4.2 %collective-permute-start.18 = (bf16[2,2,5,128,128]{4,3,2,1,0:T(8,128)(2,1)}, bf16[2,2,5,128,128]{4,3,2,1,0:T(8,128)(2,1)}, u32[]{:S(2)}, u32[]{:S(2)}) collective-permute-start(bf16[2,2,5,128,128]{4,3,2,1,0:T(8,128)(2,1)} %collective-permute-done.12.both), channel_id=1, source_target_pairs={{0,8},{1,9},{2,10},{3,11},{4,12},{5,13},{6,14},{7,15},{8,0},{9,1},... | collective-permute-start | bytes 1966088 | tf_op jit(solution)/shard_map/ppermute | solution.py:22
  69.2 4.2 %collective-permute-start.20 = (bf16[2,2,5,128,128]{4,3,2,1,0:T(8,128)(2,1)}, bf16[2,2,5,128,128]{4,3,2,1,0:T(8,128)(2,1)}, u32[]{:S(2)}, u32[]{:S(2)}) collective-permute-start(bf16[2,2,5,128,128]{4,3,2,1,0:T(8,128)(2,1)} %collective-permute-done.13.beside), channel_id=1, source_target_pairs={{0,8},{1,9},{2,10},{3,11},{4,12},{5,13},{6,14},{7,15},{8,0},{9,1},... | collective-permute-start | bytes 1966088 | tf_op jit(solution)/shard_map/ppermute | solution.py:22
  69.7 1.7 %copy-start.1 = (bf16[4,5,256,256]{3,2,1,0:T(8,128)(2,1)S(1)}, bf16[4,5,256,256]{3,2,1,0:T(8,128)(2,1)}, u32[]{:S(2)}) copy-start(bf16[4,5,256,256]{3,2,1,0:T(8,128)(2,1)} %copy-done) | copy-start | bytes 7864324
  78.1 4.6 %collective-permute-start.23 = (bf16[2,2,128,128]{3,2,0,1:T(8,128)(2,1)S(1)}, bf16[2,2,128,128]{3,2,0,1:T(8,128)(2,1)S(1)}, u32[]{:S(2)}, u32[]{:S(2)}) collective-permute-start(bf16[2,2,128,128]{3,2,0,1:T(8,128)(2,1)S(1)} %copy.8), channel_id=1, source_target_pairs={{0,0},{1,1},{2,2},{3,3},{4,4},{5,5},{6,6},{7,7},{8,9},{9,8},{10,11... | collective-permute-start | bytes 393224 | tf_op jit(solution)/shard_map/ppermute | solution.py:22
  78.8 5.0 %collective-permute-start.24 = (bf16[2,2,128,128]{3,2,0,1:T(8,128)(2,1)S(1)}, bf16[2,2,128,128]{3,2,0,1:T(8,128)(2,1)S(1)}, u32[]{:S(2)}, u32[]{:S(2)}) collective-permute-start(bf16[2,2,128,128]{3,2,0,1:T(8,128)(2,1)S(1)} %copy.9), channel_id=1, source_target_pairs={{0,16},{1,17},{2,18},{3,19},{4,20},{5,21},{6,22},{7,23},{8,25},{9,... | collective-permute-start | bytes 393224 | tf_op jit(solution)/shard_map/ppermute | solution.py:22
  79.9 7.4 %collective-permute-start.21 = (bf16[2,2,128,128]{3,2,1,0:T(8,128)(2,1)S(1)}, bf16[2,2,128,128]{3,2,1,0:T(8,128)(2,1)S(1)}, u32[]{:S(2)}, u32[]{:S(2)}) collective-permute-start(bf16[2,2,128,128]{3,2,1,0:T(8,128)(2,1)S(1)} %get-tuple-element.76), channel_id=1, source_target_pairs={{0,8},{1,9},{2,10},{3,11},{4,12},{5,13},{6,14},{7,15},{8,1},{9,0},... | collective-permute-start | bytes 393224 | tf_op jit(solution)/shard_map/ppermute | solution.py:22
  82.2 6.6 %collective-permute-start.22 = (bf16[2,2,128,128]{3,2,1,0:T(8,128)(2,1)S(1)}, bf16[2,2,128,128]{3,2,1,0:T(8,128)(2,1)S(1)}, u32[]{:S(2)}, u32[]{:S(2)}) collective-permute-start(bf16[2,2,128,128]{3,2,1,0:T(8,128)(2,1)S(1)} %get-tuple-element.75), channel_id=1, source_target_pairs={{0,24},{1,25},{2,26},{3,27},{4,28},{5,29},{6,30},{7,31},{8,17},{9,... | collective-permute-start | bytes 393224 | tf_op jit(solution)/shard_map/ppermute | solution.py:22
